TPU v7x, 32 devices: a whole 2x2x4 slice. The times are simulated.
32 devices in a mesh: seq: 2 (over x), dp: 4 (over y, core), rep: 4 (over z).
Axes of the slice: x: 2, y: 2, z: 4, core: 2. Of those that a mesh axis runs over, the one named last changes fastest.
Arguments:
- inputs: bfloat16 [2, 16, 2048, 1024], P(None, ('dp', 'rep'), 'seq'), may hold values from -6 to 6
- segments: int32 [2, 16, 2048], P(None, ('dp', 'rep')), may hold values from 0 to 6, as said below
- cotangent: bfloat16 [2, 16, 2048, 1024], P(None, ('dp', 'rep'), 'seq'), may hold values from -6 to 6
- attn_gain: bfloat16 [1024], P(('seq', 'dp')), may hold values from 0.25 to 1.75
- mlp_gain: bfloat16 [1024], P(('seq', 'dp')), may hold values from 0.25 to 1.75
- w_qkv: bfloat16 [1024, 3072], P(('seq', 'dp')), may hold values from -0.1875 to 0.1875
- w_out: bfloat16 [1024, 1024], P(('seq', 'dp')), may hold values from -3 to 3
- w_in: bfloat16 [1024, 5248], P(('seq', 'dp')), may hold values from -0.1875 to 0.1875
- w_down: bfloat16 [2624, 1024], P(('seq', 'dp')), may hold values from -0.125 to 0.125
Outputs:
- outputs: bfloat16 [2, 16, 2048, 1024], P(None, ('dp', 'rep'), 'seq')
- grad_inputs: float32 [2, 16, 2048, 1024], P(None, ('dp', 'rep'), 'seq')
- grad_attn_gain: float32 [1024], P(('seq', 'dp'))
- grad_mlp_gain: float32 [1024], P(('seq', 'dp'))
- grad_qkv: float32 [1024, 3072], P(('seq', 'dp'))
- grad_out: float32 [1024, 1024], P(('seq', 'dp'))
- grad_in: float32 [1024, 5248], P(('seq', 'dp'))
- grad_down: float32 [2624, 1024], P(('seq', 'dp'))
Inputs may be any that keep to these rules, and one draw needn't show every extreme that they name: `segments`: along each packed sequence the document number never falls; it is 0 at the first token and 6 at the last.
All inputs are finite; a program needn't handle non-finite values.
Results may differ from a plain program's by a relative error of at most 0.02.
Values may be sent and summed in bfloat16 or wider, within the bound.
A program may use at most 576 MiB of HBM per device.

v0:
```python
import jax
import jax.numpy as jnp
from jax import lax
from jax.sharding import PartitionSpec as P

HEADS = 16
HEAD_DIM = 64
FF = 2624
HALF = 512


EPS = 1e-05
THETA = 10000.0
MASKED = -1e30


def from_behind(block, axis, distance):
    devices = range(lax.axis_size(axis))
    route = [(i - distance, i) for i in devices if i - distance in devices]
    return lax.ppermute(block, axis, route)


def shortened(shard):

    def short(part):
        return part.astype(jnp.bfloat16) if part.dtype == jnp.float32 else part

    return jax.tree.map(short, shard)


def layer_norm(values, scaling):
    centre = values - jnp.mean(values, axis=-1, keepdims=True)
    spread = jnp.mean(centre * centre, axis=-1, keepdims=True)
    return centre * lax.rsqrt(spread + EPS) * scaling


def positions_of(labels):
    places = jnp.arange(labels.shape[0], dtype=jnp.int32)
    changes = jnp.concatenate([jnp.ones((1,), dtype=bool), labels[1:] != labels[:-1]])
    starts = lax.cummax(jnp.where(changes, places, 0), axis=0)
    return places - starts


def rope_tables(positions, head_size):
    half_dim = head_size // 2
    frequency = THETA ** (-(jnp.arange(half_dim, dtype=jnp.float32) * 2.0 / head_size))
    angles = positions.astype(jnp.float32)[:, None] * frequency[None, :]
    return (jnp.cos(angles)[:, None, :], jnp.sin(angles)[:, None, :])


def rotate(values, cosines, sines):
    half_dim = values.shape[-1] // 2
    leading = values[..., :half_dim]
    trailing = values[..., half_dim:]
    return jnp.concatenate(
        [leading * cosines - trailing * sines, trailing * cosines + leading * sines], axis=-1
    )


def window_mask(query_labels, key_labels, half_window):
    gaps = (
        jnp.arange(key_labels.shape[0], dtype=jnp.int32)[None, :]
        - jnp.arange(query_labels.shape[0], dtype=jnp.int32)[:, None]
    )
    return (gaps >= 0) & (gaps <= 2 * half_window) & (query_labels[:, None] == key_labels[None, :])


def contract_rows(left, right):
    return lax.dot_general(
        left, right, (((0,), (0,)), ((), ())), preferred_element_type=jnp.float32
    )


def times_back(left, weight):
    return lax.dot_general(
        left, weight, (((1,), (1,)), ((), ())), preferred_element_type=jnp.float32
    )


def gelu_gate(gate_part, up_part):
    return jax.nn.gelu(gate_part, approximate=False) * up_part


def body(inputs, segments, cotangent, attn_gain, mlp_gain, w_qkv, w_out, w_in, w_down):
    micro_count = inputs.shape[0]
    stretch_rows = inputs.shape[2]
    model_width = inputs.shape[3]
    head_count = HEADS
    head_size = HEAD_DIM
    hidden_units = FF
    half_window = HALF
    reach_count = (half_window + stretch_rows - 1) // stretch_rows
    block_rows = min(512, stretch_rows)
    blocks = stretch_rows // block_rows
    key_span = block_rows + 2 * half_window
    extent = (2 * reach_count + 1) * stretch_rows
    score_scale = head_size ** (-0.5)
    offsets = list(range(reach_count, 0, -1)) + list(range(-1, -reach_count - 1, -1))
    seq_index = lax.axis_index("seq")
    shards = (attn_gain, mlp_gain, w_qkv, w_out, w_in, w_down)
    outside = jnp.full((reach_count * stretch_rows,), -1, jnp.int32)

    def fetch_weights():
        return (
            lax.all_gather(shards[0], ("seq", "dp"), axis=0, tiled=True),
            lax.all_gather(shards[1], ("seq", "dp"), axis=0, tiled=True),
            lax.all_gather(shards[2], ("seq", "dp"), axis=0, tiled=True),
            lax.all_gather(shards[3], ("seq", "dp"), axis=0, tiled=True),
            lax.all_gather(shards[4], ("seq", "dp"), axis=0, tiled=True),
            lax.all_gather(shards[5], ("seq", "dp"), axis=0, tiled=True),
        )

    totals = None
    results = []
    input_grads = []
    for micro_index in range(micro_count):
        weights = fetch_weights()
        gain_one = weights[0].astype(jnp.float32)
        gain_two = weights[1].astype(jnp.float32)
        qkv_weight, out_weight, in_weight, down_weight = (
            weights[2],
            weights[3],
            weights[4],
            weights[5],
        )
        stream = inputs[micro_index, 0].astype(jnp.float32)
        labels = segments[micro_index, 0]
        own_start = seq_index * stretch_rows
        positions = lax.dynamic_slice_in_dim(positions_of(labels), own_start, stretch_rows, 0)
        own_labels = lax.dynamic_slice_in_dim(labels, own_start, stretch_rows, 0)
        wide_labels = lax.dynamic_slice_in_dim(
            jnp.concatenate([outside, labels, outside]), own_start, extent, 0
        )
        cosines, sines = rope_tables(positions, head_size)
        normed_one = layer_norm(stream, gain_one).astype(jnp.bfloat16)
        projected = jnp.dot(normed_one, qkv_weight, preferred_element_type=jnp.float32)
        query_raw = projected[:, :model_width].reshape(stretch_rows, head_count, head_size)
        key_raw = projected[:, model_width : 2 * model_width].reshape(
            stretch_rows, head_count, head_size
        )
        queries = (
            rotate(query_raw, cosines, sines)
            .reshape(stretch_rows, model_width)
            .astype(jnp.bfloat16)
        )
        keys = (
            rotate(key_raw, cosines, sines).reshape(stretch_rows, model_width).astype(jnp.bfloat16)
        )
        values = projected[:, 2 * model_width :].astype(jnp.bfloat16)
        pieces = {}
        for distance in offsets:
            pieces[distance] = from_behind((keys, values), "seq", distance)
        wide_keys = jnp.concatenate(
            [pieces[d][0] for d in offsets[:reach_count]]
            + [keys]
            + [pieces[d][0] for d in offsets[reach_count:]],
            axis=0,
        )
        wide_values = jnp.concatenate(
            [pieces[d][1] for d in offsets[:reach_count]]
            + [values]
            + [pieces[d][1] for d in offsets[reach_count:]],
            axis=0,
        )

        def block_inputs(number, query_side):
            first_row = number * block_rows
            key_start = reach_count * stretch_rows + first_row - half_window
            query_rows = lax.dynamic_slice_in_dim(query_side, first_row, block_rows, 0).reshape(
                block_rows, head_count, head_size
            )
            key_rows = lax.dynamic_slice_in_dim(wide_keys, key_start, key_span, 0).reshape(
                key_span, head_count, head_size
            )
            value_rows = lax.dynamic_slice_in_dim(wide_values, key_start, key_span, 0).reshape(
                key_span, head_count, head_size
            )
            allowed = window_mask(
                lax.dynamic_slice_in_dim(own_labels, first_row, block_rows, 0),
                lax.dynamic_slice_in_dim(wide_labels, key_start, key_span, 0),
                half_window,
            )
            scores = (
                jnp.einsum("qhd,khd->hqk", query_rows, key_rows, preferred_element_type=jnp.float32)
                * score_scale
            )
            scores = jnp.where(allowed[None], scores, MASKED)
            return (first_row, key_start, query_rows, key_rows, value_rows, scores)

        def forward_block(number):
            first_row, key_start, query_rows, key_rows, value_rows, scores = block_inputs(
                number, queries
            )
            highest = jnp.max(scores, axis=-1, keepdims=True)
            powers = jnp.exp(scores - highest)
            denominator = jnp.sum(powers, axis=-1, keepdims=True)
            probs = powers / denominator
            mixed = jnp.einsum(
                "hqk,khd->qhd",
                probs.astype(jnp.bfloat16),
                value_rows,
                preferred_element_type=jnp.float32,
            )
            return (mixed.reshape(block_rows, model_width), highest + jnp.log(denominator))

        block_numbers = jnp.arange(blocks, dtype=jnp.int32)
        mixed_blocks, log_totals = lax.map(forward_block, block_numbers)
        mixed_rows = mixed_blocks.reshape(stretch_rows, model_width).astype(jnp.bfloat16)
        after_attn = stream + jnp.dot(mixed_rows, out_weight, preferred_element_type=jnp.float32)
        normed_two = layer_norm(after_attn, gain_two).astype(jnp.bfloat16)
        gate_up = jnp.dot(normed_two, in_weight, preferred_element_type=jnp.float32)
        gate_part = gate_up[:, :hidden_units]
        up_part = gate_up[:, hidden_units:]
        activated = gelu_gate(gate_part, up_part).astype(jnp.bfloat16)
        results.append(
            (
                after_attn + jnp.dot(activated, down_weight, preferred_element_type=jnp.float32)
            ).astype(jnp.bfloat16)
        )
        weights = fetch_weights()
        qkv_weight, out_weight, in_weight, down_weight = (
            weights[2],
            weights[3],
            weights[4],
            weights[5],
        )
        seed_rows = cotangent[micro_index, 0]
        grad_down_weight = contract_rows(activated, seed_rows)
        grad_hidden = times_back(seed_rows, down_weight)
        gelu_back = jax.vjp(gelu_gate, gate_part, up_part)[1]
        grad_gate, grad_up = gelu_back(grad_hidden)
        grad_gate_up = jnp.concatenate([grad_gate, grad_up], axis=1).astype(jnp.bfloat16)
        grad_in_weight = contract_rows(normed_two, grad_gate_up)
        grad_normed_two = times_back(grad_gate_up, in_weight)
        norm_back_two = jax.vjp(layer_norm, after_attn, gain_two)[1]
        grad_after_part, grad_gain_two = norm_back_two(grad_normed_two)
        grad_after = seed_rows.astype(jnp.float32) + grad_after_part
        grad_branch = grad_after.astype(jnp.bfloat16)
        grad_out_weight = contract_rows(mixed_rows, grad_branch)
        grad_mixed = times_back(grad_branch, out_weight).astype(jnp.bfloat16)

        def backward_block(carry, number):
            key_grad, value_grad = carry
            first_row, key_start, query_rows, key_rows, value_rows, scores = block_inputs(
                number, queries
            )
            grad_rows = lax.dynamic_slice_in_dim(grad_mixed, first_row, block_rows, 0).reshape(
                block_rows, head_count, head_size
            )
            probs = jnp.exp(scores - log_totals[number])
            grad_probs = jnp.einsum(
                "qhd,khd->hqk", grad_rows, value_rows, preferred_element_type=jnp.float32
            )
            centred = jnp.sum(probs * grad_probs, axis=-1, keepdims=True)
            grad_scores = (probs * (grad_probs - centred)).astype(jnp.bfloat16)
            grad_query = (
                jnp.einsum(
                    "hqk,khd->qhd", grad_scores, key_rows, preferred_element_type=jnp.float32
                )
                * score_scale
            )
            grad_key = (
                jnp.einsum(
                    "hqk,qhd->khd", grad_scores, query_rows, preferred_element_type=jnp.float32
                )
                * score_scale
            )
            grad_value = jnp.einsum(
                "hqk,qhd->khd",
                probs.astype(jnp.bfloat16),
                grad_rows,
                preferred_element_type=jnp.float32,
            )
            key_grad = lax.dynamic_update_slice_in_dim(
                key_grad,
                lax.dynamic_slice_in_dim(key_grad, key_start, key_span, 0)
                + grad_key.reshape(key_span, model_width),
                key_start,
                0,
            )
            value_grad = lax.dynamic_update_slice_in_dim(
                value_grad,
                lax.dynamic_slice_in_dim(value_grad, key_start, key_span, 0)
                + grad_value.reshape(key_span, model_width),
                key_start,
                0,
            )
            return ((key_grad, value_grad), grad_query.reshape(block_rows, model_width))

        empty = jnp.zeros((extent, model_width), jnp.float32)
        (wide_key_grad, wide_value_grad), query_blocks = lax.scan(
            backward_block, (empty, empty), block_numbers
        )
        own_first = reach_count * stretch_rows
        own_key_grad = wide_key_grad[own_first : own_first + stretch_rows]
        own_value_grad = wide_value_grad[own_first : own_first + stretch_rows]
        for distance in offsets:
            region = reach_count - distance
            returned = (
                from_behind(
                    wide_key_grad[region * stretch_rows : (region + 1) * stretch_rows].astype(
                        jnp.bfloat16
                    ),
                    "seq",
                    -distance,
                ).astype(jnp.float32),
                from_behind(
                    wide_value_grad[region * stretch_rows : (region + 1) * stretch_rows].astype(
                        jnp.bfloat16
                    ),
                    "seq",
                    -distance,
                ).astype(jnp.float32),
            )
            own_key_grad = own_key_grad + returned[0]
            own_value_grad = own_value_grad + returned[1]

        def turned(raw_rows):
            return rotate(raw_rows, cosines, sines)

        rope_back = jax.vjp(turned, query_raw)[1]
        grad_query_raw = rope_back(query_blocks.reshape(stretch_rows, head_count, head_size))[0]
        grad_key_raw = rope_back(own_key_grad.reshape(stretch_rows, head_count, head_size))[0]
        grad_projected = jnp.concatenate(
            [
                grad_query_raw.reshape(stretch_rows, model_width),
                grad_key_raw.reshape(stretch_rows, model_width),
                own_value_grad,
            ],
            axis=1,
        ).astype(jnp.bfloat16)
        grad_qkv_weight = contract_rows(normed_one, grad_projected)
        grad_normed_one = times_back(grad_projected, qkv_weight)
        norm_back_one = jax.vjp(layer_norm, stream, gain_one)[1]
        grad_stream_part, grad_gain_one = norm_back_one(grad_normed_one)
        input_grads.append(grad_after + grad_stream_part)
        gradients = (
            grad_gain_one,
            grad_gain_two,
            grad_qkv_weight,
            grad_out_weight,
            grad_in_weight,
            grad_down_weight,
        )
        totals = (
            gradients
            if totals is None
            else tuple((older + newer for older, newer in zip(totals, gradients)))
        )
    totals = jax.tree.map(
        lambda part: part.astype(jnp.float32),
        lax.psum_scatter(shortened(totals), ("seq", "dp"), scatter_dimension=0, tiled=True),
    )
    summed = jax.tree.map(lambda part: part.astype(jnp.float32), lax.psum(shortened(totals), "rep"))
    outputs = jnp.stack(results)[:, None]
    grad_inputs = jnp.stack(input_grads)[:, None]
    return (outputs, grad_inputs, summed[0], summed[1], summed[2], summed[3], summed[4], summed[5])


def solution(mesh):
    return jax.shard_map(
        body,
        mesh=mesh,
        in_specs=(
            P(None, ("dp", "rep"), "seq", None),
            P(None, ("dp", "rep"), None),
            P(None, ("dp", "rep"), "seq", None),
            P(("seq", "dp")),
            P(("seq", "dp")),
            P(("seq", "dp"), None),
            P(("seq", "dp"), None),
            P(("seq", "dp"), None),
            P(("seq", "dp"), None),
        ),
        out_specs=(
            P(None, ("dp", "rep"), "seq", None),
            P(None, ("dp", "rep"), "seq", None),
            P(("seq", "dp")),
            P(("seq", "dp")),
            P(("seq", "dp"), None),
            P(("seq", "dp"), None),
            P(("seq", "dp"), None),
            P(("seq", "dp"), None),
        ),
        check_vma=False,
    )
```

profile of v0, /device:TPU:0, one launch (start us, length us, event | category | flops | bytes accessed | tf_op | source)
XLA Modules:
  0.0 2256.8 jit_solution(1532360114424424220)
XLA Ops:
  160.6 92.9 %collective-permute-done = bf16[1024,1024]{1,0:T(8,128)(2,1)} collective-permute-done((bf16[1024,1024]{1,0:T(8,128)(2,1)}, bf16[1024,1024]{1,0:T(8,128)(2,1)}, u32[]{:S(2)}, u32[]{:S(2)}) %collective-permute-start) | collective-permute-done | bytes 2097184 | tf_op jit(solution)/shard_map/ppermute | solution.py:20
  286.2 149.5 %while.68 = (s32[]{:T(128)}, bf16[2,512,1024]{2,1,0:T(8,128)(2,1)}, f32[2,16,512,1]{2,1,3,0:T(8,128)S(1)}, s32[2]{0:T(128)S(1)}, bf16[3072,1024]{0,1:T(8,128)(2,...) while((s32[]{:T(128)}, bf16[2,512,1024]{2,1,0:T(8,128)(2,1)}, ...), condition=%wide.region_7.8_spmd, body=%wide.region_4.7_spmd.sunk | while | flops 3376930816 | bytes 193225552 | solution.py:207
  295.2 20.5 fusion.243
  315.7 22.2 fusion.244
  337.9 21.4 fusion.245
  369.9 20.5 fusion.243
  390.4 22.2 fusion.244
  412.7 21.4 fusion.245
  458.2 150.1 %while.69 = (s32[]{:T(128)}, bf16[2,512,1024]{2,1,0:T(8,128)(2,1)}, f32[2,16,512,1]{2,1,3,0:T(8,128)S(1)}, s32[2]{0:T(128)S(1)}, bf16[3072,1024]{0,1:T(8,128)(2,...) while((s32[]{:T(128)}, bf16[2,512,1024]{2,1,0:T(8,128)(2,1)}, ...), condition=%wide.region_17.18_spmd, body=%wide.region_14.17_spmd.sunk | while | flops 3376930816 | bytes 193225552 | solution.py:207
  467.4 20.5 fusion.250
  487.9 22.2 fusion.251
  510.2 21.4 fusion.252
  542.2 20.5 fusion.250
  562.7 22.2 fusion.251
  584.9 21.4 fusion.252
  623.2 20.8 fusion.127
  644.0 37.0 %add_convert_fusion.3 = (bf16[1024,2624]{1,0:T(8,128)(2,1)}, f32[1024,2624]{1,0:T(8,128)S(1)}, f32[1024,2624]{1,0:T(8,128)}) fusion(f32[1024,5248]{1,0:T(8,128)} %fusion.127, bf16[2624,1024]{1,0:T(8,128)(2,1)} %all-gather.13.cloned.1.call-done, bf16[2,1,1024,1024]{3,2,1,0:T(8,128)(2,1)} %param.19), kind=kOutput, calls=%fused_computation.93 | convolution fusion | flops 5699076096 | bytes 56360960 | tf_op jit(solution)/shard_map/dot_general | solution.py:75
  681.1 16.8 multiply_convert_fusion.3
  697.8 19.5 fusion.128
  717.4 36.1 %add_convert_fusion.2 = (bf16[1024,2624]{1,0:T(8,128)(2,1)}, f32[1024,2624]{1,0:T(8,128)S(1)}, f32[1024,2624]{1,0:T(8,128)}) fusion(f32[1024,5248]{1,0:T(8,128)} %fusion.128, bf16[2624,1024]{1,0:T(8,128)(2,1)} %all-gather.13.cloned.1.call-done, bf16[2,1,1024,1024]{3,2,1,0:T(8,128)(2,1)S(1)} %copy-done.26), kind=kOutput, calls=%fused_computation.91 | convolution fusion | flops 5699076096 | bytes 55836672 | tf_op jit(solution)/shard_map/dot_general | solution.py:75
  753.5 17.0 multiply_convert_fusion.2
  770.6 19.0 fusion.52
  789.6 22.7 %multiply_reduce_fusion.3 = (f32[1024]{0:T(1024)}, f32[1024]{0:T(1024)S(1)}, f32[1024]{0:T(1024)S(1)}, f32[1024]{0:T(1024)}, f32[1024,1024]{0,1:T(8,128)}) fusion(f32[1024,1024]{0,1:T(8,128)} %copy-done.16, f32[1024]{0:T(1024)S(1)} %copy-done.96, f32[1024]{0:T(1024)S(1)} %copy-done.87, f32[1024]{0:T(1024)S(1)} %bitcast.410, f32[1024,1024]{0,1:T(8,128)} %fusion.52, ...), kind=kOutput, calls=%fused_computation.176 | convolution fusion | flops 11042025472 | bytes 38309888 | tf_op jit(solution)/shard_map/dot_general | solution.py:75
  851.8 432.0 %while.71 = (s32[]{:T(128)}, f32[3072,1024]{0,1:T(8,128)}, f32[3072,1024]{0,1:T(8,128)}, f32[2,512,1024]{1,0,2:T(2,128)}, s32[2]{0:T(128)S(1)}, /*index=5*/bf16[...) while((s32[]{:T(128)}, f32[3072,1024]{0,1:T(8,128)}, ...), condition=%wide.region_31.32_spmd, body=%wide.region_29.31_spmd.sunk | while | flops 8251760640 | bytes 489939328 | solution.py:291
  857.9 21.0 fusion.276
  889.5 37.0 %multiply_reduce_fusion.11 = (f32[16,512]{1,0:T(8,128)S(1)}, f32[16,512,1536]{2,1,0:T(8,128)}) fusion(f32[16,512,1536]{2,1,0:T(8,128)} %fusion.276, f32[16,512]{1,0:T(8,128)S(1)} %dynamic-slice_bitcast_fusion.5, pred[512,1536]{1,0:T(8,128)(4,1)} %fusion.277, bf16[512,16,64]{0,2,1:T(8,128)(2,1)} %bitcast.365, bf16[1536,16,64]{0,2,1:T(8,128)(2,1)} %bitcast.355), kind=kOutput, calls=%fused_computation.61.clone.1 | convolution fusion | flops 1673519104 | bytes 105709568 | tf_op jit(solution)/shard_map/while/body/eval_jaxpr/qhd,khd->hqk/dot_general | solution.py:251
  926.5 41.3 %multiply_convert_fusion.15 = bf16[16,512,1536]{2,1,0:T(8,128)(2,1)} fusion(f32[16,512,1536]{2,1,0:T(8,128)} %get-tuple-element.1489, f32[16,512,1536]{2,1,0:T(8,128)} %fusion.276, f32[16,512]{1,0:T(8,128)S(1)} %get-tuple-element.1490, f32[16,512]{1,0:T(8,128)S(1)} %dynamic-slice_bitcast_fusion.5, pred[512,1536]{1,0:T(8,128)(4,1)} %fusion.277), kind=kLoop, calls=%fused_computation.60.clone.1 | loop fusion | flops 75497472 | bytes 126681088 | tf_op jit(solution)/shard_map/while/body/eval_jaxpr/convert_element_type | solution.py:255
  978.6 22.9 %fusion.278 = f32[16,64,1536]{2,1,0:T(8,128)} fusion(bf16[512,16,64]{0,2,1:T(8,128)(2,1)S(1)} %bitcast.366, f32[16,512,1536]{2,1,0:T(8,128)} %fusion.276, f32[16,512]{1,0:T(8,128)S(1)} %dynamic-slice_bitcast_fusion.5, pred[512,1536]{1,0:T(8,128)(4,1)S(1)} %copy-done), kind=kOutput, calls=%fused_computation.64.clone.1 | convolution fusion | flops 1660944384 | bytes 58490880 | tf_op jit(solution)/shard_map/while/body/eval_jaxpr/hqk,qhd->khd/dot_general | solution.py:268
  1001.5 11.2 constant_dynamic-update-slice_fusion.13
  1012.7 14.1 convolution_multiply_fusion.11
  1030.5 37.7 %dynamic_update_slice.115 = f32[2,512,1024]{1,0,2:T(2,128)} dynamic-update-slice(f32[2,512,1024]{1,0,2:T(2,128)} %get-tuple-element.1658, f32[1,512,1024]{1,0,2:T(1,128)S(1)} %copy.156, s32[]{:T(128)} %get-tuple-element.1655, s32[]{:T(128)} %constant.440.clone.1..sunk.3, s32[]{:T(128)} %constant.440.clone.1..sunk.3) | dynamic-update-slice | bytes 4194308 | tf_op jit(solution)/shard_map/while/body/jit(dynamic_update_index_in_dim)/dynamic_update_slice | solution.py:207
  1073.8 20.6 fusion.276
  1105.0 37.0 %multiply_reduce_fusion.11 = (f32[16,512]{1,0:T(8,128)S(1)}, f32[16,512,1536]{2,1,0:T(8,128)}) fusion(f32[16,512,1536]{2,1,0:T(8,128)} %fusion.276, f32[16,512]{1,0:T(8,128)S(1)} %dynamic-slice_bitcast_fusion.5, pred[512,1536]{1,0:T(8,128)(4,1)} %fusion.277, bf16[512,16,64]{0,2,1:T(8,128)(2,1)} %bitcast.365, bf16[1536,16,64]{0,2,1:T(8,128)(2,1)} %bitcast.355), kind=kOutput, calls=%fused_computation.61.clone.1 | convolution fusion | flops 1673519104 | bytes 105709568 | tf_op jit(solution)/shard_map/while/body/eval_jaxpr/qhd,khd->hqk/dot_general | solution.py:251
  1142.1 41.3 %multiply_convert_fusion.15 = bf16[16,512,1536]{2,1,0:T(8,128)(2,1)} fusion(f32[16,512,1536]{2,1,0:T(8,128)} %get-tuple-element.1489, f32[16,512,1536]{2,1,0:T(8,128)} %fusion.276, f32[16,512]{1,0:T(8,128)S(1)} %get-tuple-element.1490, f32[16,512]{1,0:T(8,128)S(1)} %dynamic-slice_bitcast_fusion.5, pred[512,1536]{1,0:T(8,128)(4,1)} %fusion.277), kind=kLoop, calls=%fused_computation.60.clone.1 | loop fusion | flops 75497472 | bytes 126681088 | tf_op jit(solution)/shard_map/while/body/eval_jaxpr/convert_element_type | solution.py:255
  1194.2 22.9 %fusion.278 = f32[16,64,1536]{2,1,0:T(8,128)} fusion(bf16[512,16,64]{0,2,1:T(8,128)(2,1)S(1)} %bitcast.366, f32[16,512,1536]{2,1,0:T(8,128)} %fusion.276, f32[16,512]{1,0:T(8,128)S(1)} %dynamic-slice_bitcast_fusion.5, pred[512,1536]{1,0:T(8,128)(4,1)S(1)} %copy-done), kind=kOutput, calls=%fused_computation.64.clone.1 | convolution fusion | flops 1660944384 | bytes 58490880 | tf_op jit(solution)/shard_map/while/body/eval_jaxpr/hqk,qhd->khd/dot_general | solution.py:268
  1217.1 11.1 constant_dynamic-update-slice_fusion.13
  1228.2 14.1 convolution_multiply_fusion.11
  1246.0 37.7 %dynamic_update_slice.115 = f32[2,512,1024]{1,0,2:T(2,128)} dynamic-update-slice(f32[2,512,1024]{1,0,2:T(2,128)} %get-tuple-element.1658, f32[1,512,1024]{1,0,2:T(1,128)S(1)} %copy.156, s32[]{:T(128)} %get-tuple-element.1655, s32[]{:T(128)} %constant.440.clone.1..sunk.3, s32[]{:T(128)} %constant.440.clone.1..sunk.3) | dynamic-update-slice | bytes 4194308 | tf_op jit(solution)/shard_map/while/body/jit(dynamic_update_index_in_dim)/dynamic_update_slice | solution.py:207
  1330.4 431.5 %while.70 = (s32[]{:T(128)}, f32[3072,1024]{0,1:T(8,128)}, f32[3072,1024]{0,1:T(8,128)}, f32[2,512,1024]{1,0,2:T(2,128)}, s32[2]{0:T(128)S(1)}, /*index=5*/bf16[...) while((s32[]{:T(128)}, f32[3072,1024]{0,1:T(8,128)}, ...), condition=%wide.region_24.25_spmd, body=%wide.region_22.24_spmd.sunk | while | flops 8251760640 | bytes 489939328 | solution.py:291
  1336.4 20.6 fusion.263
  1367.7 37.0 %multiply_reduce_fusion.10 = (f32[16,512]{1,0:T(8,128)S(1)}, f32[16,512,1536]{2,1,0:T(8,128)}) fusion(f32[16,512,1536]{2,1,0:T(8,128)} %fusion.263, f32[16,512]{1,0:T(8,128)S(1)} %dynamic-slice_bitcast_fusion.4, pred[512,1536]{1,0:T(8,128)(4,1)} %fusion.264, bf16[512,16,64]{0,2,1:T(8,128)(2,1)} %bitcast.367, bf16[1536,16,64]{0,2,1:T(8,128)(2,1)} %bitcast.356), kind=kOutput, calls=%fused_computation.37.clone.1 | convolution fusion | flops 1673519104 | bytes 105709568 | tf_op jit(solution)/shard_map/while/body/eval_jaxpr/qhd,khd->hqk/dot_general | solution.py:251
  1404.6 41.3 %multiply_convert_fusion.14 = bf16[16,512,1536]{2,1,0:T(8,128)(2,1)} fusion(f32[16,512,1536]{2,1,0:T(8,128)} %get-tuple-element.1473, f32[16,512,1536]{2,1,0:T(8,128)} %fusion.263, f32[16,512]{1,0:T(8,128)S(1)} %get-tuple-element.1474, f32[16,512]{1,0:T(8,128)S(1)} %dynamic-slice_bitcast_fusion.4, pred[512,1536]{1,0:T(8,128)(4,1)} %fusion.264), kind=kLoop, calls=%fused_computation.36.clone.1 | loop fusion | flops 75497472 | bytes 126681088 | tf_op jit(solution)/shard_map/while/body/eval_jaxpr/convert_element_type | solution.py:255
  1456.7 23.0 %fusion.265 = f32[16,64,1536]{2,1,0:T(8,128)} fusion(bf16[512,16,64]{0,2,1:T(8,128)(2,1)S(1)} %bitcast.368, f32[16,512,1536]{2,1,0:T(8,128)} %fusion.263, f32[16,512]{1,0:T(8,128)S(1)} %dynamic-slice_bitcast_fusion.4, pred[512,1536]{1,0:T(8,128)(4,1)S(1)} %copy-done.1), kind=kOutput, calls=%fused_computation.40.clone.1 | convolution fusion | flops 1660944384 | bytes 58490880 | tf_op jit(solution)/shard_map/while/body/eval_jaxpr/hqk,qhd->khd/dot_general | solution.py:268
  1479.7 11.1 constant_dynamic-update-slice_fusion.12
  1490.7 14.0 convolution_multiply_fusion.9
  1508.5 37.7 %dynamic_update_slice.113 = f32[2,512,1024]{1,0,2:T(2,128)} dynamic-update-slice(f32[2,512,1024]{1,0,2:T(2,128)} %get-tuple-element.1604, f32[1,512,1024]{1,0,2:T(1,128)S(1)} %copy.154, s32[]{:T(128)} %get-tuple-element.1601, s32[]{:T(128)} %constant.440.clone.1..sunk.2, s32[]{:T(128)} %constant.440.clone.1..sunk.2) | dynamic-update-slice | bytes 4194308 | tf_op jit(solution)/shard_map/while/body/jit(dynamic_update_index_in_dim)/dynamic_update_slice | solution.py:207
  1551.9 20.6 fusion.263
  1583.1 37.0 %multiply_reduce_fusion.10 = (f32[16,512]{1,0:T(8,128)S(1)}, f32[16,512,1536]{2,1,0:T(8,128)}) fusion(f32[16,512,1536]{2,1,0:T(8,128)} %fusion.263, f32[16,512]{1,0:T(8,128)S(1)} %dynamic-slice_bitcast_fusion.4, pred[512,1536]{1,0:T(8,128)(4,1)} %fusion.264, bf16[512,16,64]{0,2,1:T(8,128)(2,1)} %bitcast.367, bf16[1536,16,64]{0,2,1:T(8,128)(2,1)} %bitcast.356), kind=kOutput, calls=%fused_computation.37.clone.1 | convolution fusion | flops 1673519104 | bytes 105709568 | tf_op jit(solution)/shard_map/while/body/eval_jaxpr/qhd,khd->hqk/dot_general | solution.py:251
  1620.1 41.3 %multiply_convert_fusion.14 = bf16[16,512,1536]{2,1,0:T(8,128)(2,1)} fusion(f32[16,512,1536]{2,1,0:T(8,128)} %get-tuple-element.1473, f32[16,512,1536]{2,1,0:T(8,128)} %fusion.263, f32[16,512]{1,0:T(8,128)S(1)} %get-tuple-element.1474, f32[16,512]{1,0:T(8,128)S(1)} %dynamic-slice_bitcast_fusion.4, pred[512,1536]{1,0:T(8,128)(4,1)} %fusion.264), kind=kLoop, calls=%fused_computation.36.clone.1 | loop fusion | flops 75497472 | bytes 126681088 | tf_op jit(solution)/shard_map/while/body/eval_jaxpr/convert_element_type | solution.py:255
  1672.2 23.0 %fusion.265 = f32[16,64,1536]{2,1,0:T(8,128)} fusion(bf16[512,16,64]{0,2,1:T(8,128)(2,1)S(1)} %bitcast.368, f32[16,512,1536]{2,1,0:T(8,128)} %fusion.263, f32[16,512]{1,0:T(8,128)S(1)} %dynamic-slice_bitcast_fusion.4, pred[512,1536]{1,0:T(8,128)(4,1)S(1)} %copy-done.1), kind=kOutput, calls=%fused_computation.40.clone.1 | convolution fusion | flops 1660944384 | bytes 58490880 | tf_op jit(solution)/shard_map/while/body/eval_jaxpr/hqk,qhd->khd/dot_general | solution.py:268
  1706.2 14.0 convolution_multiply_fusion.9
  1724.0 37.7 %dynamic_update_slice.113 = f32[2,512,1024]{1,0,2:T(2,128)} dynamic-update-slice(f32[2,512,1024]{1,0,2:T(2,128)} %get-tuple-element.1604, f32[1,512,1024]{1,0,2:T(1,128)S(1)} %copy.154, s32[]{:T(128)} %get-tuple-element.1601, s32[]{:T(128)} %constant.440.clone.1..sunk.2, s32[]{:T(128)} %constant.440.clone.1..sunk.2) | dynamic-update-slice | bytes 4194308 | tf_op jit(solution)/shard_map/while/body/jit(dynamic_update_index_in_dim)/dynamic_update_slice | solution.py:207
  1852.2 36.9 %collective-permute-done.15 = bf16[1024,1024]{0,1:T(8,128)(2,1)S(1)} collective-permute-done((bf16[1024,1024]{0,1:T(8,128)(2,1)}, bf16[1024,1024]{0,1:T(8,128)(2,1)S(1)}, u32[]{:S(2)}, u32[]{:S(2)}) %collective-permute-start.15) | collective-permute-done | bytes 2097184 | tf_op jit(solution)/shard_map/ppermute | solution.py:20
  1893.3 41.1 %collective-permute-done.11 = bf16[1024,1024]{0,1:T(8,128)(2,1)} collective-permute-done((bf16[1024,1024]{0,1:T(8,128)(2,1)}, bf16[1024,1024]{0,1:T(8,128)(2,1)}, u32[]{:S(2)}, u32[]{:S(2)}) %collective-permute-start.11) | collective-permute-done | bytes 2097184 | tf_op jit(solution)/shard_map/ppermute | solution.py:20
  1940.3 13.5 fusion.81
  1953.8 16.5 add_convert_fusion.1
  1971.0 21.2 fusion.53
  1992.2 23.0 %add_convert_fusion = bf16[1024,5248]{1,0:T(8,128)(2,1)} fusion(f32[1024,5248]{1,0:T(8,128)} %fusion.53, bf16[1024,2624]{1,0:T(8,128)(2,1)} %get-tuple-element.1133, bf16[1024,2624]{1,0:T(8,128)(2,1)} %get-tuple-element.1113, f32[1024,1024]{0,1:T(8,128)} %copy-done.17, f32[1024]{0:T(1024)S(1)} %copy-done.99, f32[1024]{0:T(1024)S(1)} %copy-done.90, ...), kind=kOutput, calls=%fused_computation.84 | convolution fusion | flops 11042291712 | bytes 47198208 | tf_op jit(solution)/shard_map/dot_general | solution.py:69
  2046.6 13.9 fusion.76
  2062.5 13.6 fusion.74
  2076.1 44.7 %reduce-scatter.9.cloned.1.call-done = bf16[128,5248]{1,0:T(8,128)(2,1)} async-done(((bf16[1024,5248]{1,0:T(8,128)(2,1)}), bf16[128,5248]{1,0:T(8,128)(2,1)}) %reduce-scatter.9.cloned.1.call-update) | async-done | bytes 1343504 | tf_op jit(solution)/shard_map/reduce_scatter | solution.py:352
  2124.6 13.1 all-reduce.10
  2137.8 12.1 all-reduce.11
  2173.5 69.9 %all-reduce.15.cloned.1.call-done = (bf16[128,3072]{1,0:T(8,128)(2,1)}, bf16[128,1024]{1,0:T(8,128)(2,1)}, bf16[128,5248]{1,0:T(8,128)(2,1)}, bf16[328,1024]{1,0:T(8,128)(2,1)}) async-done(((bf16[128,3072]{1,0:T(8,128)(2,1)}, bf16[128,1024]{1,0:T(8,128)(2,1)}, bf16[128,5248]{1,0:T(8,128)(2,1)}, bf16[328,1024]{1,0:T(8,128)(2,1)}), (bf16[128,3072]{1,0:T(8,128)(2,1)}, bf16[128,1024]{1,0:T(8,128)(2,1)}, ...) | async-done | bytes 3063824 | tf_op jit(solution)/shard_map/psum | solution.py:354
  (521 shorter events, 639.8 us)
Async XLA Ops:
  7.2 59.6 %all-gather.7.cloned.1.call-start = ((), (), s32[]{:S(2)}) async-start(), calls=%async_computation.4 | async-start | bytes 7077888 | tf_op jit(solution)/shard_map/all_gather | solution.py:107
  7.9 600.5 %all-gather.9.cloned.1.call-start = ((), (), s32[]{:S(2)}) async-start(), calls=%async_computation.5 | async-start | bytes 2359296 | tf_op jit(solution)/shard_map/all_gather | solution.py:108
  8.6 614.6 %all-gather.11.cloned.1.call-start = ((), (), s32[]{:S(2)}) async-start(), calls=%async_computation.6 | async-start | bytes 12091392 | tf_op jit(solution)/shard_map/all_gather | solution.py:109
  9.4 634.7 %all-gather.13.cloned.1.call-start = ((), (), s32[]{:S(2)}) async-start(), calls=%async_computation.7 | async-start | bytes 6045696 | tf_op jit(solution)/shard_map/all_gather | solution.py:110
  10.0 2066.1 %reduce-scatter.7.cloned.1.call-start = ((), (), s32[]{:S(2)}) async-start(), calls=%async_computation.9 | async-start | bytes 2359296 | tf_op jit(solution)/shard_map/reduce_scatter | solution.py:352
  19.2 100.9 %copy-start.8 = (bf16[1,1,1024,1024]{2,3,1,0:T(8,128)(2,1)}, bf16[1,1,1024,1024]{2,3,1,0:T(8,128)(2,1)S(1)}, u32[]{:S(2)}) copy-start(bf16[1,1,1024,1024]{2,3,1,0:T(8,128)(2,1)S(1)} %copy.116) | copy-start | bytes 6291460
  19.6 20.8 copy-start.103
  26.0 30.4 %copy-start.64 = (f32[1024]{0:T(1024)}, f32[1024]{0:T(1024)S(1)}, u32[]{:S(2)}) copy-start(f32[1024]{0:T(1024)S(1)} %get-tuple-element.1203) | copy-start | bytes 12292
  26.0 40.7 %copy-start.76 = (f32[1024]{0:T(1024)}, f32[1024]{0:T(1024)S(1)}, u32[]{:S(2)}) copy-start(f32[1024]{0:T(1024)S(1)} %get-tuple-element.1204) | copy-start | bytes 12292
  28.2 38.5 %copy-start.91 = (f32[1024]{0:T(1024)}, f32[1024]{0:T(1024)S(1)}, u32[]{:S(2)}) copy-start(f32[1024]{0:T(1024)S(1)} %fusion.111) | copy-start | bytes 12292
  39.0 27.8 %copy-start.67 = (f32[8,1,128]{2,1,0:T(1,128)}, f32[8,1,128]{2,1,0:T(1,128)S(1)}, u32[]{:S(2)}) copy-start(f32[8,1,128]{2,1,0:T(1,128)S(1)} %convert_element_type.286) | copy-start | bytes 12292
  66.0 28.7 %copy-start.41 = (f32[1024,32]{0,1:T(8,128)}, f32[1024,32]{0,1:T(8,128)S(1)}, u32[]{:S(2)}) copy-start(f32[1024,32]{0,1:T(8,128)S(1)} %get-tuple-element.1177) | copy-start | bytes 393220
  66.0 28.7 %copy-start.43 = (f32[1024,32]{0,1:T(8,128)}, f32[1024,32]{0,1:T(8,128)S(1)}, u32[]{:S(2)}) copy-start(f32[1024,32]{0,1:T(8,128)S(1)} %get-tuple-element.1178) | copy-start | bytes 393220
  66.1 77.8 %copy-start.45 = (f32[1024,32]{0,1:T(8,128)}, f32[1024,32]{0,1:T(8,128)S(1)}, u32[]{:S(2)}) copy-start(f32[1024,32]{0,1:T(8,128)S(1)} %get-tuple-element.1189) | copy-start | bytes 393220
  94.7 25.4 %slice-start.2 = ((s8[6291456]{0:T(1024)(128)(4,1)}), s8[4194304]{0:T(1024)(128)(4,1)S(1)}, s32[]{:S(2)}) async-start(s8[6291456]{0:T(1024)(128)(4,1)} %bitcast.416), calls=%async_computation.15 | async-start | bytes 8388608
  94.8 25.4 %slice-start.3 = ((s8[6291456]{0:T(1024)(128)(4,1)}), s8[2097152]{0:T(1024)(128)(4,1)S(1)}, s32[]{:S(2)}) async-start(s8[6291456]{0:T(1024)(128)(4,1)} %bitcast.416), calls=%async_computation.16 | async-start | bytes 4194304
  101.7 18.5 copy-start.65
  101.7 18.5 copy-start.68
  101.7 18.5 copy-start.70
  103.2 173.3 %collective-permute-start.2 = (bf16[1024,1024]{0,1:T(8,128)(2,1)}, bf16[1024,1024]{0,1:T(8,128)(2,1)}, u32[]{:S(2)}, u32[]{:S(2)}) collective-permute-start(bf16[1024,1024]{0,1:T(8,128)(2,1)} %bitcast.48), channel_id=1, source_target_pairs={{0,16},{1,17},{2,18},{3,19},{4,20},{5,21},{6,22},{7,23},{8,24},{9,... | collective-permute-start | bytes 6291464 | tf_op jit(solution)/shard_map/ppermute | solution.py:20
  106.3 171.9 %collective-permute-start.3 = (bf16[1024,1024]{0,1:T(8,128)(2,1)}, bf16[1024,1024]{0,1:T(8,128)(2,1)}, u32[]{:S(2)}, u32[]{:S(2)}) collective-permute-start(bf16[1024,1024]{0,1:T(8,128)(2,1)} %bitcast.48), channel_id=1, source_target_pairs={{16,0},{17,1},{18,2},{19,3},{20,4},{21,5},{22,6},{23,7},{24,8},{25... | collective-permute-start | bytes 6291464 | tf_op jit(solution)/shard_map/ppermute | solution.py:20
  111.5 142.1 %collective-permute-start = (bf16[1024,1024]{1,0:T(8,128)(2,1)}, bf16[1024,1024]{1,0:T(8,128)(2,1)}, u32[]{:S(2)}, u32[]{:S(2)}) collective-permute-start(bf16[1024,1024]{1,0:T(8,128)(2,1)} %slice.303), channel_id=1, source_target_pairs={{0,16},{1,17},{2,18},{3,19},{4,20},{5,21},{6,22},{7,23},{8,24},{9,... | collective-permute-start | bytes 6291464 | tf_op jit(solution)/shard_map/ppermute | solution.py:20
  118.6 136.9 %collective-permute-start.1 = (bf16[1024,1024]{1,0:T(8,128)(2,1)}, bf16[1024,1024]{1,0:T(8,128)(2,1)}, u32[]{:S(2)}, u32[]{:S(2)}) collective-permute-start(bf16[1024,1024]{1,0:T(8,128)(2,1)} %slice.303), channel_id=1, source_target_pairs={{16,0},{17,1},{18,2},{19,3},{20,4},{21,5},{22,6},{23,7},{24,8},{25... | collective-permute-start | bytes 6291464 | tf_op jit(solution)/shard_map/ppermute | solution.py:20
  150.5 299.8 %collective-permute-start.6 = (bf16[1024,1024]{0,1:T(8,128)(2,1)}, bf16[1024,1024]{0,1:T(8,128)(2,1)}, u32[]{:S(2)}, u32[]{:S(2)}) collective-permute-start(bf16[1024,1024]{0,1:T(8,128)(2,1)} %bitcast.61), channel_id=1, source_target_pairs={{0,16},{1,17},{2,18},{3,19},{4,20},{5,21},{6,22},{7,23},{8,24},{9,... | collective-permute-start | bytes 6291464 | tf_op jit(solution)/shard_map/ppermute | solution.py:20
  253.5 196.7 %collective-permute-start.7 = (bf16[1024,1024]{0,1:T(8,128)(2,1)}, bf16[1024,1024]{0,1:T(8,128)(2,1)}, u32[]{:S(2)}, u32[]{:S(2)}) collective-permute-start(bf16[1024,1024]{0,1:T(8,128)(2,1)} %bitcast.61), channel_id=1, source_target_pairs={{16,0},{17,1},{18,2},{19,3},{20,4},{21,5},{22,6},{23,7},{24,8},{25... | collective-permute-start | bytes 6291464 | tf_op jit(solution)/shard_map/ppermute | solution.py:20
  255.5 180.3 %collective-permute-start.4 = (bf16[1024,1024]{1,0:T(8,128)(2,1)}, bf16[1024,1024]{1,0:T(8,128)(2,1)}, u32[]{:S(2)}, u32[]{:S(2)}) collective-permute-start(bf16[1024,1024]{1,0:T(8,128)(2,1)} %slice.302), channel_id=1, source_target_pairs={{0,16},{1,17},{2,18},{3,19},{4,20},{5,21},{6,22},{7,23},{8,24},{9,... | collective-permute-start | bytes 6291464 | tf_op jit(solution)/shard_map/ppermute | solution.py:20
  276.5 159.2 %collective-permute-start.5 = (bf16[1024,1024]{1,0:T(8,128)(2,1)}, bf16[1024,1024]{1,0:T(8,128)(2,1)}, u32[]{:S(2)}, u32[]{:S(2)}) collective-permute-start(bf16[1024,1024]{1,0:T(8,128)(2,1)} %slice.302), channel_id=1, source_target_pairs={{16,0},{17,1},{18,2},{19,3},{20,4},{21,5},{22,6},{23,7},{24,8},{25... | collective-permute-start | bytes 6291464 | tf_op jit(solution)/shard_map/ppermute | solution.py:20
  315.7 22.2 copy-start.2
  390.4 22.2 copy-start.2
  487.9 22.2 copy-start.3
  562.7 22.2 copy-start.3
  620.1 192.2 %copy-start.89 = (f32[1024]{0:T(1024)}, f32[1024]{0:T(1024)S(1)}, u32[]{:S(2)}) copy-start(f32[1024]{0:T(1024)S(1)} %broadcast_multiply_fusion) | copy-start | bytes 12292
  623.2 189.2 %copy-start.98 = (f32[1024]{0:T(1024)}, f32[1024]{0:T(1024)S(1)}, u32[]{:S(2)}) copy-start(f32[1024]{0:T(1024)S(1)} %fusion.114) | copy-start | bytes 12292
  681.1 16.8 copy-start.18
  697.8 19.5 copy-start.26
  770.5 19.0 copy-start.87
  770.5 19.0 copy-start.96
  789.6 22.8 %copy-start.85 = (f32[1024]{0:T(1024)S(1)}, f32[1024]{0:T(1024)}, u32[]{:S(2)}) copy-start(f32[1024]{0:T(1024)} %copy-done.84) | copy-start | bytes 12292
  789.6 22.8 %copy-start.83 = (f32[1024]{0:T(1024)S(1)}, f32[1024]{0:T(1024)}, u32[]{:S(2)}) copy-start(f32[1024]{0:T(1024)} %copy-done.82) | copy-start | bytes 12292
  831.0 1245.1 %reduce-scatter.11.cloned.1.call-start = ((), (), s32[]{:S(2)}) async-start(), calls=%async_computation.11 | async-start | bytes 6045696 | tf_op jit(solution)/shard_map/reduce_scatter | solution.py:352
  1291.9 529.9 %collective-permute-start.12 = (bf16[1024,1024]{0,1:T(8,128)(2,1)}, bf16[1024,1024]{0,1:T(8,128)(2,1)}, u32[]{:S(2)}, u32[]{:S(2)}) collective-permute-start(bf16[1024,1024]{0,1:T(8,128)(2,1)} %get-tuple-element.1143), channel_id=1, source_target_pairs={{16,0},{17,1},{18,2},{19,3},{20,4},{21,5},{22,6},{23,7},{24,8},{25... | collective-permute-start | bytes 6291464 | tf_op jit(solution)/shard_map/ppermute | solution.py:20
  1293.2 530.0 %collective-permute-start.13 = (bf16[1024,1024]{0,1:T(8,128)(2,1)}, bf16[1024,1024]{0,1:T(8,128)(2,1)}, u32[]{:S(2)}, u32[]{:S(2)}) collective-permute-start(bf16[1024,1024]{0,1:T(8,128)(2,1)} %get-tuple-element.1144), channel_id=1, source_target_pairs={{0,16},{1,17},{2,18},{3,19},{4,20},{5,21},{6,22},{7,23},{8,24},{9,... | collective-permute-start | bytes 6291464 | tf_op jit(solution)/shard_map/ppermute | solution.py:20
  1310.0 542.2 %collective-permute-start.14 = (bf16[1024,1024]{0,1:T(8,128)(2,1)}, bf16[1024,1024]{0,1:T(8,128)(2,1)}, u32[]{:S(2)}, u32[]{:S(2)}) collective-permute-start(bf16[1024,1024]{0,1:T(8,128)(2,1)} %get-tuple-element.1145), channel_id=1, source_target_pairs={{16,0},{17,1},{18,2},{19,3},{20,4},{21,5},{22,6},{23,7},{24,8},{25... | collective-permute-start | bytes 6291464 | tf_op jit(solution)/shard_map/ppermute | solution.py:20
  1767.4 20.4 slice-start
  1770.0 62.6 %collective-permute-start.8 = (bf16[1024,1024]{0,1:T(8,128)(2,1)}, bf16[1024,1024]{0,1:T(8,128)(2,1)}, u32[]{:S(2)}, u32[]{:S(2)}) collective-permute-start(bf16[1024,1024]{0,1:T(8,128)(2,1)} %get-tuple-element.1139), channel_id=1, source_target_pairs={{16,0},{17,1},{18,2},{19,3},{20,4},{21,5},{22,6},{23,7},{24,8},{25... | collective-permute-start | bytes 6291464 | tf_op jit(solution)/shard_map/ppermute | solution.py:20
  1771.5 70.4 %collective-permute-start.9 = (bf16[1024,1024]{0,1:T(8,128)(2,1)}, bf16[1024,1024]{0,1:T(8,128)(2,1)}, u32[]{:S(2)}, u32[]{:S(2)}) collective-permute-start(bf16[1024,1024]{0,1:T(8,128)(2,1)} %get-tuple-element.1140), channel_id=1, source_target_pairs={{0,16},{1,17},{2,18},{3,19},{4,20},{5,21},{6,22},{7,23},{8,24},{9,... | collective-permute-start | bytes 6291464 | tf_op jit(solution)/shard_map/ppermute | solution.py:20
  1817.0 259.1 %reduce-scatter.5.cloned.1.call-start = ((), (), s32[]{:S(2)}) async-start(), calls=%async_computation.8 | async-start | bytes 7077888 | tf_op jit(solution)/shard_map/reduce_scatter | solution.py:352
  1821.7 67.3 %collective-permute-start.15 = (bf16[1024,1024]{0,1:T(8,128)(2,1)}, bf16[1024,1024]{0,1:T(8,128)(2,1)S(1)}, u32[]{:S(2)}, u32[]{:S(2)}) collective-permute-start(bf16[1024,1024]{0,1:T(8,128)(2,1)} %get-tuple-element.1146), channel_id=1, source_target_pairs={{0,16},{1,17},{2,18},{3,19},{4,20},{5,21},{6,22},{7,23},{8,24},{9,... | collective-permute-start | bytes 6291464 | tf_op jit(solution)/shard_map/ppermute | solution.py:20
  1823.2 70.0 %collective-permute-start.10 = (bf16[1024,1024]{0,1:T(8,128)(2,1)}, bf16[1024,1024]{0,1:T(8,128)(2,1)}, u32[]{:S(2)}, u32[]{:S(2)}) collective-permute-start(bf16[1024,1024]{0,1:T(8,128)(2,1)} %get-tuple-element.1141), channel_id=1, source_target_pairs={{16,0},{17,1},{18,2},{19,3},{20,4},{21,5},{22,6},{23,7},{24,8},{25... | collective-permute-start | bytes 6291464 | tf_op jit(solution)/shard_map/ppermute | solution.py:20
  1832.6 101.8 %collective-permute-start.11 = (bf16[1024,1024]{0,1:T(8,128)(2,1)}, bf16[1024,1024]{0,1:T(8,128)(2,1)}, u32[]{:S(2)}, u32[]{:S(2)}) collective-permute-start(bf16[1024,1024]{0,1:T(8,128)(2,1)} %get-tuple-element.1142), channel_id=1, source_target_pairs={{0,16},{1,17},{2,18},{3,19},{4,20},{5,21},{6,22},{7,23},{8,24},{9,... | collective-permute-start | bytes 6291464 | tf_op jit(solution)/shard_map/ppermute | solution.py:20
  1840.1 100.2 %copy-start.30 = (bf16[1024,16,64]{0,2,1:T(8,128)(2,1)}, bf16[1024,16,64]{0,2,1:T(8,128)(2,1)S(1)}, u32[]{:S(2)}) copy-start(bf16[1024,16,64]{0,2,1:T(8,128)(2,1)S(1)} %add_convert_fusion.8) | copy-start | bytes 6291460
  1893.1 47.2 %copy-start.34 = (bf16[1024,1024]{0,1:T(8,128)(2,1)}, bf16[1024,1024]{0,1:T(8,128)(2,1)S(1)}, u32[]{:S(2)}) copy-start(bf16[1024,1024]{0,1:T(8,128)(2,1)S(1)} %add_convert_fusion.6) | copy-start | bytes 6291460
  1893.1 47.2 %copy-start.10 = (bf16[1,1,1024,1024]{2,3,1,0:T(8,128)(2,1)S(1)}, bf16[1,1,1024,1024]{2,3,1,0:T(8,128)(2,1)}, u32[]{:S(2)}) copy-start(bf16[1,1,1024,1024]{2,3,1,0:T(8,128)(2,1)} %copy-done.8) | copy-start | bytes 6291460
  1893.1 47.1 %copy-start.32 = (bf16[1024,16,64]{0,2,1:T(8,128)(2,1)S(1)}, bf16[1024,16,64]{0,2,1:T(8,128)(2,1)}, u32[]{:S(2)}) copy-start(bf16[1024,16,64]{0,2,1:T(8,128)(2,1)} %add_convert_fusion.7) | copy-start | bytes 6291460
  1893.1 47.1 %copy-start.66 = (f32[1024]{0:T(1024)S(1)}, f32[1024]{0:T(1024)}, u32[]{:S(2)}) copy-start(f32[1024]{0:T(1024)} %copy-done.64) | copy-start | bytes 12292
  1893.1 47.1 %copy-start.69 = (f32[8,1,128]{2,1,0:T(1,128)S(1)}, f32[8,1,128]{2,1,0:T(1,128)}, u32[]{:S(2)}) copy-start(f32[8,1,128]{2,1,0:T(1,128)} %copy-done.67) | copy-start | bytes 12292
  1893.2 47.1 %copy-start.71 = (f32[1024]{0:T(1024)S(1)}, f32[1024]{0:T(1024)}, u32[]{:S(2)}) copy-start(f32[1024]{0:T(1024)} %fusion.113) | copy-start | bytes 12292
  1970.3 21.9 copy-start.90
  1970.3 21.9 copy-start.99
  1970.3 150.5 %reduce-scatter.9.cloned.1.call-start = ((), (), s32[]{:S(2)}) async-start(), calls=%async_computation.10 | async-start | bytes 12091392 | tf_op jit(solution)/shard_map/reduce_scatter | solution.py:352
  2015.2 228.2 %all-reduce.15.cloned.1.call-start = ((), (), s32[]{:S(2)}) async-start(), calls=%async_computation.12 | async-start | bytes 6127616 | tf_op jit(solution)/shard_map/psum | solution.py:354
  2062.5 58.3 %copy-start.81 = (f32[1024]{0:T(1024)S(1)}, f32[1024]{0:T(1024)}, u32[]{:S(2)}) copy-start(f32[1024]{0:T(1024)} %copy-done.80) | copy-start | bytes 12292
  2120.8 30.1 %copy-start.73 = (f32[1024]{0:T(1024)S(1)}, f32[1024]{0:T(1024)}, u32[]{:S(2)}) copy-start(f32[1024]{0:T(1024)} %copy-done.72) | copy-start | bytes 12292
  2120.8 30.1 %copy-start.75 = (f32[1024]{0:T(1024)S(1)}, f32[1024]{0:T(1024)}, u32[]{:S(2)}) copy-start(f32[1024]{0:T(1024)} %copy-done.74) | copy-start | bytes 12292
  (82 other events, 513.5 us)
Sparse Core Ops, SparseCore 0:
  9.9 48.2 all-gather.6
  60.0 27.8 all-gather.8
  89.9 99.1 all-gather.10
  190.8 62.9 all-gather.12
  831.1 44.8 reduce-scatter.6
  1817.2 76.8 reduce-scatter.10
  1970.4 63.9 reduce-scatter.4
  2038.0 82.7 reduce-scatter.8
  2123.6 119.7 all-reduce.14
where the time goes:
time: 2270 us; the launch traced here: 2260 us
  matrix products  923 us (41%)
  other arithmetic  490 us (22%)
  local copies, waits for them, and re-layouts  419 us (18%)
  waiting for transfers between devices  289 us (13%)
  starting transfers between devices  61.5 us (3%)
  blocking collectives  44.2 us (2%)
    dynamic_update_slice x16, local copies, waits for them, and re-layouts, body(): mixed_blocks, log_totals = lax.map(forward_block, block_numbers)  172 us
    ppermute x16, waiting for transfers between devices, from_behind(): return lax.ppermute(block, axis, route)  172 us
    convert_element_type x4, other arithmetic, backward_block(): grad_scores = (probs * (grad_probs - centred)).astype(jnp.bfloat16)  165 us
    dot_general x8, matrix products, block_inputs(): jnp.einsum('qhd,khd->hqk', query_rows, key_rows, preferred_element_type=j...  165 us
    dot_general x8, matrix products, times_back(): lax.dot_general(left, weight, (((1,), (1,)), ((), ())), preferred_element...  151 us
    dot_general x4, matrix products, backward_block(): jnp.einsum('qhd,khd->hqk', grad_rows, value_rows, preferred_element_type=...  148 us
    dot_general x8, matrix products, contract_rows(): lax.dot_general(left, right, (((0,), (0,)), ((), ())), preferred_element_...  95.7 us
    dot_general x4, matrix products, backward_block(): jnp.einsum('hqk,qhd->khd', probs.astype(jnp.bfloat16), grad_rows, preferr...  91.7 us
  transfers between devices with their start and end apart: 25, of which 7 were waited for; matrix products, arithmetic and copies ran while one was open for 72% of the time, Pallas kernels for 0%

commit v1 on v0

v1 whole, which is shorter than its diff:
```python
import functools

import jax
import jax.numpy as jnp
from jax import lax
from jax.experimental import pallas as pl
from jax.experimental.pallas import tpu as pltpu
from jax.sharding import PartitionSpec as P

HEADS = 16
HEAD_DIM = 64
FF = 2624
HALF = 512
DOCS = 7

EPS = 1e-05
THETA = 10000.0
MASKED = -1e30

TILE = 256
REACH = HALF // TILE
LANES = 128
FF_PAD = -(-FF // LANES) * LANES
PAIRS = HEADS // 2
WIDE = 4
WIDE_BACK = 2
VMEM = 60 * 1024 * 1024

F32 = jnp.float32
BF16 = jnp.bfloat16

NN = (((1,), (0,)), ((), ()))
NT = (((1,), (1,)), ((), ()))


def dot(left, right, dims=NN):
    return lax.dot_general(left, right, dims, preferred_element_type=F32)


def params(**more):
    return pltpu.CompilerParams(vmem_limit_bytes=VMEM, **more)


def normed(values):
    centre = values - jnp.mean(values, axis=-1, keepdims=True)
    spread = jnp.mean(centre * centre, axis=-1, keepdims=True)
    inverse = lax.rsqrt(spread + EPS)
    return centre * inverse, inverse


def norm_back(grads, unit, inverse):
    first = jnp.mean(grads, axis=-1, keepdims=True)
    second = jnp.mean(grads * unit, axis=-1, keepdims=True)
    return (grads - first - unit * second) * inverse


def swapped(values):
    lane = lax.broadcasted_iota(jnp.int32, values.shape, 1)
    ahead = pltpu.roll(values, LANES - HEAD_DIM // 2, 1)
    behind = pltpu.roll(values, HEAD_DIM // 2, 1)
    return jnp.where(lane % HEAD_DIM < HEAD_DIM // 2, ahead, behind)


def project_kernel(keep, shards, x_ref, w_ref, cos_ref, sin_ref, *outs):
    qkv_ref = outs[-1]
    width = x_ref.shape[2]
    share = width // shards
    gain = jnp.concatenate(
        [w_ref[share * i : share * i + 1, 3 * width : 3 * width + share] for i in range(shards)], axis=1
    ).astype(F32)
    unit, _ = normed(x_ref[0].astype(F32))
    h1 = (unit * gain).astype(BF16)
    if keep:
        outs[0][...] = h1.T
    cosines, sines = cos_ref[0], sin_ref[0]
    for start in range(0, 3 * width, 512):
        part = dot(h1, w_ref[:, start : start + 512])
        for column in range(0, 512, LANES):
            piece = part[:, column : column + LANES]
            if start < 2 * width:
                piece = piece * cosines + swapped(piece) * sines
            if start < width:
                piece = piece * HEAD_DIM**-0.5
            qkv_ref[0, :, start + column : start + column + LANES] = piece.astype(BF16)


def project(x, weight, cosines, sines, first_tile, held, extent, shards):
    batch, rows, width = x.shape
    steps = rows // TILE
    grid = (batch, steps)
    keep = held is None
    block = lambda b, i: (b, i, 0)
    shifted = lambda b, i: (b, i + first_tile, 0)
    qkv_spec = pl.BlockSpec((1, TILE, 3 * width), shifted)
    qkv_shape = jax.ShapeDtypeStruct((batch, extent, 3 * width), BF16)
    in_specs = [
        pl.BlockSpec((1, TILE, width), block),
        pl.BlockSpec(weight.shape, lambda b, i: (0, 0), pipeline_mode=pl.Buffered(1)),
        pl.BlockSpec((1, TILE, LANES), shifted),
        pl.BlockSpec((1, TILE, LANES), shifted),
    ]
    cost = pl.CostEstimate(
        flops=2 * batch * rows * width * 3 * width,
        bytes_accessed=8 * batch * rows * width + 6 * width * width,
        transcendentals=0,
    )
    if keep:
        return pl.pallas_call(
            functools.partial(project_kernel, True, shards),
            grid=grid,
            in_specs=in_specs,
            out_specs=[pl.BlockSpec((width, TILE), lambda b, i: (0, b * steps + i)), qkv_spec],
            out_shape=[jax.ShapeDtypeStruct((width, batch * rows), BF16), qkv_shape],
            compiler_params=params(),
            cost_estimate=cost,
            name="project_own",
        )(x, weight, cosines, sines)

    def halo_kernel(x_ref, w_ref, cos_ref, sin_ref, held_ref, qkv_ref):
        project_kernel(False, shards, x_ref, w_ref, cos_ref, sin_ref, qkv_ref)

    return pl.pallas_call(
        halo_kernel,
        grid=grid,
        in_specs=in_specs + [pl.BlockSpec(memory_space=pl.ANY)],
        out_specs=qkv_spec,
        out_shape=qkv_shape,
        input_output_aliases={4: 0},
        compiler_params=params(),
        cost_estimate=cost,
        name="project_halo",
    )(x, weight, cosines, sines, held)


def edge_masks():
    key = lax.broadcasted_iota(jnp.int32, (TILE, TILE), 0)
    query = lax.broadcasted_iota(jnp.int32, (TILE, TILE), 1)
    return (
        jnp.where(key >= query, 0.0, MASKED).astype(F32),
        jnp.where(key <= query, 0.0, MASKED).astype(F32),
    )


def edge_of(key_tile, query_tile):
    gap = key_tile - query_tile
    return jnp.where(gap == -REACH, 0, jnp.where(gap == REACH, 2, 1))


def low_half(rows):
    return lax.broadcasted_iota(jnp.int32, (rows, LANES), 1) < HEAD_DIM


def split3(values):
    high = values.astype(BF16).astype(F32)
    rest = values - high
    middle = rest.astype(BF16).astype(F32)
    return high, middle, rest - middle


def attend_kernel(tiles, wide, own_ref, lo_ref, hi_ref, q_ref, k_ref, v_ref, ek_ref, eq_ref, o_ref, ot_ref, lse_ref,
                  kx, qx, vx, edges):
    batch = pl.program_id(0)
    stretch, extent = q_ref.shape[1], k_ref.shape[1]

    @pl.when((batch == 0) & (pl.program_id(1) == 0))
    def _():
        before, after = edge_masks()
        edges[0] = before
        edges[1] = jnp.zeros((TILE, TILE), F32)
        edges[2] = after

    low = low_half(extent)
    marks = ek_ref[0]
    ones = jnp.ones((16, extent), BF16)
    for pair in range(wide):
        span = slice(pair * LANES, (pair + 1) * LANES)
        keys = k_ref[0, :, span]
        kx[2 * pair] = jnp.where(low, keys, marks)
        kx[2 * pair + 1] = jnp.where(low, marks, keys)
        turned = q_ref[0, :, span].T
        qx[2 * pair] = jnp.concatenate([turned[:HEAD_DIM], eq_ref[0]], axis=0)
        qx[2 * pair + 1] = jnp.concatenate([eq_ref[0], turned[HEAD_DIM:]], axis=0)
        flipped = v_ref[0, :, span].T
        vx[2 * pair] = jnp.concatenate([flipped[:HEAD_DIM], ones], axis=0)
        vx[2 * pair + 1] = jnp.concatenate([flipped[HEAD_DIM:], ones], axis=0)
    own = own_ref[0]

    def one_tile(index, carry):
        query_tile = own + index
        first, last = lo_ref[batch, query_tile], hi_ref[batch, query_tile]
        columns = pl.ds(pl.multiple_of(index * TILE, TILE), TILE)

        def some(count):
            places, masks = [], []
            for step in range(count):
                key_tile = first + step
                places.append(pl.multiple_of(lax.rem(key_tile - own + tiles, tiles) * TILE, TILE))
                masks.append(edge_of(key_tile, query_tile))

            def score(head):
                return [
                    dot(kx[head, pl.ds(place, TILE), :], qx[head, :, columns]) + edges[mask]
                    for place, mask in zip(places, masks)
                ]

            heads = 2 * wide
            scores = {head: score(head) for head in range(min(1, heads))}
            mixed, waiting = [], []

            def close_head(head, top, powers):
                sums = dot(
                    jnp.concatenate([vx[head, :, pl.ds(place, TILE)] for place in places], axis=1),
                    jnp.concatenate(powers, axis=0),
                )
                total = sums[HEAD_DIM : HEAD_DIM + 1]
                mixed.append(sums[:HEAD_DIM] * (1.0 / total))
                lse_ref[0, head // 2, head % 2 : head % 2 + 1, columns] = top + jnp.log(total)
                if head % 2 == 1:
                    both = jnp.concatenate(mixed[-2:], axis=0)
                    span = slice(head // 2 * LANES, (head // 2 + 1) * LANES)
                    ot_ref[span, columns] = both.astype(BF16)
                    o_ref[0, columns, span] = both.T.astype(BF16)

            for head in range(heads):
                if head + 1 < heads:
                    scores[head + 1] = score(head + 1)
                parts = scores.pop(head)
                top = parts[0]
                for part in parts[1:]:
                    top = jnp.maximum(top, part)
                top = jnp.max(top, axis=0, keepdims=True)
                powers = [jnp.exp(part - top).astype(BF16) for part in parts]
                waiting.append((head, top, powers))
                if len(waiting) > 1:
                    close_head(*waiting.pop(0))
            for item in waiting:
                close_head(*item)

        for count in range(1, 2 * REACH + 2):
            pl.when(last - first == count)(functools.partial(some, count))
        return carry

    lax.fori_loop(0, stretch // TILE, one_tile, 0)


def attend(own, lows, highs, qkv, marks_k, marks_q, stretch):
    batch, extent, _ = qkv.shape
    tiles = extent // TILE
    width = PAIRS * LANES
    wide = WIDE
    groups = PAIRS // wide
    spec = lambda rows, offset: pl.BlockSpec((1, rows, wide * LANES), lambda b, p, *_: (b, 0, p + offset))
    per = pl.BlockSpec((1, extent, LANES), lambda b, p, *_: (b, 0, 0))
    return pl.pallas_call(
        functools.partial(attend_kernel, tiles, wide),
        grid_spec=pltpu.PrefetchScalarGridSpec(
            num_scalar_prefetch=3,
            grid=(batch, groups),
            in_specs=[
                spec(stretch, 0),
                spec(extent, groups),
                spec(extent, 2 * groups),
                per,
                pl.BlockSpec((1, HEAD_DIM, stretch), lambda b, p, *_: (b, 0, 0)),
            ],
            out_specs=[
                spec(stretch, 0),
                pl.BlockSpec((wide * LANES, stretch), lambda b, p, *_: (p, b)),
                pl.BlockSpec((1, wide, 2, stretch), lambda b, p, *_: (b, p, 0, 0)),
            ],
            scratch_shapes=[
                pltpu.VMEM((2 * wide, extent, LANES), BF16),
                pltpu.VMEM((2 * wide, LANES, stretch), BF16),
                pltpu.VMEM((2 * wide, HEAD_DIM + 16, extent), BF16),
                pltpu.VMEM((3, TILE, TILE), F32),
            ],
        ),
        out_shape=[
            jax.ShapeDtypeStruct((batch, stretch, width), BF16),
            jax.ShapeDtypeStruct((width, batch * stretch), BF16),
            jax.ShapeDtypeStruct((batch, PAIRS, 2, stretch), F32),
        ],
        compiler_params=params(),
        cost_estimate=pl.CostEstimate(
            flops=2 * 2 * HEADS * batch * stretch * extent * 128, bytes_accessed=32 * 1024 * 1024, transcendentals=0
        ),
        name="attend",
    )(own, lows, highs, qkv, qkv, qkv, marks_k, marks_q)


def attend_back_kernel(tiles, wide, own_ref, lo_ref, hi_ref, q_ref, k_ref, v_ref, do_ref, doh_ref, st_ref, sth_ref,
                       ek_ref, eq_ref, cos_ref, sin_ref, out_ref,
                       kx, vx, qx, dx, dn, kt, dqt, edges):
    batch = pl.program_id(0)
    extent = k_ref.shape[1]
    stretch = do_ref.shape[1]
    mine = stretch // TILE
    heads = 2 * wide

    @pl.when((batch == 0) & (pl.program_id(1) == 0))
    def _():
        before, after = edge_masks()
        edges[0] = before
        edges[1] = jnp.zeros((TILE, TILE), F32)
        edges[2] = after

    low = low_half(extent)
    marks = ek_ref[0]
    lane = lax.broadcasted_iota(jnp.int32, (extent, LANES), 1) % HEAD_DIM
    units = jnp.where((lane >= 8) & (lane < 11), 1.0, 0.0).astype(BF16)
    row = lax.broadcasted_iota(jnp.int32, (HEAD_DIM, extent), 0)
    label_rows = eq_ref[0].astype(F32)
    dn[:stretch] = do_ref[0]
    dn[stretch:] = doh_ref[0]
    for pair in range(wide):
        span = slice(pair * LANES, (pair + 1) * LANES)
        keys, values = k_ref[0, :, span], v_ref[0, :, span]
        kx[2 * pair] = jnp.where(low, keys, marks)
        kx[2 * pair + 1] = jnp.where(low, marks, keys)
        kt[span] = keys.T
        vx[2 * pair] = jnp.where(low, values, units)
        vx[2 * pair + 1] = jnp.where(low, units, values)
        turned, flipped = q_ref[0, :, span].T, dn[:, span].T
        stats = jnp.concatenate([st_ref[0, pair], sth_ref[0, pair]], axis=1)
        for half in range(2):
            lse = split3(stats[half : half + 1])
            delta = split3(stats[half + 2 : half + 3])
            mark, shift = label_rows, jnp.zeros((HEAD_DIM, extent), F32)
            for place in range(3):
                mark = jnp.where(row == 8 + place, -lse[place], mark)
                shift = jnp.where(row == 8 + place, -delta[place], shift)
            mark, shift = mark.astype(BF16), shift.astype(BF16)
            rows = slice(half * HEAD_DIM, (half + 1) * HEAD_DIM)
            order = (lambda a, b: [a, b]) if half == 0 else (lambda a, b: [b, a])
            qx[2 * pair + half] = jnp.concatenate(order(turned[rows], mark), axis=0)
            dx[2 * pair + half] = jnp.concatenate(order(flipped[rows], shift), axis=0)

    own = own_ref[0]
    dqt[...] = jnp.zeros_like(dqt)
    low_tile = low_half(TILE)

    def place(tile):
        return pl.ds(pl.multiple_of(lax.rem(tile - own + tiles, tiles) * TILE, TILE), TILE)

    def some(key_tile, begin, count, key_grad, out_rows):
        rows = place(key_tile)
        columns = [place(begin + step) for step in range(count)]
        masks = [edge_of(key_tile, begin + step) for step in range(count)]
        items = [(head, step) for head in range(heads) for step in range(count)]
        powers, slopes, sums = {}, {}, {}

        def first_products(head, step):
            score = dot(kx[head, rows, :], qx[head, :, columns[step]]) + edges[masks[step]]
            return score, dot(vx[head, rows, :], dx[head, :, columns[step]])

        def last_products(head, step):
            span = slice(head * HEAD_DIM, (head + 1) * HEAD_DIM)
            dqt[span, columns[step]] += dot(kt[span, rows], slopes[head][step])
            if not key_grad or step + 1 < count:
                return
            pair = slice(head // 2 * LANES, (head // 2 + 1) * LANES)
            grads = jnp.concatenate([dn[column, pair] for column in columns], axis=0)
            queries = jnp.concatenate([q_ref[0, column, pair] for column in columns], axis=0)
            sums[head] = (
                dot(jnp.concatenate(slopes.pop(head), axis=1), queries),
                dot(jnp.concatenate(powers.pop(head), axis=1), grads),
            )
            if head % 2 == 1:
                key_sum, value_sum = (jnp.where(low_tile, a, b) for a, b in zip(sums[head - 1], sums[head]))
                cosines, sines = cos_ref[0, out_rows, :], sin_ref[0, out_rows, :]
                out_ref[1, 0, out_rows, pair] = (key_sum * cosines - swapped(key_sum) * sines).astype(BF16)
                out_ref[2, 0, out_rows, pair] = value_sum.astype(BF16)

        ahead = [first_products(*items[0])]
        for index, (head, step) in enumerate(items):
            if index + 1 < len(items):
                ahead.append(first_products(*items[index + 1]))
            score, slope = ahead.pop(0)
            power = jnp.exp(score)
            powers.setdefault(head, []).append(power.astype(BF16))
            slopes.setdefault(head, []).append((power * slope).astype(BF16))
            if index >= 1:
                last_products(*items[index - 1])
        last_products(*items[-1])

    def own_keys(index, carry):
        key_tile = own + index
        first, last = lo_ref[batch, key_tile], hi_ref[batch, key_tile]
        out_rows = pl.ds(pl.multiple_of(index * TILE, TILE), TILE)
        for count in range(1, 2 * REACH + 2):
            pl.when(last - first == count)(functools.partial(some, key_tile, first, count, True, out_rows))
        return carry

    lax.fori_loop(0, mine, own_keys, 0)

    def other_keys(mem, carry):
        ahead = own + mem
        key_tile = jnp.where(ahead < own + mine + REACH, ahead, ahead - tiles)
        if tiles == mine + REACH:
            key_tile = jnp.where(own == 0, ahead, ahead - tiles)
        valid = (key_tile >= 0) & (key_tile < lo_ref.shape[1])
        safe = jnp.where(valid, key_tile, 0)
        begin = jnp.maximum(lo_ref[batch, safe], own)
        end = jnp.where(valid, jnp.minimum(hi_ref[batch, safe], own + mine), begin)
        for count in range(1, min(REACH, mine) + 1):
            pl.when(end - begin == count)(functools.partial(some, safe, begin, count, False, None))
        return carry

    lax.fori_loop(mine, tiles, other_keys, 0)
    for pair in range(wide):
        span = slice(pair * LANES, (pair + 1) * LANES)
        raw = dqt[span, :stretch].T * HEAD_DIM**-0.5
        out_ref[0, 0, :, span] = (raw * cos_ref[0] - swapped(raw) * sin_ref[0]).astype(BF16)


def attend_back(own, lows, highs, qkv, grads, grads_halo, stats, stats_halo, marks_k, marks_q, cosines, sines):
    batch, extent, _ = qkv.shape
    stretch, width = grads.shape[1:]
    halo = extent - stretch
    tiles = extent // TILE
    wide = WIDE_BACK
    groups = PAIRS // wide
    spec = lambda rows, offset: pl.BlockSpec((1, rows, wide * LANES), lambda b, p, *_: (b, 0, p + offset))
    per = lambda rows: pl.BlockSpec((1, rows, LANES), lambda b, p, *_: (b, 0, 0))
    numbers = lambda rows: pl.BlockSpec((1, wide, 4, rows), lambda b, p, *_: (b, p, 0, 0))
    return pl.pallas_call(
        functools.partial(attend_back_kernel, tiles, wide),
        grid_spec=pltpu.PrefetchScalarGridSpec(
            num_scalar_prefetch=3,
            grid=(batch, groups),
            in_specs=[
                spec(extent, 0),
                spec(extent, groups),
                spec(extent, 2 * groups),
                spec(stretch, 0),
                spec(halo, 0),
                numbers(stretch),
                numbers(halo),
                per(extent),
                pl.BlockSpec((1, HEAD_DIM, extent), lambda b, p, *_: (b, 0, 0)),
                per(stretch),
                per(stretch),
            ],
            out_specs=pl.BlockSpec((3, 1, stretch, wide * LANES), lambda b, p, *_: (0, b, 0, p)),
            scratch_shapes=[
                pltpu.VMEM((2 * wide, extent, LANES), BF16),
                pltpu.VMEM((2 * wide, extent, LANES), BF16),
                pltpu.VMEM((2 * wide, LANES, extent), BF16),
                pltpu.VMEM((2 * wide, LANES, extent), BF16),
                pltpu.VMEM((extent, wide * LANES), BF16),
                pltpu.VMEM((wide * LANES, extent), BF16),
                pltpu.VMEM((wide * LANES, extent), F32),
                pltpu.VMEM((3, TILE, TILE), F32),
            ],
        ),
        out_shape=jax.ShapeDtypeStruct((3, batch, stretch, width), BF16),
        compiler_params=params(),
        cost_estimate=pl.CostEstimate(
            flops=5 * 2 * HEADS * batch * stretch * extent * 128, bytes_accessed=64 * 1024 * 1024, transcendentals=0
        ),
        name="attend_back",
    )(own, lows, highs, qkv, qkv, qkv, grads, grads_halo, stats, stats_halo, marks_k, marks_q, cosines, sines)


def feed_kernel(x_ref, o_ref, g_ref, gain_ref, w_ref, wd_ref,
                out_ref, h2t_ref, hidt_ref, slopes_ref, dr_ref, do_ref, delta_ref):
    mixed = o_ref[0]
    seeds = g_ref[0]
    gain = gain_ref[...]
    width = mixed.shape[1]
    w_out = slice(2 * FF_PAD, 2 * FF_PAD + width)
    r1 = x_ref[0].astype(F32) + dot(mixed, w_ref[:, w_out])
    unit, inverse = normed(r1)
    h2 = (unit * gain).astype(BF16)
    h2t_ref[...] = h2.T
    total = r1
    back = jnp.zeros_like(r1)
    edges = list(range(0, FF - 511, 512))
    for start, stop in zip(edges, edges[1:] + [FF]):
        gates, ups = slice(start, stop), slice(FF_PAD + start, FF_PAD + stop)
        gate = dot(h2, w_ref[:, gates])
        up = dot(h2, w_ref[:, ups])
        grad = dot(seeds, wd_ref[start:stop, :], NT)
        phi = 0.5 + 0.5 * lax.erf(gate * (0.5**0.5))
        bell = jnp.exp(gate * gate * -0.5) * 0.3989422804014327
        act = gate * phi
        hid = (act * up).astype(BF16)
        grad_gate = (grad * up * (phi + gate * bell)).astype(BF16)
        grad_up = (grad * act).astype(BF16)
        hidt_ref[start:stop, :] = hid.T
        slopes_ref[0, :, gates] = grad_gate
        slopes_ref[0, :, ups] = grad_up
        total = total + dot(hid, wd_ref[start:stop, :])
        back = back + dot(grad_gate, w_ref[:, gates], NT) + dot(grad_up, w_ref[:, ups], NT)
    blank = jnp.zeros((TILE, FF_PAD - FF), BF16)
    slopes_ref[0, :, FF:FF_PAD] = blank
    slopes_ref[0, :, FF_PAD + FF : 2 * FF_PAD] = blank
    out_ref[0] = total.astype(BF16)
    dr = seeds.astype(F32) + norm_back(back * gain, unit, inverse)
    dr_ref[0] = dr
    da = dr.astype(BF16)
    slopes_ref[0, :, w_out] = da
    do = dot(da, w_ref[:, w_out], NT).astype(BF16)
    do_ref[0] = do
    product = do.astype(F32) * mixed.astype(F32)
    high = product.astype(BF16)
    rest = (product - high.astype(F32)).astype(BF16)
    head = lax.broadcasted_iota(jnp.int32, (HEADS, width), 0)
    column = lax.broadcasted_iota(jnp.int32, (HEADS, width), 1)
    pick = jnp.where(column // HEAD_DIM == head, 1.0, 0.0).astype(BF16)
    delta = dot(pick, high, NT) + dot(pick, rest, NT)
    for pair in range(PAIRS):
        delta_ref[0, pair] = delta[2 * pair : 2 * pair + 2]


def feed(x, mixed, seeds, gain, w_rest, w_down):
    batch, rows, width = x.shape
    steps = rows // TILE
    block = lambda n: pl.BlockSpec((1, TILE, n), lambda b, i: (b, i, 0))
    turned = lambda n: pl.BlockSpec((n, TILE), lambda b, i: (0, b * steps + i))
    fixed = lambda m, n: pl.BlockSpec((m, n), lambda b, i: (0, 0), pipeline_mode=pl.Buffered(1))
    shape = lambda n, t: jax.ShapeDtypeStruct((batch, rows, n), t)
    columns = w_rest.shape[1]
    return pl.pallas_call(
        feed_kernel,
        grid=(batch, steps),
        in_specs=[
            block(width), block(width), block(width), fixed(1, width), fixed(width, columns), fixed(FF, width),
        ],
        out_specs=[
            block(width), turned(width), turned(FF), block(columns), block(width), block(width),
            pl.BlockSpec((1, PAIRS, 2, TILE), lambda b, i: (b, 0, 0, i)),
        ],
        out_shape=[
            shape(width, BF16),
            jax.ShapeDtypeStruct((width, batch * rows), BF16),
            jax.ShapeDtypeStruct((FF, batch * rows), BF16),
            shape(columns, BF16),
            shape(width, F32),
            shape(width, BF16),
            jax.ShapeDtypeStruct((batch, PAIRS, 2, rows), F32),
        ],
        compiler_params=params(),
        cost_estimate=pl.CostEstimate(
            flops=2 * batch * rows * width * (6 * FF + 2 * width), bytes_accessed=64 * 1024 * 1024, transcendentals=0
        ),
        name="feed",
    )(x, mixed, seeds, gain, w_rest, w_down)


def weigh_kernel(left_ref, right_ref, *outs):
    outs[-1][...] = dot(left_ref[...], right_ref[...].reshape(right_ref.shape[-2:])).astype(BF16)


def weigh(left, right, name, left_block, right_block, out_block, left_map, right_map, out_map, steps, shape, held=None):
    specs = [pl.BlockSpec(left_block, left_map), pl.BlockSpec(right_block, right_map)]
    arrays = [left, right]
    if held is not None:
        specs.append(pl.BlockSpec(memory_space=pl.ANY))
        arrays.append(held)
    rows, columns = out_block
    return pl.pallas_call(
        weigh_kernel,
        grid=(steps,),
        in_specs=specs,
        out_specs=pl.BlockSpec(out_block, out_map),
        out_shape=jax.ShapeDtypeStruct(shape, BF16),
        input_output_aliases={} if held is None else {2: 0},
        compiler_params=params(),
        cost_estimate=pl.CostEstimate(
            flops=2 * steps * rows * columns * left.shape[1], bytes_accessed=16 * 1024 * 1024, transcendentals=0
        ),
        name=name,
    )(*arrays)


MESH = pl.DeviceIdType.MESH
CUT = 512
LAGS = (1, 3, 5, 6, 7, 8)


def close_kernel(blocks, seqs, reps, h1t_ref, right_ref, three_ref, w_ref, x_ref, dr_ref, gain_ref, gi_ref, sum_ref,
                 prod, kept0, kept1x, kept1y, kept2, s0, r0, s1x, r1x, s1y, r1y, s2x, r2x, s2y, r2y,
                 mine, ends, half, others, whole, send_sem, recv_sem):
    step = pl.program_id(0)
    width = h1t_ref.shape[0]
    share = mine.shape[1]
    seq, dp, rep = lax.axis_index("seq"), lax.axis_index("dp"), lax.axis_index("rep")
    core, side = lax.rem(dp, 2), dp // 2
    mate, across = dp + 1 - 2 * core, lax.rem(dp + 2, 4)
    seq_peers = [lax.rem(seq + hop, seqs) for hop in range(1, seqs)]
    inner = (rep == 1) | (rep == 2)
    beside = rep + 1 - 2 * lax.rem(rep, 2)
    slot_seq, slot_side, slot_in = 1, seqs, seqs + 1

    def copy(source, target, n, slot, device):
        return pltpu.make_async_remote_copy(
            src_ref=source, dst_ref=target, send_sem=send_sem.at[n, slot], recv_sem=recv_sem.at[n, slot],
            device_id=device, device_id_type=MESH,
        )

    def rows(first, count):
        return pl.ds(pl.multiple_of(first * share, share), count * share)

    def to_mate(n):
        return [copy(s0.at[n], r0.at[n], n, 0, {"dp": mate})]

    def to_seq(n, source, target):
        return [
            copy(source.at[n // 2, hop], target.at[n // 2, hop], n, slot_seq + hop, {"seq": peer})
            for hop, peer in enumerate(seq_peers)
        ]

    def to_side(n, source, target):
        return [copy(source.at[n // 2], target.at[n // 2], n, slot_side, {"dp": across})]

    def inwards(n):
        return copy(mine.at[n], ends.at[n], n, slot_in, {"rep": beside})

    def between(n):
        return copy(half.at[n], others.at[n], n, slot_in + 1, {"rep": reps - 1 - rep})

    def outwards(n):
        return copy(whole.at[n], whole.at[n], n, slot_in + 2, {"rep": beside})

    def start(copies):
        for each in copies:
            each.start()

    def wait(copies):
        for each in copies:
            each.wait()

    @pl.when(step == 0)
    def _():
        barrier = pltpu.get_barrier_semaphore()
        partners = [{"dp": mate}, {"dp": across}]
        partners += [{"seq": peer} for peer in seq_peers] + [{"rep": beside}]
        for partner in partners:
            pl.semaphore_signal(barrier, inc=1, device_id=partner, device_id_type=MESH)

        @pl.when(inner)
        def _():
            pl.semaphore_signal(barrier, inc=1, device_id={"rep": reps - 1 - rep}, device_id_type=MESH)
            pl.semaphore_wait(barrier, len(partners) + 1)

        @pl.when(jnp.logical_not(inner))
        def _():
            pl.semaphore_wait(barrier, len(partners))

    @pl.when(step < blocks)
    def _():
        prod[...] = dot(h1t_ref[...], right_ref[0])
        for place in range(2 * seqs):
            span = slice(place * share, (place + 1) * share)
            s0[step, span, :] = prod[rows(2 * place + 1 - core, 1), :].astype(BF16)
        start(to_mate(step))
        for place in range(2 * seqs):
            span = slice(place * share, (place + 1) * share)
            kept0[step % 2, span, :] = prod[rows(2 * place + core, 1), :]

    @pl.when((step >= blocks) & (step < blocks + gi_steps(three_ref, right_ref)))
    def _():
        back = None
        for part in range(3):
            term = dot(three_ref[part], w_ref[:, part * width : (part + 1) * width], NT)
            back = term if back is None else back + term
        unit, inverse = normed(x_ref[...].astype(F32))
        gi_ref[...] = dr_ref[...] + norm_back(back * gain_ref[...], unit, inverse)

    n6 = step - LAGS[5]

    @pl.when((n6 >= 0) & (n6 < blocks))
    def _():
        @pl.when(inner)
        def _():
            outwards(n6).wait_send()

        @pl.when(jnp.logical_not(inner))
        def _():
            outwards(n6).wait_recv()

        sum_ref[:, pl.ds(pl.multiple_of(n6 * CUT, CUT), CUT)] = whole[n6].astype(F32)

    n5 = step - LAGS[4]

    @pl.when((n5 >= 0) & (n5 < blocks) & inner)
    def _():
        between(n5).wait()
        whole[n5] = (half[n5].astype(F32) + others[n5].astype(F32)).astype(BF16)
        outwards(n5).start()

    n4 = step - LAGS[3]

    @pl.when((n4 >= 0) & (n4 < blocks) & inner)
    def _():
        inwards(n4).wait_recv()
        half[n4] = (mine[n4].astype(F32) + ends[n4].astype(F32)).astype(BF16)
        between(n4).start()

    @pl.when((n4 >= 0) & (n4 < blocks) & jnp.logical_not(inner))
    def _():
        inwards(n4).wait_send()

    n3 = step - LAGS[2]

    @pl.when((n3 >= 0) & (n3 < blocks))
    def _():
        total = kept2[n3 % 2]

        @pl.when(n3 % 2 == 0)
        def _():
            wait(to_side(n3, s2y, r2y))
            mine[n3] = (total + r2y[n3 // 2].astype(F32)).astype(BF16)

        @pl.when(n3 % 2 == 1)
        def _():
            wait(to_seq(n3, s2x, r2x))
            added = total
            for hop in range(seqs - 1):
                added = added + r2x[n3 // 2, hop].astype(F32)
            mine[n3] = added.astype(BF16)

        @pl.when(jnp.logical_not(inner))
        def _():
            inwards(n3).start()

    n2 = step - LAGS[1]

    @pl.when((n2 >= 0) & (n2 < blocks) & (n2 % 2 == 0))
    def _():
        wait(to_seq(n2, s1x, r1x))
        total = kept1x[...]
        for hop in range(seqs - 1):
            total = total + r1x[n2 // 2, hop].astype(F32)
        kept1x[...] = total
        s2y[n2 // 2] = kept1x[rows(1 - side, 1), :].astype(BF16)
        start(to_side(n2, s2y, r2y))
        kept2[0] = kept1x[rows(side, 1), :]

    @pl.when((n2 >= 0) & (n2 < blocks) & (n2 % 2 == 1))
    def _():
        wait(to_side(n2, s1y, r1y))
        kept1y[...] = kept1y[...] + r1y[n2 // 2].astype(F32)
        for hop, peer in enumerate(seq_peers):
            s2x[n2 // 2, hop] = kept1y[rows(peer, 1), :].astype(BF16)
        start(to_seq(n2, s2x, r2x))
        kept2[1] = kept1y[rows(seq, 1), :]

    n1 = step - LAGS[0]

    @pl.when((n1 >= 0) & (n1 < blocks))
    def _():
        wait(to_mate(n1))
        held = n1 % 2
        kept0[held] = kept0[held] + r0[n1].astype(F32)

        @pl.when(n1 % 2 == 0)
        def _():
            for hop, peer in enumerate(seq_peers):
                s1x[n1 // 2, hop] = kept0[held, rows(2 * peer, 2), :].astype(BF16)
            start(to_seq(n1, s1x, r1x))
            kept1x[...] = kept0[held, rows(2 * seq, 2), :]

        @pl.when(n1 % 2 == 1)
        def _():
            for place in range(seqs):
                s1y[n1 // 2, place * share : (place + 1) * share, :] = kept0[held, rows(2 * place + 1 - side, 1), :].astype(BF16)
            start(to_side(n1, s1y, r1y))
            for place in range(seqs):
                kept1y[place * share : (place + 1) * share, :] = kept0[held, rows(2 * place + side, 1), :]


def gi_steps(three_ref, right_ref):
    return right_ref.shape[1] // three_ref.shape[1]


def close(h1t, slopes, weight, x, dr, gain, seqs, dps, reps):
    assert (dps, reps) == (4, 4)
    width, tokens = h1t.shape
    share = width // (seqs * dps)
    blocks = 3 * width // CUT
    halves = width // CUT
    token_blocks = tokens // TILE
    steps = max(blocks + token_blocks, blocks + LAGS[5])
    late = lambda s: jnp.clip(s - blocks, 0, token_blocks - 1)
    early = lambda s: jnp.minimum(s, blocks - 1)
    fixed = lambda m, n: pl.BlockSpec((m, n), lambda s: (0, 0), pipeline_mode=pl.Buffered(1))
    row = pl.BlockSpec((TILE, width), lambda s: (late(s), 0))
    pairs = (blocks + 1) // 2
    half_rows = 2 * seqs * share
    buffers = lambda *shape: [pltpu.VMEM(shape + (CUT,), BF16)] * 2
    slots = seqs + 4
    return pl.pallas_call(
        functools.partial(close_kernel, blocks, seqs, reps),
        grid=(steps,),
        in_specs=[
            fixed(width, tokens),
            pl.BlockSpec((1, tokens, CUT), lambda s: (early(s) // halves, 0, early(s) % halves)),
            pl.BlockSpec((3, TILE, width), lambda s: (0, late(s), 0)),
            fixed(*weight.shape),
            row,
            row,
            fixed(1, width),
        ],
        out_specs=[row, fixed(share, 3 * width)],
        out_shape=[
            jax.ShapeDtypeStruct((tokens, width), F32),
            jax.ShapeDtypeStruct((share, 3 * width), F32),
        ],
        scratch_shapes=[
            pltpu.VMEM((width, CUT), F32),
            pltpu.VMEM((2, half_rows, CUT), F32),
            pltpu.VMEM((2 * share, CUT), F32),
            pltpu.VMEM((seqs * share, CUT), F32),
            pltpu.VMEM((2, share, CUT), F32),
            *buffers(blocks, half_rows),
            *buffers(pairs, seqs - 1, 2 * share),
            *buffers(pairs, seqs * share),
            *buffers(pairs, seqs - 1, share),
            *buffers(pairs, share),
            *[pltpu.VMEM((blocks, share, CUT), BF16)] * 5,
            pltpu.SemaphoreType.DMA((blocks, slots)),
            pltpu.SemaphoreType.DMA((blocks, slots)),
        ],
        compiler_params=params(collective_id=1, has_side_effects=True),
        cost_estimate=pl.CostEstimate(
            flops=4 * tokens * width * 3 * width, bytes_accessed=48 * 1024 * 1024, transcendentals=0
        ),
        name="close",
    )(h1t, slopes, slopes, weight, x, dr, gain)


def neighbours(block, axis, along):
    count = lax.axis_size(axis)
    rows = block.shape[along]
    if count == 2:
        start = (1 - lax.axis_index(axis)) * (rows - HALF)
        facing = lax.dynamic_slice_in_dim(block, start, HALF, along)
        return lax.ppermute(facing, axis, [(0, 1), (1, 0)])
    step = min(rows, HALF)
    head = lax.slice_in_dim(block, 0, step, axis=along)
    tail = lax.slice_in_dim(block, rows - step, rows, axis=along)
    hops = range(1, HALF // step + 1)
    after = [lax.ppermute(head, axis, [(i + hop, i) for i in range(count - hop)]) for hop in hops]
    before = [lax.ppermute(tail, axis, [(i, i + hop) for i in range(count - hop)]) for hop in reversed(hops)]
    return jnp.concatenate(after + before, axis=along)


def survey(labels, stretch, extent, seq_index, seq_count):
    length = labels.shape[1]
    mem = jnp.arange(extent, dtype=jnp.int32)
    own_start = seq_index * stretch
    wraps = stretch + HALF if seq_count > 2 else jnp.where(seq_index == 0, extent, stretch)
    places = own_start + mem - jnp.where(mem >= wraps, extent, 0)
    padded = jnp.pad(labels, ((0, 0), (HALF, HALF)))
    cut = lambda first, size: lax.dynamic_slice_in_dim(padded, first + HALF, size, 1)
    parts = [cut(own_start, stretch)]
    if seq_count == 2:
        parts.append(cut(jnp.where(seq_index == 0, own_start + stretch, own_start - HALF), HALF))
    else:
        parts += [cut(own_start + stretch, HALF), cut(own_start - HALF, HALF)]
    near = jnp.concatenate(parts, axis=1)
    docs = jnp.arange(DOCS, dtype=jnp.int32)
    starts = jnp.sum(labels[:, :, None] < docs, axis=1, dtype=jnp.int32)
    stops = jnp.sum(labels[:, :, None] <= docs, axis=1, dtype=jnp.int32) - 1
    same = near[:, :, None] == docs
    positions = places - jnp.sum(jnp.where(same, starts[:, None, :], 0), axis=-1)
    lane = jnp.arange(LANES, dtype=jnp.int32)
    half_dim = HEAD_DIM // 2
    frequency = THETA ** (-((lane % half_dim).astype(F32) * 2.0 / HEAD_DIM))
    angles = positions.astype(F32)[:, :, None] * frequency
    cosines = jnp.cos(angles)
    sines = jnp.sin(angles) * jnp.where(lane % HEAD_DIM < half_dim, -1.0, 1.0)
    slot = lane % HEAD_DIM
    marks_k = jnp.where(
        slot < DOCS,
        jnp.where(near[:, :, None] == slot, 0.0, MASKED),
        jnp.where((slot >= 8) & (slot < 11), 1.0, 0.0),
    ).astype(BF16)
    kind = jnp.arange(HEAD_DIM, dtype=jnp.int32)[None, :, None]
    marks_q = jnp.where((kind < DOCS) & (near[:, None, :] == kind), 1.0, 0.0).astype(BF16)
    at = jnp.arange(length // TILE, dtype=jnp.int32) * TILE
    first_label, last_label = labels[:, ::TILE], labels[:, TILE - 1 :: TILE]
    pick = lambda table, which: jnp.sum(
        jnp.where(which[:, :, None] == docs, table[:, None, :], 0), axis=-1
    )
    lows = jnp.maximum(pick(starts, first_label), at - HALF) // TILE
    highs = jnp.minimum(pick(stops, last_label), at + TILE - 1 + HALF) // TILE + 1
    own = (own_start // TILE).astype(jnp.int32).reshape(1)
    return own, lows, highs, cosines, sines, marks_k, marks_q


def body(inputs, segments, cotangent, attn_gain, mlp_gain, w_qkv, w_out, w_in, w_down):
    stretch, width = inputs.shape[2:]
    length = segments.shape[2]
    x = inputs.reshape(-1, stretch, width)
    seeds = cotangent.reshape(-1, stretch, width)
    labels = segments.reshape(-1, length)
    batch = x.shape[0]
    group = ("seq", "dp")
    seq_index = lax.axis_index("seq")
    seq_count = lax.axis_size("seq")

    share = attn_gain.shape[0]
    shards = width // share
    x_halo = neighbours(x, "seq", 1)
    gather = lambda shard: lax.all_gather(shard, group, axis=0, tiled=True)
    gain_rows = jnp.pad(jnp.stack([attn_gain, mlp_gain]), ((0, share - 2), (0, LANES - share)))
    qkv_full = gather(jnp.concatenate([w_qkv, gain_rows], axis=1))
    blank = jnp.zeros((share, FF_PAD - FF), BF16)
    rest_full = gather(jnp.concatenate([w_in[:, :FF], blank, w_in[:, FF:], blank, w_out], axis=1))
    down_full = gather(w_down)
    gains = qkv_full[:, 3 * width : 3 * width + share].reshape(shards, share, share).astype(F32)
    gain_one, gain_two = gains[:, 0].reshape(1, width), gains[:, 1].reshape(1, width)

    halo = x_halo.shape[1]
    extent = stretch + halo
    own, lows, highs, cosines, sines, marks_k, marks_q = survey(labels, stretch, extent, seq_index, seq_count)

    h1t, qkv = project(x, qkv_full, cosines, sines, 0, None, extent, shards)
    qkv = project(x_halo, qkv_full, cosines, sines, stretch // TILE, qkv, extent, shards)
    mixed, mixed_t, lse = attend(own, lows, highs, qkv, marks_k, marks_q, stretch)
    result, h2t, hidt, slopes, dr, do, delta = feed(x, mixed, seeds, gain_two, rest_full, down_full)
    stats = jnp.concatenate([lse, delta], axis=2)
    do_halo = neighbours(do, "seq", 1)
    stats_halo = neighbours(stats, "seq", 3)

    scatter = lambda part: lax.psum_scatter(part, group, scatter_dimension=0, tiled=True)
    tokens = batch * stretch
    columns = rest_full.shape[1]
    flat = slopes.reshape(tokens, columns)
    step = FF_PAD * 2 // 7
    part_rest = weigh(
        h2t, flat, "weigh_in", (width, tokens), (tokens, step), (width, step),
        lambda n: (0, 0), lambda n: (0, n), lambda n: (0, n), 7, (width, columns),
    )
    first = FF_PAD * 2 // TILE
    part_rest = weigh(
        mixed_t, flat, "weigh_out", (width, tokens), (tokens, TILE), (width, TILE),
        lambda n: (0, 0), lambda n: (0, n + first), lambda n: (0, n + first), width // TILE, (width, columns), part_rest,
    )
    shard_rest = scatter(part_rest)
    do_halo, stats_halo, hidt = lax.optimization_barrier((do_halo, stats_halo, hidt))
    step = FF // 4
    part_down = weigh(
        hidt, seeds.reshape(tokens, width), "weigh_down", (step, tokens), (tokens, width), (step, width),
        lambda n: (n, 0), lambda n: (0, 0), lambda n: (n, 0), 4, (FF, width),
    )
    shard_down = scatter(part_down)
    do_halo, stats_halo, part_down, part_rest = lax.optimization_barrier((do_halo, stats_halo, part_down, part_rest))
    rest_sum, down_sum = lax.psum((shard_rest, shard_down), "rep")
    slopes_qkv = attend_back(
        own, lows, highs, qkv, do, do_halo, stats, stats_halo, marks_k, marks_q, cosines, sines
    )
    grad_x, grad_qkv = close(
        h1t, slopes_qkv.reshape(3, tokens, width), qkv_full, x.reshape(tokens, width), dr.reshape(tokens, width),
        gain_one, seq_count, lax.axis_size("dp"), lax.axis_size("rep"),
    )
    rest_sum = rest_sum.astype(F32)
    grad_in = jnp.concatenate([rest_sum[:, :FF], rest_sum[:, FF_PAD : FF_PAD + FF]], axis=1)
    grad_attn_gain = jnp.sum(grad_qkv * w_qkv.astype(F32), axis=1) / attn_gain.astype(F32)
    grad_mlp_gain = jnp.sum(grad_in * w_in.astype(F32), axis=1) / mlp_gain.astype(F32)
    return (
        result.reshape(cotangent.shape),
        grad_x.reshape(inputs.shape),
        grad_attn_gain,
        grad_mlp_gain,
        grad_qkv,
        rest_sum[:, 2 * FF_PAD :],
        grad_in,
        down_sum.astype(F32),
    )


def solution(mesh):
    return jax.shard_map(
        body,
        mesh=mesh,
        in_specs=(
            P(None, ("dp", "rep"), "seq", None),
            P(None, ("dp", "rep"), None),
            P(None, ("dp", "rep"), "seq", None),
            P(("seq", "dp")),
            P(("seq", "dp")),
            P(("seq", "dp"), None),
            P(("seq", "dp"), None),
            P(("seq", "dp"), None),
            P(("seq", "dp"), None),
        ),
        out_specs=(
            P(None, ("dp", "rep"), "seq", None),
            P(None, ("dp", "rep"), "seq", None),
            P(("seq", "dp")),
            P(("seq", "dp")),
            P(("seq", "dp"), None),
            P(("seq", "dp"), None),
            P(("seq", "dp"), None),
            P(("seq", "dp"), None),
        ),
        check_vma=False,
    )
```

time: 2270 us -> 673 us (0.30)
  matrix products: 923 us -> 0 us
  other arithmetic: 490 us -> 20.4 us
  Pallas kernels: 0 us -> 442 us
  local copies, waits for them, and re-layouts: 419 us -> 18.9 us
  waiting for transfers between devices: 289 us -> 167 us
  starting transfers between devices: 61.5 us -> 5.34 us
  blocking collectives: 44.2 us -> 0 us
    dot_general x52 -> x0, matrix products: 923 us -> none  [the longest x8 165 us: block_inputs(): jnp.einsum('qhd,khd->hqk', query_rows, key_rows, preferred_element_type=j...]
    pallas_call x0 -> x9, Pallas kernels: none -> 442 us  [the longest x1 109 us: attend_back(): pl.pallas_call(functools.partial(attend_back_kernel, tiles, wide), grid_s...]
    dynamic_update_slice x16 -> x0, local copies, waits for them, and re-layouts: 172 us -> none  [body(): mixed_blocks, log_totals = lax.map(forward_block, block_numbers)]
    convert_element_type x17 -> x5, other arithmetic: 175 us -> 3.52 us  [the longest x1 1.31 us: survey(): marks_k = jnp.where(slot < DOCS, jnp.where(near[:, :, None] == slot, 0.0,...]
    ppermute x16 -> x3, waiting for transfers between devices: 172 us -> 48.4 us  [neighbours(): return lax.ppermute(facing, axis, [(0, 1), (1, 0)])]
    reduce_sum x12 -> x6, other arithmetic: 106 us -> 4.32 us  [the longest x1 2.05 us: body(): jnp.sum(grad_in * w_in.astype(F32), axis=1) / mlp_gain.astype(F32)]
    another operation x21 -> x1, other arithmetic: 96.5 us -> 0.78 us  [body(): jnp.stack([attn_gain, mlp_gain])]
    all_gather x4 -> x3, waiting for transfers between devices: 0.03 us -> 88 us  [body(): gather = lambda shard: lax.all_gather(shard, group, axis=0, tiled=True)]
  transfers between devices with their start and end apart: 25 -> 9, of which waited for: 7 -> 5; matrix products, arithmetic and copies ran while one was open for 72% -> 3% of each run, Pallas kernels for 0% -> 48%
where the time goes in v1:
time: 673 us; the launch traced here: 668 us
  Pallas kernels  442 us (66%)
  waiting for transfers between devices  167 us (25%)
  other arithmetic  20.4 us (3%)
  local copies, waits for them, and re-layouts  18.9 us (3%)
  between operations  14.6 us (2%)
    pallas_call x1, Pallas kernels, attend_back(): pl.pallas_call(functools.partial(attend_back_kernel, tiles, wide), grid_s...  109 us
    pallas_call x1, Pallas kernels, feed(): pl.pallas_call(feed_kernel, grid=(batch, steps), in_specs=[block(width),...  105 us
    all_gather x3, waiting for transfers between devices, body(): gather = lambda shard: lax.all_gather(shard, group, axis=0, tiled=True)  88 us
    pallas_call x1, Pallas kernels, close(): pl.pallas_call(functools.partial(close_kernel, blocks, seqs, reps), grid=...  87.9 us
    pallas_call x3, Pallas kernels, weigh(): pl.pallas_call(weigh_kernel, grid=(steps,), in_specs=specs, out_specs=pl....  53.9 us
    pallas_call x1, Pallas kernels, attend(): pl.pallas_call(functools.partial(attend_kernel, tiles, wide), grid_spec=p...  50.3 us
    ppermute x3, waiting for transfers between devices, neighbours(): return lax.ppermute(facing, axis, [(0, 1), (1, 0)])  48.4 us
    pallas_call x1, Pallas kernels, project(): pl.pallas_call(functools.partial(project_kernel, True, shards), grid=grid...  21.3 us
  transfers between devices with their start and end apart: 9, of which 5 were waited for; matrix products, arithmetic and copies ran while one was open for 3% of the time, Pallas kernels for 48%

profile of v1, /device:TPU:0, one launch (start us, length us, event | category | flops | bytes accessed | tf_op | source)
XLA Modules:
  0.0 667.7 jit_solution(1238565716765785958)
XLA Ops:
  7.2 0.0 all-gather.4.cloned.1.call-start
  7.2 0.8 fusion.8
  8.0 2.1 pad_maximum_fusion.1
  10.1 0.0 all-gather.4.cloned.1.call-update
  10.1 0.0 all-gather.8.cloned.1.call-start
  10.2 0.7 all-gather.8.cloned.1.call-update
  10.9 0.0 all-gather.6.cloned.1.call-start
  10.9 0.3 fusion.19
  11.2 1.9 concatenate.17
  13.1 0.0 all-gather.6.cloned.1.call-update
  13.1 0.0 reduce-scatter.5.cloned.1.call-start
  13.2 0.0 copy-start.9
  13.2 3.1 dynamic-slice_bitcast_fusion
  16.3 2.9 collective-permute-start
  19.3 0.1 slice.31
  19.4 0.1 slice.30
  19.6 0.3 fusion.4
  19.9 0.1 fusion.10
  20.0 0.1 fusion.9
  20.1 0.1 fusion.5
  20.2 0.6 and_select_fusion.4
  20.9 0.9 select_convert_fusion.1.eq_ref
  21.8 1.3 select_convert_fusion.ek_ref
  23.1 7.0 %fusion = (f32[2,1536,128]{2,1,0:T(8,128)}, f32[2,1536,128]{2,1,0:T(8,128)}) fusion(f32[128]{0:T(128)S(1)} %get-tuple-element.76, f32[128]{0:T(128)S(1)} %get-tuple-element.77, f32[2,1536]{1,0:T(2,128)S(1)} %subtract_convert_fusion), kind=kLoop, calls=%fused_computation.5 | loop fusion | flops 786432 | bytes 3159040 | tf_op jit(solution)/shard_map/mul | solution.py:874
  30.1 55.7 %all-gather.4.cloned.1.call-done.w_ref = bf16[1024,3200]{1,0:T(8,128)(2,1)} async-done(((bf16[128,3200]{1,0:T(8,128)(2,1)}), bf16[1024,3200]{1,0:T(8,128)(2,1)}) %all-gather.4.cloned.1.call-update) | async-done | bytes 6553616 | tf_op jit(solution)/shard_map/all_gather | solution.py:908
  85.8 1.0 slice.40
  86.8 0.6 slice_bitcast_fusion
  87.4 21.3 %project_own.1 = (bf16[1024,2048]{1,0:T(8,128)(2,1)}, bf16[2,1536,3072]{2,1,0:T(8,128)(2,1)}) custom-call(bf16[2,1024,1024]{2,1,0:T(8,128)(2,1)} %bitcast.35, bf16[1024,3200]{1,0:T(8,128)(2,1)} %all-gather.4.cloned.1.call-done.w_ref, f32[2,1536,128]{2,1,0:T(8,128)} %get-tuple-element.75.cos_ref, f32[2,1536,128]{2,1,0:T(8,128)} %get-tuple-element.74.sin_ref), custom_call_target="tpu_custom_call" | custom-call | flops 12884901888 | bytes 23068672 | tf_op jit(solution)/shard_map/project_own/pallas_call | solution.py:108
  108.7 1.3 copy-done.4
  110.0 13.5 %project_halo.1.q_ref.k_ref.v_ref = bf16[2,1536,3072]{2,1,0:T(8,128)(2,1)} custom-call(bf16[2,512,1024]{2,1,0:T(8,128)(2,1)} %copy-done.4, bf16[1024,3200]{1,0:T(8,128)(2,1)} %all-gather.4.cloned.1.call-done.w_ref, f32[2,1536,128]{2,1,0:T(8,128)} %get-tuple-element.75.cos_ref, ...), custom_call_target="tpu_custom_call", output_to_operand_aliasing={{}: (4, {})} | custom-call | flops 6442450944 | bytes 14680064 | tf_op jit(solution)/shard_map/project_halo/pallas_call | solution.py:122
  123.6 50.3 %attend.1 = (bf16[2,1024,1024]{2,1,0:T(8,128)(2,1)}, bf16[1024,2048]{1,0:T(8,128)(2,1)}, f32[2,8,2,1024]{3,2,1,0:T(2,128)}) custom-call(s32[1]{0:T(128)} %bitcast.1.own_ref, s32[2,8]{1,0:T(2,128)} %get-tuple-element.78.lo_ref, s32[2,8]{1,0:T(2,128)} %get-tuple-element.79.hi_ref, bf16[2,1536,3072]{2,1,0:T(8,128)(2,1)} %project_halo.1.q_ref.k_ref.v_ref, ...), custom_call_target="tpu_custom_call" | custom-call | flops 25769803776 | bytes 33554432 | tf_op jit(solution)/shard_map/attend/pallas_call | solution.py:254
  173.9 0.0 all-gather.8.cloned.1.call-done.wd_ref
  174.0 32.3 %all-gather.6.cloned.1.call-done.w_ref = bf16[1024,6400]{1,0:T(8,128)(2,1)} async-done(((bf16[128,6400]{1,0:T(8,128)(2,1)}), bf16[1024,6400]{1,0:T(8,128)(2,1)}) %all-gather.6.cloned.1.call-update) | async-done | bytes 13107216 | tf_op jit(solution)/shard_map/all_gather | solution.py:908
  206.2 105.3 %feed.1 = (bf16[2,1024,1024]{2,1,0:T(8,128)(2,1)}, bf16[1024,2048]{1,0:T(8,128)(2,1)}, bf16[2624,2048]{1,0:T(8,128)(2,1)}, bf16[2,1024,6400]{2,1,0:T(8,128)(2,1)...) custom-call(bf16[2,1024,1024]{2,1,0:T(8,128)(2,1)} %bitcast.36, ...), custom_call_target="tpu_custom_call" | custom-call | flops 74625056768 | bytes 67108864 | tf_op jit(solution)/shard_map/feed/pallas_call | solution.py:524
  311.5 1.8 constant_dynamic-slice_fusion
  313.4 1.5 collective-permute-start.1
  314.9 0.1 fusion.2
  315.1 0.6 collective-permute-start.2
  315.7 48.4 %collective-permute-done.2.sth_ref = f32[2,8,4,512]{3,2,1,0:T(4,128)S(1)} collective-permute-done((f32[2,8,4,512]{3,2,1,0:T(4,128)S(1)}, f32[2,8,4,512]{3,2,1,0:T(4,128)S(1)}, u32[]{:S(2)}, u32[]{:S(2)}) %collective-permute-start.2) | collective-permute-done | bytes 131104 | tf_op jit(solution)/shard_map/ppermute | solution.py:840
  364.1 16.7 %weigh_down.1 = bf16[2624,1024]{1,0:T(8,128)(2,1)} custom-call(bf16[2624,2048]{1,0:T(8,128)(2,1)} %get-tuple-element.37.left_ref, bf16[2048,1024]{1,0:T(8,128)(2,1)} %bitcast.46), custom_call_target="tpu_custom_call" | custom-call | flops 11005853696 | bytes 16777216 | tf_op jit(solution)/shard_map/weigh_down/pallas_call | solution.py:562
  380.8 0.0 reduce-scatter.5.cloned.1.call-update
  380.8 0.0 reduce-scatter.3.cloned.1.call-start
  380.9 28.4 %weigh_in.1.outs_0_ = bf16[1024,6400]{1,0:T(8,128)(2,1)} custom-call(bf16[1024,2048]{1,0:T(8,128)(2,1)} %get-tuple-element.40.left_ref, bf16[2048,6400]{1,0:T(8,128)(2,1)} %bitcast.29), custom_call_target="tpu_custom_call" | custom-call | flops 22548578304 | bytes 16777216 | tf_op jit(solution)/shard_map/weigh_in/pallas_call | solution.py:562
  409.3 8.7 %weigh_out.1 = bf16[1024,6400]{1,0:T(8,128)(2,1)} custom-call(bf16[1024,2048]{1,0:T(8,128)(2,1)} %get-tuple-element.38.left_ref, bf16[2048,6400]{1,0:T(8,128)(2,1)} %bitcast.30, bf16[1024,6400]{1,0:T(8,128)(2,1)} %weigh_in.1.outs_0_), custom_call_target="tpu_custom_call", output_to_operand_aliasing={{}: (2, {})} | custom-call | flops 4294967296 | bytes 16777216 | tf_op jit(solution)/shard_map/weigh_out/pallas_call | solution.py:562
  418.0 0.0 reduce-scatter.3.cloned.1.call-update
  418.0 0.0 all-reduce.5.cloned.1.call-start
  418.1 0.8 pad_maximum_fusion.2.st_ref
  418.9 109.5 %attend_back.1 = bf16[3,2,1024,1024]{3,2,1,0:T(8,128)(2,1)} custom-call(s32[1]{0:T(128)} %bitcast.1.own_ref, s32[2,8]{1,0:T(2,128)} %get-tuple-element.78.lo_ref, s32[2,8]{1,0:T(2,128)} %get-tuple-element.79.hi_ref, bf16[2,1536,3072]{2,1,0:T(8,128)(2,1)} %project_halo.1.q_ref.k_ref.v_ref, bf16[2,1536,3072]{2,1,0:T(8,128)(2,1)} %project_halo.1.q_ref.k_ref.v_ref, ...), custom_call_target="tpu_custom_call" | custom-call | flops 64424509440 | bytes 67108864 | tf_op jit(solution)/shard_map/attend_back/pallas_call | solution.py:426
  528.4 0.0 reduce-scatter.5.cloned.1.call-done
  528.4 8.5 %reduce-scatter.3.cloned.1.call-done = bf16[128,6400]{1,0:T(8,128)(2,1)} async-done(((bf16[1024,6400]{1,0:T(8,128)(2,1)}), bf16[128,6400]{1,0:T(8,128)(2,1)}) %reduce-scatter.3.cloned.1.call-update) | async-done | bytes 1638416 | tf_op jit(solution)/shard_map/reduce_scatter | solution.py:929
  536.9 0.0 all-reduce.5.cloned.1.call-update
  536.9 0.0 copy-start.3
  536.9 87.9 %close.1 = (f32[2048,1024]{1,0:T(8,128)}, f32[128,3072]{1,0:T(8,128)}) custom-call(bf16[1024,2048]{1,0:T(8,128)(2,1)} %get-tuple-element.30.h1t_ref, bf16[3,2048,1024]{2,1,0:T(8,128)(2,1)} %bitcast.47, bf16[3,2048,1024]{2,1,0:T(8,128)(2,1)} %bitcast.48, bf16[1024,3200]{1,0:T(8,128)(2,1)} %all-gather.4.cloned.1.call-done.w_ref, bf16[2048,1024]{1,0:T(8,128)(2,1)} %bitcast.37, ...), custom_call_target="tpu_custom_call" | custom-call | flops 25769803776 | bytes 50331648 | tf_op jit(solution)/shard_map/close/pallas_call | solution.py:794
  624.9 1.6 multiply_reduce_fusion.1
  626.5 0.5 convert_divide_fusion.1
  627.0 21.1 %all-reduce.5.cloned.1.call-done = (bf16[128,6400]{1,0:T(8,128)(2,1)}, bf16[328,1024]{1,0:T(8,128)(2,1)}) async-done(((bf16[128,6400]{1,0:T(8,128)(2,1)}, bf16[328,1024]{1,0:T(8,128)(2,1)}), (bf16[128,6400]{1,0:T(8,128)(2,1)}, bf16[328,1024]{1,0:T(8,128)(2,1)})) %all-reduce.5.cloned.1.call-update) | async-done | bytes 2310160 | tf_op jit(solution)/shard_map/psum | solution.py:952
  648.1 1.9 slice.45
  650.1 1.6 fusion.18
  651.7 1.2 convert_element_type.65
  652.9 0.6 copy-done.2
  653.5 2.0 multiply_reduce_fusion
  655.5 0.5 convert_divide_fusion
  656.0 3.4 copy.35
  659.4 1.1 copy.36
  (47 shorter events, 0.2 us)
Async XLA Ops:
  7.2 3.7 copy-start.1
  7.2 78.6 %all-gather.4.cloned.1.call-start = ((), (), s32[]{:S(2)}) async-start(), calls=%async_computation.2 | async-start | bytes 7372800 | tf_op jit(solution)/shard_map/all_gather | solution.py:908
  10.1 1.1 copy-start.8
  10.1 163.8 %all-gather.8.cloned.1.call-start = ((), (), s32[]{:S(2)}) async-start(), calls=%async_computation.4 | async-start | bytes 6045696 | tf_op jit(solution)/shard_map/all_gather | solution.py:908
  10.9 195.4 %all-gather.6.cloned.1.call-start = ((), (), s32[]{:S(2)}) async-start(), calls=%async_computation.3 | async-start | bytes 14745600 | tf_op jit(solution)/shard_map/all_gather | solution.py:908
  13.1 515.3 %reduce-scatter.5.cloned.1.call-start = ((), (), s32[]{:S(2)}) async-start(), calls=%async_computation.6 | async-start | bytes 6045696 | tf_op jit(solution)/shard_map/reduce_scatter | solution.py:929
  13.2 6.0 copy-start.9
  16.3 92.4 %collective-permute-start = (bf16[2,512,1024]{2,1,0:T(8,128)(2,1)}, bf16[2,512,1024]{2,1,0:T(8,128)(2,1)S(1)}, u32[]{:S(2)}, u32[]{:S(2)}) collective-permute-start(bf16[2,512,1024]{2,1,0:T(8,128)(2,1)} %dynamic-slice_bitcast_fusion), channel_id=1, source_target_pairs={{0,16},{16,0},{1,17},{17,1},{2,18},{18,2},{3,19},{19,3},{4,20},{20... | collective-permute-start | bytes 6291464 | tf_op jit(solution)/shard_map/ppermute | solution.py:840
  108.7 1.3 copy-start.4
  311.5 3.4 copy-start.6
  311.5 3.4 copy-start.7
  313.4 50.7 %collective-permute-start.1 = (bf16[2,512,1024]{2,1,0:T(8,128)(2,1)S(1)}, bf16[2,512,1024]{2,1,0:T(8,128)(2,1)S(1)}, u32[]{:S(2)}, u32[]{:S(2)}) collective-permute-start(bf16[2,512,1024]{2,1,0:T(8,128)(2,1)S(1)} %constant_dynamic-slice_fusion), channel_id=1, source_target_pairs={{0,16},{16,0},{1,17},{17,1},{2,18},{18,2},{3,19},{19,3},{4,20},{20... | collective-permute-start | bytes 6291464 | tf_op jit(solution)/shard_map/ppermute | solution.py:840
  315.1 49.0 %collective-permute-start.2 = (f32[2,8,4,512]{3,2,1,0:T(4,128)S(1)}, f32[2,8,4,512]{3,2,1,0:T(4,128)S(1)}, u32[]{:S(2)}, u32[]{:S(2)}) collective-permute-start(f32[2,8,4,512]{3,2,1,0:T(4,128)S(1)} %fusion.2), channel_id=1, source_target_pairs={{0,16},{16,0},{1,17},{17,1},{2,18},{18,2},{3,19},{19,3},{4,20},{20... | collective-permute-start | bytes 393224 | tf_op jit(solution)/shard_map/ppermute | solution.py:840
  364.0 16.8 %copy-start.13 = (f32[2,8,4,512]{3,2,1,0:T(4,128)}, f32[2,8,4,512]{3,2,1,0:T(4,128)S(1)}, u32[]{:S(2)}) copy-start(f32[2,8,4,512]{3,2,1,0:T(4,128)S(1)} %collective-permute-done.2.sth_ref) | copy-start | bytes 393220
  364.0 16.8 %copy-start.12 = (bf16[2,512,1024]{2,1,0:T(8,128)(2,1)}, bf16[2,512,1024]{2,1,0:T(8,128)(2,1)S(1)}, u32[]{:S(2)}) copy-start(bf16[2,512,1024]{2,1,0:T(8,128)(2,1)S(1)} %collective-permute-done.1.doh_ref) | copy-start | bytes 6291460
  380.8 156.1 %reduce-scatter.3.cloned.1.call-start = ((), (), s32[]{:S(2)}) async-start(), calls=%async_computation.5 | async-start | bytes 14745600 | tf_op jit(solution)/shard_map/reduce_scatter | solution.py:929
  418.0 230.1 %all-reduce.5.cloned.1.call-start = ((), (), s32[]{:S(2)}) async-start(), calls=%async_computation.7 | async-start | bytes 4620288 | tf_op jit(solution)/shard_map/psum | solution.py:952
  536.9 87.9 %copy-start.3 = (bf16[128,3072]{1,0:T(8,128)(2,1)S(1)}, bf16[128,3072]{1,0:T(8,128)(2,1)}, u32[]{:S(2)}) copy-start(bf16[128,3072]{1,0:T(8,128)(2,1)} %param.14) | copy-start | bytes 2359300
  624.8 1.7 copy-start.10
  648.1 7.9 %slice-start = ((s8[8388608]{0:T(1024)(128)(4,1)}), s8[4194304]{0:T(1024)(128)(4,1)S(1)}, s32[]{:S(2)}) async-start(s8[8388608]{0:T(1024)(128)(4,1)} %bitcast.31), calls=%async_computation.8 | async-start | bytes 8388608
  650.1 1.6 copy-start.5
  651.6 1.8 copy-start.2
  651.7 4.4 slice-start.1
  653.5 2.1 copy-start.11
  656.0 3.4 copy-start
Sparse Core Ops, SparseCore 0:
  10.5 75.2 all-gather.3
  87.7 41.6 all-gather.7
  131.9 74.3 all-gather.5
  381.0 57.2 reduce-scatter.4
  441.7 95.1 reduce-scatter.2
  539.2 108.8 all-reduce.4

commit v2 on v1

--- a/solution.py
+++ b/solution.py
@@ -18,6 +18,7 @@
 MASKED = -1e30
 
 TILE = 256
+CUT = 512
 REACH = HALF // TILE
 LANES = 128
 FF_PAD = -(-FF // LANES) * LANES
@@ -28,6 +29,8 @@
 
 F32 = jnp.float32
 BF16 = jnp.bfloat16
+
+MESH = pl.DeviceIdType.MESH
 
 NN = (((1,), (0,)), ((), ()))
 NT = (((1,), (1,)), ((), ()))
@@ -288,8 +291,8 @@
     )(own, lows, highs, qkv, qkv, qkv, marks_k, marks_q)
 
 
-def attend_back_kernel(tiles, wide, own_ref, lo_ref, hi_ref, q_ref, k_ref, v_ref, do_ref, doh_ref, st_ref, sth_ref,
-                       ek_ref, eq_ref, cos_ref, sin_ref, out_ref,
+def attend_back_kernel(tiles, wide, own_ref, lo_ref, hi_ref, q_ref, k_ref, v_ref, do_ref, doh_ref, lse_ref, lseh_ref,
+                       delta_ref, deltah_ref, ek_ref, eq_ref, cos_ref, sin_ref, out_ref,
                        kx, vx, qx, dx, dn, kt, dqt, edges):
     batch = pl.program_id(0)
     extent = k_ref.shape[1]
@@ -321,10 +324,11 @@
         vx[2 * pair] = jnp.where(low, values, units)
         vx[2 * pair + 1] = jnp.where(low, units, values)
         turned, flipped = q_ref[0, :, span].T, dn[:, span].T
-        stats = jnp.concatenate([st_ref[0, pair], sth_ref[0, pair]], axis=1)
+        lses = jnp.concatenate([lse_ref[0, pair], lseh_ref[0, pair]], axis=1)
+        deltas = jnp.concatenate([delta_ref[0, pair], deltah_ref[0, pair]], axis=1)
         for half in range(2):
-            lse = split3(stats[half : half + 1])
-            delta = split3(stats[half + 2 : half + 3])
+            lse = split3(lses[half : half + 1])
+            delta = split3(deltas[half : half + 1])
             mark, shift = label_rows, jnp.zeros((HEAD_DIM, extent), F32)
             for place in range(3):
                 mark = jnp.where(row == 8 + place, -lse[place], mark)
@@ -413,7 +417,8 @@
         out_ref[0, 0, :, span] = (raw * cos_ref[0] - swapped(raw) * sin_ref[0]).astype(BF16)
 
 
-def attend_back(own, lows, highs, qkv, grads, grads_halo, stats, stats_halo, marks_k, marks_q, cosines, sines):
+def attend_back(own, lows, highs, qkv, grads, grads_halo, lse, lse_halo, delta, delta_halo, marks_k, marks_q,
+                cosines, sines):
     batch, extent, _ = qkv.shape
     stretch, width = grads.shape[1:]
     halo = extent - stretch
@@ -422,7 +427,7 @@
     groups = PAIRS // wide
     spec = lambda rows, offset: pl.BlockSpec((1, rows, wide * LANES), lambda b, p, *_: (b, 0, p + offset))
     per = lambda rows: pl.BlockSpec((1, rows, LANES), lambda b, p, *_: (b, 0, 0))
-    numbers = lambda rows: pl.BlockSpec((1, wide, 4, rows), lambda b, p, *_: (b, p, 0, 0))
+    numbers = lambda rows: pl.BlockSpec((1, wide, 2, rows), lambda b, p, *_: (b, p, 0, 0))
     return pl.pallas_call(
         functools.partial(attend_back_kernel, tiles, wide),
         grid_spec=pltpu.PrefetchScalarGridSpec(
@@ -434,6 +439,8 @@
                 spec(extent, 2 * groups),
                 spec(stretch, 0),
                 spec(halo, 0),
+                numbers(stretch),
+                numbers(halo),
                 numbers(stretch),
                 numbers(halo),
                 per(extent),
@@ -459,11 +466,58 @@
             flops=5 * 2 * HEADS * batch * stretch * extent * 128, bytes_accessed=64 * 1024 * 1024, transcendentals=0
         ),
         name="attend_back",
-    )(own, lows, highs, qkv, qkv, qkv, grads, grads_halo, stats, stats_halo, marks_k, marks_q, cosines, sines)
-
-
-def feed_kernel(x_ref, o_ref, g_ref, gain_ref, w_ref, wd_ref,
-                out_ref, h2t_ref, hidt_ref, slopes_ref, dr_ref, do_ref, delta_ref):
+    )(own, lows, highs, qkv, qkv, qkv, grads, grads_halo, lse, lse_halo, delta, delta_halo, marks_k, marks_q,
+      cosines, sines)
+
+
+def feed_kernel(seqs, halo_tiles, x_ref, o_ref, g_ref, gain_ref, w_ref, wd_ref,
+                out_ref, h2t_ref, hidt_ref, slopes_ref, dr_ref, do_ref, delta_ref, do_halo, delta_halo,
+                do_sent, delta_sent, send_sem, recv_sem):
+    batch, steps = pl.num_programs(1), pl.num_programs(0)
+    step, sequence = pl.program_id(0), pl.program_id(1)
+    seq = lax.axis_index("seq")
+    mine, tiles = steps, steps + halo_tiles
+    reach = -(-REACH // mine)
+    hops = [hop for hop in range(-reach, reach + 1) if hop != 0]
+
+    def exists(hop):
+        return (seq + hop >= 0) & (seq + hop < seqs)
+
+    def sent(which, tile, hop):
+        peer = seq + hop
+        place = seq * mine + tile
+        wanted = exists(hop) & (place >= peer * mine - REACH) & (place < (peer + 1) * mine + REACH)
+        slot = lax.rem(place - peer * mine + tiles, tiles) - mine
+        slot = jnp.where(wanted, slot, 0)
+        return wanted, halo_copies(which, tile, slot, hops.index(hop), peer)
+
+    def halo_copies(which, tile, slot, hop, peer):
+        span = pl.ds(pl.multiple_of(slot * TILE, TILE), TILE)
+        pieces = [
+            (do_sent.at[which, tile], do_halo.at[which, span]),
+            (delta_sent.at[which, tile], delta_halo.at[which, :, :, span]),
+        ]
+        return [
+            pltpu.make_async_remote_copy(
+                src_ref=source, dst_ref=target, send_sem=send_sem.at[kind, which, tile, hop],
+                recv_sem=recv_sem.at[kind, which, slot], device_id={"seq": peer}, device_id_type=MESH,
+            )
+            for kind, (source, target) in enumerate(pieces)
+        ]
+
+    @pl.when((step == 0) & (sequence == 0))
+    def _():
+        barrier = pltpu.get_barrier_semaphore()
+        for hop in hops:
+            @pl.when(exists(hop))
+            def _():
+                pl.semaphore_signal(barrier, inc=1, device_id={"seq": seq + hop}, device_id_type=MESH)
+
+        for hop in hops:
+            @pl.when(exists(hop))
+            def _():
+                pl.semaphore_wait(barrier, 1)
+
     mixed = o_ref[0]
     seeds = g_ref[0]
     gain = gain_ref[...]
@@ -493,6 +547,7 @@
         total = total + dot(hid, wd_ref[start:stop, :])
         back = back + dot(grad_gate, w_ref[:, gates], NT) + dot(grad_up, w_ref[:, ups], NT)
     blank = jnp.zeros((TILE, FF_PAD - FF), BF16)
+    slopes_ref[0, :, 2 * FF_PAD + width :] = jnp.zeros((TILE, slopes_ref.shape[2] - 2 * FF_PAD - width), BF16)
     slopes_ref[0, :, FF:FF_PAD] = blank
     slopes_ref[0, :, FF_PAD + FF : 2 * FF_PAD] = blank
     out_ref[0] = total.astype(BF16)
@@ -509,38 +564,100 @@
     column = lax.broadcasted_iota(jnp.int32, (HEADS, width), 1)
     pick = jnp.where(column // HEAD_DIM == head, 1.0, 0.0).astype(BF16)
     delta = dot(pick, high, NT) + dot(pick, rest, NT)
+    tile = facing_first(step, steps, seqs)
+    do_sent[sequence, tile] = do
     for pair in range(PAIRS):
         delta_ref[0, pair] = delta[2 * pair : 2 * pair + 2]
-
-
-def feed(x, mixed, seeds, gain, w_rest, w_down):
+        delta_sent[sequence, tile, pair] = delta[2 * pair : 2 * pair + 2]
+    for hop in hops:
+        wanted, copies = sent(sequence, tile, hop)
+
+        @pl.when(wanted)
+        def _():
+            for copy in copies:
+                copy.start()
+
+    @pl.when((step == steps - 1) & (sequence == batch - 1))
+    def _():
+        def settle(index, carry):
+            which, tile = index // mine, lax.rem(index, mine)
+            for hop in hops:
+                wanted, copies = sent(which, tile, hop)
+
+                @pl.when(wanted)
+                def _():
+                    for copy in copies:
+                        copy.wait_send()
+
+            return carry
+
+        lax.fori_loop(0, batch * mine, settle, 0)
+
+        def arrive(index, carry):
+            which, slot = index // halo_tiles, lax.rem(index, halo_tiles)
+            place = seq * mine + mine + slot
+            if halo_tiles == REACH:
+                place = jnp.where(seq == 0, place, place - tiles)
+            else:
+                place = jnp.where(slot < REACH, place, place - tiles)
+
+            @pl.when((place >= 0) & (place < seqs * mine))
+            def _():
+                for copy in halo_copies(which, 0, slot, 0, seq):
+                    copy.wait_recv()
+
+            return carry
+
+        lax.fori_loop(0, batch * halo_tiles, arrive, 0)
+
+
+def facing_first(step, steps, seqs):
+    if seqs != 2:
+        return step
+    return lax.rem(step + (1 - lax.axis_index("seq")) * (steps // 2), steps)
+
+
+def feed(x, mixed, seeds, gain, w_rest, w_down, seqs, halo):
     batch, rows, width = x.shape
     steps = rows // TILE
-    block = lambda n: pl.BlockSpec((1, TILE, n), lambda b, i: (b, i, 0))
-    turned = lambda n: pl.BlockSpec((n, TILE), lambda b, i: (0, b * steps + i))
-    fixed = lambda m, n: pl.BlockSpec((m, n), lambda b, i: (0, 0), pipeline_mode=pl.Buffered(1))
+    place = lambda i: facing_first(i, steps, seqs)
+    block = lambda n: pl.BlockSpec((1, TILE, n), lambda i, b: (b, place(i), 0))
+    turned = lambda n: pl.BlockSpec((n, TILE), lambda i, b: (0, b * steps + place(i)))
+    fixed = lambda m, n: pl.BlockSpec((m, n), lambda i, b: (0, 0), pipeline_mode=pl.Buffered(1))
     shape = lambda n, t: jax.ShapeDtypeStruct((batch, rows, n), t)
     columns = w_rest.shape[1]
+    padded = -(-columns // CUT) * CUT
+    reach = -(-REACH // steps)
     return pl.pallas_call(
-        feed_kernel,
-        grid=(batch, steps),
+        functools.partial(feed_kernel, seqs, halo // TILE),
+        grid=(steps, batch),
         in_specs=[
             block(width), block(width), block(width), fixed(1, width), fixed(width, columns), fixed(FF, width),
         ],
         out_specs=[
-            block(width), turned(width), turned(FF), block(columns), block(width), block(width),
-            pl.BlockSpec((1, PAIRS, 2, TILE), lambda b, i: (b, 0, 0, i)),
+            block(width), turned(width), turned(FF), block(padded), block(width), block(width),
+            pl.BlockSpec((1, PAIRS, 2, TILE), lambda i, b: (b, 0, 0, place(i))),
+            pl.BlockSpec(memory_space=pl.ANY),
+            pl.BlockSpec(memory_space=pl.ANY),
         ],
         out_shape=[
             shape(width, BF16),
             jax.ShapeDtypeStruct((width, batch * rows), BF16),
             jax.ShapeDtypeStruct((FF, batch * rows), BF16),
-            shape(columns, BF16),
+            shape(padded, BF16),
             shape(width, F32),
             shape(width, BF16),
             jax.ShapeDtypeStruct((batch, PAIRS, 2, rows), F32),
+            jax.ShapeDtypeStruct((batch, halo, width), BF16),
+            jax.ShapeDtypeStruct((batch, PAIRS, 2, halo), F32),
         ],
-        compiler_params=params(),
+        scratch_shapes=[
+            pltpu.VMEM((batch, steps, TILE, width), BF16),
+            pltpu.VMEM((batch, steps, PAIRS, 2, TILE), F32),
+            pltpu.SemaphoreType.DMA((2, batch, steps, 2 * reach)),
+            pltpu.SemaphoreType.DMA((2, batch, halo // TILE)),
+        ],
+        compiler_params=params(collective_id=2, has_side_effects=True),
         cost_estimate=pl.CostEstimate(
             flops=2 * batch * rows * width * (6 * FF + 2 * width), bytes_accessed=64 * 1024 * 1024, transcendentals=0
         ),
@@ -548,40 +665,95 @@
     )(x, mixed, seeds, gain, w_rest, w_down)
 
 
-def weigh_kernel(left_ref, right_ref, *outs):
-    outs[-1][...] = dot(left_ref[...], right_ref[...].reshape(right_ref.shape[-2:])).astype(BF16)
-
-
-def weigh(left, right, name, left_block, right_block, out_block, left_map, right_map, out_map, steps, shape, held=None):
-    specs = [pl.BlockSpec(left_block, left_map), pl.BlockSpec(right_block, right_map)]
-    arrays = [left, right]
-    if held is not None:
-        specs.append(pl.BlockSpec(memory_space=pl.ANY))
-        arrays.append(held)
-    rows, columns = out_block
+def weigh_kernel(blocks, share, held, turns, *refs):
+    lefts, (right_ref, out_ref, prod, kept, sent, got, send_sem, recv_sem) = refs[:-8], refs[-8:]
+    step = pl.program_id(0)
+    dp = lax.axis_index("dp")
+    core = lax.rem(dp, 2)
+    mate = dp + 1 - 2 * core
+    places = prod.shape[0] // (2 * share)
+
+    def to_mate(n):
+        return pltpu.make_async_remote_copy(
+            src_ref=sent.at[n], dst_ref=got.at[n], send_sem=send_sem.at[n], recv_sem=recv_sem.at[n],
+            device_id={"dp": mate}, device_id_type=MESH,
+        )
+
+    @pl.when(step == 0)
+    def _():
+        barrier = pltpu.get_barrier_semaphore()
+        pl.semaphore_signal(barrier, inc=1, device_id={"dp": mate}, device_id_type=MESH)
+        pl.semaphore_wait(barrier, 1)
+
+    columns = right_ref.shape[1]
+    for first, last, pieces in turns:
+
+        @pl.when((step >= first) & (step < last))
+        def _():
+            start = 0
+            for which, count in pieces:
+                span = slice(start, start + count)
+                prod[:, span] = dot(lefts[which][...], right_ref[:, span])
+                start += count
+
+    @pl.when(step < blocks)
+    def _():
+        for place in range(places):
+            even = prod[2 * place * share : (2 * place + 1) * share, :]
+            odd = prod[(2 * place + 1) * share : (2 * place + 2) * share, :]
+            rows = slice(place * held, place * held + share)
+            sent[step, rows, :] = jnp.where(core == 0, odd, even).astype(BF16)
+            kept[step % 2, rows, :] = jnp.where(core == 0, even, odd)
+            if held > share:
+                rows = slice(place * held + share, (place + 1) * held)
+                sent[step, rows, :] = jnp.zeros((held - share, columns), BF16)
+                kept[step % 2, rows, :] = jnp.zeros((held - share, columns), F32)
+        to_mate(step).start()
+
+    @pl.when(step >= 1)
+    def _():
+        done = step - 1
+        to_mate(done).wait()
+        out_ref[...] = (kept[done % 2] + got[done].astype(F32)).astype(BF16)
+
+
+def weigh(lefts, right, columns, blocks, turns, share, name, number):
+    rows, tokens = lefts[0].shape
+    total = blocks * columns
+    held = -(-share // 16) * 16
+    places = rows // (2 * share)
+    fixed = pl.BlockSpec((rows, tokens), lambda n: (0, 0), pipeline_mode=pl.Buffered(1))
     return pl.pallas_call(
-        weigh_kernel,
-        grid=(steps,),
-        in_specs=specs,
-        out_specs=pl.BlockSpec(out_block, out_map),
-        out_shape=jax.ShapeDtypeStruct(shape, BF16),
-        input_output_aliases={} if held is None else {2: 0},
-        compiler_params=params(),
+        functools.partial(weigh_kernel, blocks, share, held, turns),
+        grid=(blocks + 1,),
+        in_specs=[fixed] * len(lefts) + [pl.BlockSpec((tokens, columns), lambda n: (0, jnp.minimum(n, blocks - 1)))],
+        out_specs=pl.BlockSpec((places * held, columns), lambda n: (0, jnp.maximum(n - 1, 0))),
+        out_shape=jax.ShapeDtypeStruct((places * held, total), BF16),
+        scratch_shapes=[
+            pltpu.VMEM((rows, columns), F32),
+            pltpu.VMEM((2, places * held, columns), F32),
+            pltpu.VMEM((blocks, places * held, columns), BF16),
+            pltpu.VMEM((blocks, places * held, columns), BF16),
+            pltpu.SemaphoreType.DMA((blocks,)),
+            pltpu.SemaphoreType.DMA((blocks,)),
+        ],
+        compiler_params=params(collective_id=number, has_side_effects=True),
         cost_estimate=pl.CostEstimate(
-            flops=2 * steps * rows * columns * left.shape[1], bytes_accessed=16 * 1024 * 1024, transcendentals=0
+            flops=2 * rows * tokens * total, bytes_accessed=24 * 1024 * 1024, transcendentals=0
         ),
         name=name,
-    )(*arrays)
-
-
-MESH = pl.DeviceIdType.MESH
-CUT = 512
+    )(*lefts, right)
+
+
 LAGS = (1, 3, 5, 6, 7, 8)
-
-
-def close_kernel(blocks, seqs, reps, h1t_ref, right_ref, three_ref, w_ref, x_ref, dr_ref, gain_ref, gi_ref, sum_ref,
+RING, RING_XY, RING_LINE = 5, 2, 4
+EARLY, DOWN_BLOCKS, LINE_LAG = 8, 4, 2
+
+
+def close_kernel(blocks, rest_blocks, rest_edge, seqs, reps, h2t_ref, ot_ref, h1t_ref, rest_ref, right_ref, three_ref, w_ref, x_ref, dr_ref, gain_ref, early_ref, down_ref,
+                 gi_ref, rest_sum, sum_ref, early_sum, down_sum,
                  prod, kept0, kept1x, kept1y, kept2, s0, r0, s1x, r1x, s1y, r1y, s2x, r2x, s2y, r2y,
-                 mine, ends, half, others, whole, send_sem, recv_sem):
+                 mine, ends, others, early_ends, early_others, down_ends, down_others, send_sem, recv_sem, line_sem):
     step = pl.program_id(0)
     width = h1t_ref.shape[0]
     share = mine.shape[1]
@@ -594,34 +766,57 @@
     slot_seq, slot_side, slot_in = 1, seqs, seqs + 1
 
     def copy(source, target, n, slot, device):
+        turn = lax.rem(n, 2 * RING_XY)
         return pltpu.make_async_remote_copy(
-            src_ref=source, dst_ref=target, send_sem=send_sem.at[n, slot], recv_sem=recv_sem.at[n, slot],
+            src_ref=source, dst_ref=target, send_sem=send_sem.at[turn, slot], recv_sem=recv_sem.at[turn, slot],
             device_id=device, device_id_type=MESH,
         )
 
     def rows(first, count):
         return pl.ds(pl.multiple_of(first * share, share), count * share)
 
+    def half(n):
+        return lax.rem(n // 2, RING_XY)
+
     def to_mate(n):
-        return [copy(s0.at[n], r0.at[n], n, 0, {"dp": mate})]
+        slot = lax.rem(n, RING)
+        return [copy(s0.at[slot], r0.at[slot], n, 0, {"dp": mate})]
 
     def to_seq(n, source, target):
         return [
-            copy(source.at[n // 2, hop], target.at[n // 2, hop], n, slot_seq + hop, {"seq": peer})
+            copy(source.at[half(n), hop], target.at[half(n), hop], n, slot_seq + hop, {"seq": peer})
             for hop, peer in enumerate(seq_peers)
         ]
 
     def to_side(n, source, target):
-        return [copy(source.at[n // 2], target.at[n // 2], n, slot_side, {"dp": across})]
-
-    def inwards(n):
-        return copy(mine.at[n], ends.at[n], n, slot_in, {"rep": beside})
-
-    def between(n):
-        return copy(half.at[n], others.at[n], n, slot_in + 1, {"rep": reps - 1 - rep})
-
-    def outwards(n):
-        return copy(whole.at[n], whole.at[n], n, slot_in + 2, {"rep": beside})
+        return [copy(source.at[half(n)], target.at[half(n)], n, slot_side, {"dp": across})]
+
+    def line(which, source, first, second, sends, arrivals):
+        start, target, device = (
+            (source, first, beside), (first, second, reps - 1 - rep), (second, second, beside),
+        )[which]
+        return pltpu.make_async_remote_copy(
+            src_ref=start, dst_ref=target, send_sem=sends, recv_sem=arrivals,
+            device_id={"rep": device}, device_id_type=MESH,
+        )
+
+    def own_line(n, which):
+        slot, turn = slot_in + which, lax.rem(n, RING_LINE)
+        return line(which, mine.at[turn], ends.at[turn], others.at[turn], send_sem.at[turn, slot], recv_sem.at[turn, slot])
+
+    early_columns, down_columns = early_ends.shape[2], down_ends.shape[2]
+    extra = []
+    for k in range(down_ends.shape[0]):
+        extra.append((down_ref, down_ends, down_others, down_sum, k, slice(k * down_columns, (k + 1) * down_columns)))
+    for k in range(early_ends.shape[0]):
+        extra.append((early_ref, early_ends, early_others, early_sum, k, slice(k * early_columns, (k + 1) * early_columns)))
+
+    def extra_line(index, which):
+        source, first, second, _, k, columns = extra[index]
+        return line(
+            which, source.at[:, columns], first.at[k], second.at[k],
+            line_sem.at[0, index, which], line_sem.at[1, index, which],
+        )
 
     def start(copies):
         for each in copies:
@@ -648,12 +843,38 @@
         def _():
             pl.semaphore_wait(barrier, len(partners))
 
+    for index in range(len(extra)):
+        @pl.when((step == index) & jnp.logical_not(inner))
+        def _():
+            extra_line(index, 0).start()
+
+    whole_blocks, split = rest_edge // CUT, rest_edge % CUT
+
+    @pl.when(step < whole_blocks)
+    def _():
+        prod[...] = dot(h2t_ref[...], rest_ref[...])
+
+    @pl.when((step >= whole_blocks) & (step < rest_blocks))
+    def _():
+        if split:
+            @pl.when(step == whole_blocks)
+            def _():
+                prod[:, :split] = dot(h2t_ref[...], rest_ref[:, :split])
+                prod[:, split:] = dot(ot_ref[...], rest_ref[:, split:])
+
+        @pl.when(step >= whole_blocks + (split > 0))
+        def _():
+            prod[...] = dot(ot_ref[...], rest_ref[...])
+
+    @pl.when((step >= rest_blocks) & (step < blocks))
+    def _():
+        prod[...] = dot(h1t_ref[...], right_ref[0])
+
     @pl.when(step < blocks)
     def _():
-        prod[...] = dot(h1t_ref[...], right_ref[0])
         for place in range(2 * seqs):
             span = slice(place * share, (place + 1) * share)
-            s0[step, span, :] = prod[rows(2 * place + 1 - core, 1), :].astype(BF16)
+            s0[lax.rem(step, RING), span, :] = prod[rows(2 * place + 1 - core, 1), :].astype(BF16)
         start(to_mate(step))
         for place in range(2 * seqs):
             span = slice(place * share, (place + 1) * share)
@@ -668,39 +889,75 @@
         unit, inverse = normed(x_ref[...].astype(F32))
         gi_ref[...] = dr_ref[...] + norm_back(back * gain_ref[...], unit, inverse)
 
+    for index, (source, first, second, total, k, columns) in enumerate(extra):
+        meet, share_out, close_out = (index + LINE_LAG * hop for hop in (1, 2, 3))
+
+        @pl.when((step == meet) & inner)
+        def _():
+            extra_line(index, 0).wait_recv()
+            first[k] = (source[:, columns].astype(F32) + first[k].astype(F32)).astype(BF16)
+            extra_line(index, 1).start()
+
+        @pl.when((step == share_out) & inner)
+        def _():
+            extra_line(index, 1).wait()
+            second[k] = (first[k].astype(F32) + second[k].astype(F32)).astype(BF16)
+            extra_line(index, 2).start()
+
+        @pl.when(step == close_out)
+        def _():
+            @pl.when(inner)
+            def _():
+                extra_line(index, 2).wait_send()
+
+            @pl.when(jnp.logical_not(inner))
+            def _():
+                extra_line(index, 0).wait_send()
+                extra_line(index, 2).wait_recv()
+
+            total[:, columns] = second[k]
+
     n6 = step - LAGS[5]
 
     @pl.when((n6 >= 0) & (n6 < blocks))
     def _():
         @pl.when(inner)
         def _():
-            outwards(n6).wait_send()
+            own_line(n6, 2).wait_send()
 
         @pl.when(jnp.logical_not(inner))
         def _():
-            outwards(n6).wait_recv()
-
-        sum_ref[:, pl.ds(pl.multiple_of(n6 * CUT, CUT), CUT)] = whole[n6].astype(F32)
+            own_line(n6, 2).wait_recv()
+
+        total = others[lax.rem(n6, RING_LINE)]
+
+        @pl.when(n6 < rest_blocks)
+        def _():
+            rest_sum[:, pl.ds(pl.multiple_of(n6 * CUT, CUT), CUT)] = total
+
+        @pl.when(n6 >= rest_blocks)
+        def _():
+            sum_ref[:, pl.ds(pl.multiple_of((n6 - rest_blocks) * CUT, CUT), CUT)] = total
 
     n5 = step - LAGS[4]
 
     @pl.when((n5 >= 0) & (n5 < blocks) & inner)
     def _():
-        between(n5).wait()
-        whole[n5] = (half[n5].astype(F32) + others[n5].astype(F32)).astype(BF16)
-        outwards(n5).start()
+        own_line(n5, 1).wait()
+        others[lax.rem(n5, RING_LINE)] = (ends[lax.rem(n5, RING_LINE)].astype(F32) + others[lax.rem(n5, RING_LINE)].astype(F32)).astype(BF16)
+        own_line(n5, 2).start()
 
     n4 = step - LAGS[3]
 
     @pl.when((n4 >= 0) & (n4 < blocks) & inner)
     def _():
-        inwards(n4).wait_recv()
-        half[n4] = (mine[n4].astype(F32) + ends[n4].astype(F32)).astype(BF16)
-        between(n4).start()
+        own_line(n4, 0).wait_recv()
+        ends[lax.rem(n4, RING_LINE)] = (mine[lax.rem(n4, RING_LINE)].astype(F32) + ends[lax.rem(n4, RING_LINE)].astype(F32)).astype(BF16)
+        own_line(n4, 1).start()
 
     @pl.when((n4 >= 0) & (n4 < blocks) & jnp.logical_not(inner))
     def _():
-        inwards(n4).wait_send()
+        own_line(n4, 0).wait_send()
 
     n3 = step - LAGS[2]
 
@@ -711,19 +968,19 @@
         @pl.when(n3 % 2 == 0)
         def _():
             wait(to_side(n3, s2y, r2y))
-            mine[n3] = (total + r2y[n3 // 2].astype(F32)).astype(BF16)
+            mine[lax.rem(n3, RING_LINE)] = (total + r2y[half(n3)].astype(F32)).astype(BF16)
 
         @pl.when(n3 % 2 == 1)
         def _():
             wait(to_seq(n3, s2x, r2x))
             added = total
             for hop in range(seqs - 1):
-                added = added + r2x[n3 // 2, hop].astype(F32)
-            mine[n3] = added.astype(BF16)
+                added = added + r2x[half(n3), hop].astype(F32)
+            mine[lax.rem(n3, RING_LINE)] = added.astype(BF16)
 
         @pl.when(jnp.logical_not(inner))
         def _():
-            inwards(n3).start()
+            own_line(n3, 0).start()
 
     n2 = step - LAGS[1]
 
@@ -732,18 +989,18 @@
         wait(to_seq(n2, s1x, r1x))
         total = kept1x[...]
         for hop in range(seqs - 1):
-            total = total + r1x[n2 // 2, hop].astype(F32)
+            total = total + r1x[half(n2), hop].astype(F32)
         kept1x[...] = total
-        s2y[n2 // 2] = kept1x[rows(1 - side, 1), :].astype(BF16)
+        s2y[half(n2)] = kept1x[rows(1 - side, 1), :].astype(BF16)
         start(to_side(n2, s2y, r2y))
         kept2[0] = kept1x[rows(side, 1), :]
 
     @pl.when((n2 >= 0) & (n2 < blocks) & (n2 % 2 == 1))
     def _():
         wait(to_side(n2, s1y, r1y))
-        kept1y[...] = kept1y[...] + r1y[n2 // 2].astype(F32)
+        kept1y[...] = kept1y[...] + r1y[half(n2)].astype(F32)
         for hop, peer in enumerate(seq_peers):
-            s2x[n2 // 2, hop] = kept1y[rows(peer, 1), :].astype(BF16)
+            s2x[half(n2), hop] = kept1y[rows(peer, 1), :].astype(BF16)
         start(to_seq(n2, s2x, r2x))
         kept2[1] = kept1y[rows(seq, 1), :]
 
@@ -753,19 +1010,19 @@
     def _():
         wait(to_mate(n1))
         held = n1 % 2
-        kept0[held] = kept0[held] + r0[n1].astype(F32)
+        kept0[held] = kept0[held] + r0[lax.rem(n1, RING)].astype(F32)
 
         @pl.when(n1 % 2 == 0)
         def _():
             for hop, peer in enumerate(seq_peers):
-                s1x[n1 // 2, hop] = kept0[held, rows(2 * peer, 2), :].astype(BF16)
+                s1x[half(n1), hop] = kept0[held, rows(2 * peer, 2), :].astype(BF16)
             start(to_seq(n1, s1x, r1x))
             kept1x[...] = kept0[held, rows(2 * seq, 2), :]
 
         @pl.when(n1 % 2 == 1)
         def _():
             for place in range(seqs):
-                s1y[n1 // 2, place * share : (place + 1) * share, :] = kept0[held, rows(2 * place + 1 - side, 1), :].astype(BF16)
+                s1y[half(n1), place * share : (place + 1) * share, :] = kept0[held, rows(2 * place + 1 - side, 1), :].astype(BF16)
             start(to_side(n1, s1y, r1y))
             for place in range(seqs):
                 kept1y[place * share : (place + 1) * share, :] = kept0[held, rows(2 * place + side, 1), :]
@@ -775,38 +1032,50 @@
     return right_ref.shape[1] // three_ref.shape[1]
 
 
-def close(h1t, slopes, weight, x, dr, gain, seqs, dps, reps):
+def close(h2t, mixed_t, h1t, rest, rest_edge, slopes, weight, x, dr, gain, early, down, seqs, dps, reps):
     assert (dps, reps) == (4, 4)
     width, tokens = h1t.shape
     share = width // (seqs * dps)
-    blocks = 3 * width // CUT
+    rest_blocks = rest.shape[1] // CUT - EARLY
+    rest_edge = rest_edge - EARLY * CUT
+    blocks_of = lambda array, count: (count, array.shape[0], array.shape[1] // count)
+    blocks = rest_blocks + 3 * width // CUT
     halves = width // CUT
     token_blocks = tokens // TILE
-    steps = max(blocks + token_blocks, blocks + LAGS[5])
+    steps = max(blocks + token_blocks, blocks + LAGS[5], DOWN_BLOCKS + EARLY + 3 * LINE_LAG)
     late = lambda s: jnp.clip(s - blocks, 0, token_blocks - 1)
-    early = lambda s: jnp.minimum(s, blocks - 1)
+    turn_of = lambda s: jnp.clip(s - rest_blocks, 0, blocks - rest_blocks - 1)
     fixed = lambda m, n: pl.BlockSpec((m, n), lambda s: (0, 0), pipeline_mode=pl.Buffered(1))
     row = pl.BlockSpec((TILE, width), lambda s: (late(s), 0))
-    pairs = (blocks + 1) // 2
     half_rows = 2 * seqs * share
     buffers = lambda *shape: [pltpu.VMEM(shape + (CUT,), BF16)] * 2
     slots = seqs + 4
     return pl.pallas_call(
-        functools.partial(close_kernel, blocks, seqs, reps),
+        functools.partial(close_kernel, blocks, rest_blocks, rest_edge, seqs, reps),
         grid=(steps,),
         in_specs=[
             fixed(width, tokens),
-            pl.BlockSpec((1, tokens, CUT), lambda s: (early(s) // halves, 0, early(s) % halves)),
+            fixed(width, tokens),
+            fixed(width, tokens),
+            pl.BlockSpec((tokens, CUT), lambda s: (0, EARLY + jnp.minimum(s, rest_blocks - 1))),
+            pl.BlockSpec((1, tokens, CUT), lambda s: (turn_of(s) // halves, 0, turn_of(s) % halves)),
             pl.BlockSpec((3, TILE, width), lambda s: (0, late(s), 0)),
             fixed(*weight.shape),
             row,
             row,
             fixed(1, width),
+            fixed(*early.shape),
+            fixed(*down.shape),
         ],
-        out_specs=[row, fixed(share, 3 * width)],
+        out_specs=[
+            row, fixed(share, rest_blocks * CUT), fixed(share, 3 * width), fixed(*early.shape), fixed(*down.shape),
+        ],
         out_shape=[
             jax.ShapeDtypeStruct((tokens, width), F32),
-            jax.ShapeDtypeStruct((share, 3 * width), F32),
+            jax.ShapeDtypeStruct((share, rest_blocks * CUT), BF16),
+            jax.ShapeDtypeStruct((share, 3 * width), BF16),
+            jax.ShapeDtypeStruct(early.shape, BF16),
+            jax.ShapeDtypeStruct(down.shape, BF16),
         ],
         scratch_shapes=[
             pltpu.VMEM((width, CUT), F32),
@@ -814,29 +1083,34 @@
             pltpu.VMEM((2 * share, CUT), F32),
             pltpu.VMEM((seqs * share, CUT), F32),
             pltpu.VMEM((2, share, CUT), F32),
-            *buffers(blocks, half_rows),
-            *buffers(pairs, seqs - 1, 2 * share),
-            *buffers(pairs, seqs * share),
-            *buffers(pairs, seqs - 1, share),
-            *buffers(pairs, share),
-            *[pltpu.VMEM((blocks, share, CUT), BF16)] * 5,
-            pltpu.SemaphoreType.DMA((blocks, slots)),
-            pltpu.SemaphoreType.DMA((blocks, slots)),
+            *buffers(RING, half_rows),
+            *buffers(RING_XY, seqs - 1, 2 * share),
+            *buffers(RING_XY, seqs * share),
+            *buffers(RING_XY, seqs - 1, share),
+            *buffers(RING_XY, share),
+            *[pltpu.VMEM((RING_LINE, share, CUT), BF16)] * 3,
+            *[pltpu.VMEM(blocks_of(early, EARLY), BF16)] * 2,
+            *[pltpu.VMEM(blocks_of(down, DOWN_BLOCKS), BF16)] * 2,
+            pltpu.SemaphoreType.DMA((max(2 * RING_XY, RING_LINE), slots)),
+            pltpu.SemaphoreType.DMA((max(2 * RING_XY, RING_LINE), slots)),
+            pltpu.SemaphoreType.DMA((2, EARLY + DOWN_BLOCKS, 3)),
         ],
         compiler_params=params(collective_id=1, has_side_effects=True),
         cost_estimate=pl.CostEstimate(
-            flops=4 * tokens * width * 3 * width, bytes_accessed=48 * 1024 * 1024, transcendentals=0
+            flops=2 * tokens * width * (6 * width + rest.shape[1]), bytes_accessed=48 * 1024 * 1024, transcendentals=0
         ),
         name="close",
-    )(h1t, slopes, slopes, weight, x, dr, gain)
-
-
-def neighbours(block, axis, along):
+    )(h2t, mixed_t, h1t, rest, slopes, slopes, weight, x, dr, gain, early, down)
+
+
+def neighbours(block, axis, along, after=None):
     count = lax.axis_size(axis)
     rows = block.shape[along]
     if count == 2:
         start = (1 - lax.axis_index(axis)) * (rows - HALF)
         facing = lax.dynamic_slice_in_dim(block, start, HALF, along)
+        if after is not None:
+            facing, _ = lax.optimization_barrier((facing, after))
         return lax.ppermute(facing, axis, [(0, 1), (1, 0)])
     step = min(rows, HALF)
     head = lax.slice_in_dim(block, 0, step, axis=along)
@@ -904,11 +1178,11 @@
 
     share = attn_gain.shape[0]
     shards = width // share
-    x_halo = neighbours(x, "seq", 1)
     gather = lambda shard: lax.all_gather(shard, group, axis=0, tiled=True)
     gain_rows = jnp.pad(jnp.stack([attn_gain, mlp_gain]), ((0, share - 2), (0, LANES - share)))
     qkv_full = gather(jnp.concatenate([w_qkv, gain_rows], axis=1))
     blank = jnp.zeros((share, FF_PAD - FF), BF16)
+    x_halo = neighbours(x, "seq", 1, qkv_full)
     rest_full = gather(jnp.concatenate([w_in[:, :FF], blank, w_in[:, FF:], blank, w_out], axis=1))
     down_full = gather(w_down)
     gains = qkv_full[:, 3 * width : 3 * width + share].reshape(shards, share, share).astype(F32)
@@ -921,43 +1195,34 @@
     h1t, qkv = project(x, qkv_full, cosines, sines, 0, None, extent, shards)
     qkv = project(x_halo, qkv_full, cosines, sines, stretch // TILE, qkv, extent, shards)
     mixed, mixed_t, lse = attend(own, lows, highs, qkv, marks_k, marks_q, stretch)
-    result, h2t, hidt, slopes, dr, do, delta = feed(x, mixed, seeds, gain_two, rest_full, down_full)
-    stats = jnp.concatenate([lse, delta], axis=2)
-    do_halo = neighbours(do, "seq", 1)
-    stats_halo = neighbours(stats, "seq", 3)
-
-    scatter = lambda part: lax.psum_scatter(part, group, scatter_dimension=0, tiled=True)
+    lse_halo = neighbours(lse, "seq", 3)
+    result, h2t, hidt, slopes, dr, do, delta, do_halo, delta_halo = feed(
+        x, mixed, seeds, gain_two, rest_full, down_full, seq_count, halo
+    )
+
     tokens = batch * stretch
-    columns = rest_full.shape[1]
-    flat = slopes.reshape(tokens, columns)
-    step = FF_PAD * 2 // 7
-    part_rest = weigh(
-        h2t, flat, "weigh_in", (width, tokens), (tokens, step), (width, step),
-        lambda n: (0, 0), lambda n: (0, n), lambda n: (0, n), 7, (width, columns),
-    )
-    first = FF_PAD * 2 // TILE
-    part_rest = weigh(
-        mixed_t, flat, "weigh_out", (width, tokens), (tokens, TILE), (width, TILE),
-        lambda n: (0, 0), lambda n: (0, n + first), lambda n: (0, n + first), width // TILE, (width, columns), part_rest,
-    )
-    shard_rest = scatter(part_rest)
-    do_halo, stats_halo, hidt = lax.optimization_barrier((do_halo, stats_halo, hidt))
-    step = FF // 4
+    dps = lax.axis_size("dp")
+    pairs = [list(range(core, seq_count * dps, 2)) for core in range(2)]
+    scatter = lambda part: lax.psum_scatter(part, group, scatter_dimension=0, tiled=True, axis_index_groups=pairs)
+    slopes = slopes.reshape(tokens, -1)
     part_down = weigh(
-        hidt, seeds.reshape(tokens, width), "weigh_down", (step, tokens), (tokens, width), (step, width),
-        lambda n: (n, 0), lambda n: (0, 0), lambda n: (n, 0), 4, (FF, width),
+        [hidt], seeds.reshape(tokens, width), TILE, width // TILE, ((0, width // TILE, ((0, TILE),)),),
+        w_down.shape[0], "weigh_down", 3,
     )
     shard_down = scatter(part_down)
-    do_halo, stats_halo, part_down, part_rest = lax.optimization_barrier((do_halo, stats_halo, part_down, part_rest))
-    rest_sum, down_sum = lax.psum((shard_rest, shard_down), "rep")
+    slopes, part_down = lax.optimization_barrier((slopes, part_down))
+    part_early = weigh([h2t], slopes, CUT, EARLY, ((0, EARLY, ((0, CUT),)),), share, "weigh_early", 4)
+    shard_early = scatter(part_early)
+    do_halo, part_early = lax.optimization_barrier((do_halo, part_early))
     slopes_qkv = attend_back(
-        own, lows, highs, qkv, do, do_halo, stats, stats_halo, marks_k, marks_q, cosines, sines
+        own, lows, highs, qkv, do, do_halo, lse, lse_halo, delta, delta_halo, marks_k, marks_q, cosines, sines
     )
-    grad_x, grad_qkv = close(
-        h1t, slopes_qkv.reshape(3, tokens, width), qkv_full, x.reshape(tokens, width), dr.reshape(tokens, width),
-        gain_one, seq_count, lax.axis_size("dp"), lax.axis_size("rep"),
+    grad_x, late_sum, grad_qkv, early_sum, down_sum = close(
+        h2t, mixed_t, h1t, slopes, 2 * FF_PAD, slopes_qkv.reshape(3, tokens, width), qkv_full, x.reshape(tokens, width), dr.reshape(tokens, width),
+        gain_one, shard_early, shard_down, seq_count, dps, lax.axis_size("rep"),
     )
-    rest_sum = rest_sum.astype(F32)
+    grad_qkv = grad_qkv.astype(F32)
+    rest_sum = jnp.concatenate([early_sum, late_sum], axis=1).astype(F32)
     grad_in = jnp.concatenate([rest_sum[:, :FF], rest_sum[:, FF_PAD : FF_PAD + FF]], axis=1)
     grad_attn_gain = jnp.sum(grad_qkv * w_qkv.astype(F32), axis=1) / attn_gain.astype(F32)
     grad_mlp_gain = jnp.sum(grad_in * w_in.astype(F32), axis=1) / mlp_gain.astype(F32)
@@ -967,9 +1232,9 @@
         grad_attn_gain,
         grad_mlp_gain,
         grad_qkv,
-        rest_sum[:, 2 * FF_PAD :],
+        rest_sum[:, 2 * FF_PAD : 2 * FF_PAD + width],
         grad_in,
-        down_sum.astype(F32),
+        down_sum[: w_down.shape[0]].astype(F32),
     )
 
 

time: 673 us -> 616 us (0.915)
  waiting for transfers between devices: 167 us -> 89.9 us
  Pallas kernels: 442 us -> 468 us
    all_gather x3, waiting for transfers between devices: 88 us -> 46.3 us  [body(): gather = lambda shard: lax.all_gather(shard, group, axis=0, tiled=True)]
    pallas_call x5 -> x4, Pallas kernels: 247 us -> 278 us  [the longest x1 121 us: close(): pl.pallas_call(functools.partial(close_kernel, blocks, rest_blocks, rest_...]
    psum x1 -> x0, waiting for transfers between devices: 21.1 us -> none  [body(): rest_sum, down_sum = lax.psum((shard_rest, shard_down), 'rep')]
    reduce_scatter x2, waiting for transfers between devices: 8.51 us -> 0.04 us  [body(): lax.psum_scatter(part, group, scatter_dimension=0, tiled=True, axis_index...]
    ppermute x3 -> x2, waiting for transfers between devices: 48.4 us -> 42.9 us  [neighbours(): return lax.ppermute(facing, axis, [(0, 1), (1, 0)])]
  transfers between devices with their start and end apart: 9 -> 7, of which waited for: 5 -> 4; matrix products, arithmetic and copies ran while one was open for 3% -> 3% of each run, Pallas kernels for 48% -> 35%
where the time goes in v2:
time: 616 us; the launch traced here: 613 us
  Pallas kernels  468 us (76%)
  waiting for transfers between devices  89.9 us (15%)
  other arithmetic  21.3 us (3%)
  local copies, waits for them, and re-layouts  16.9 us (3%)
  between operations  14.3 us (2%)
    pallas_call x1, Pallas kernels, close(): pl.pallas_call(functools.partial(close_kernel, blocks, rest_blocks, rest_...  121 us
    pallas_call x1, Pallas kernels, feed(): pl.pallas_call(functools.partial(feed_kernel, seqs, halo // TILE), grid=(...  110 us
    pallas_call x1, Pallas kernels, attend_back(): pl.pallas_call(functools.partial(attend_back_kernel, tiles, wide), grid_s...  106 us
    pallas_call x1, Pallas kernels, attend(): pl.pallas_call(functools.partial(attend_kernel, tiles, wide), grid_spec=p...  50.4 us
    pallas_call x2, Pallas kernels, weigh(): pl.pallas_call(functools.partial(weigh_kernel, blocks, share, held, turns...  46.9 us
    all_gather x3, waiting for transfers between devices, body(): gather = lambda shard: lax.all_gather(shard, group, axis=0, tiled=True)  46.3 us
    ppermute x2, waiting for transfers between devices, neighbours(): return lax.ppermute(facing, axis, [(0, 1), (1, 0)])  42.9 us
    pallas_call x1, Pallas kernels, project(): pl.pallas_call(functools.partial(project_kernel, True, shards), grid=grid...  21.5 us
  transfers between devices with their start and end apart: 7, of which 4 were waited for; matrix products, arithmetic and copies ran while one was open for 3% of the time, Pallas kernels for 35%

profile of v2, /device:TPU:0, one launch (start us, length us, event | category | flops | bytes accessed | tf_op | source)
XLA Modules:
  0.0 612.7 jit_solution(7767710274704530458)
XLA Ops:
  7.2 0.0 copy-start
  7.2 0.0 all-gather.4.cloned.1.call-start
  7.2 0.8 fusion.7
  8.0 2.1 pad_maximum_fusion.1
  10.1 0.0 all-gather.4.cloned.1.call-update
  10.1 0.0 all-gather.8.cloned.1.call-start
  10.2 0.7 all-gather.8.cloned.1.call-update
  10.9 0.0 all-gather.6.cloned.1.call-start
  10.9 0.0 copy-done
  10.9 0.3 fusion.18
  11.2 0.0 copy-start.11
  11.2 2.0 concatenate.17
  13.2 0.0 all-gather.6.cloned.1.call-update
  13.2 0.0 reduce-scatter.5.cloned.1.call-start
  13.3 0.1 slice.33
  13.4 0.1 slice.34
  13.7 0.3 fusion.3
  14.0 0.1 fusion.8
  14.1 0.1 fusion.9
  14.2 0.1 fusion.4
  14.3 3.1 dynamic-slice_bitcast_fusion
  17.4 0.6 and_select_fusion.4
  18.0 0.9 select_convert_fusion.1.eq_ref
  18.9 1.3 select_convert_fusion.ek_ref
  20.3 39.6 %all-gather.4.cloned.1.call-done.w_ref = bf16[1024,3200]{1,0:T(8,128)(2,1)} async-done(((bf16[128,3200]{1,0:T(8,128)(2,1)}), bf16[1024,3200]{1,0:T(8,128)(2,1)}) %all-gather.4.cloned.1.call-update) | async-done | bytes 6553616 | tf_op jit(solution)/shard_map/all_gather | solution.py:1181
  59.8 1.5 collective-permute-start
  61.3 7.0 %fusion = (f32[2,1536,128]{2,1,0:T(8,128)}, f32[2,1536,128]{2,1,0:T(8,128)}) fusion(f32[128]{0:T(128)S(1)} %get-tuple-element.82, f32[128]{0:T(128)S(1)} %get-tuple-element.83, f32[2,1536]{1,0:T(2,128)S(1)} %subtract_convert_fusion), kind=kLoop, calls=%fused_computation.6 | loop fusion | flops 786432 | bytes 3159040 | tf_op jit(solution)/shard_map/mul | solution.py:1148
  68.3 0.6 slice_bitcast_fusion
  69.0 21.5 %project_own.1 = (bf16[1024,2048]{1,0:T(8,128)(2,1)}, bf16[2,1536,3072]{2,1,0:T(8,128)(2,1)}) custom-call(bf16[2,1024,1024]{2,1,0:T(8,128)(2,1)} %bitcast.34, bf16[1024,3200]{1,0:T(8,128)(2,1)} %all-gather.4.cloned.1.call-done.w_ref, f32[2,1536,128]{2,1,0:T(8,128)} %get-tuple-element.81.cos_ref, f32[2,1536,128]{2,1,0:T(8,128)} %get-tuple-element.80.sin_ref), custom_call_target="tpu_custom_call" | custom-call | flops 12884901888 | bytes 23068672 | tf_op jit(solution)/shard_map/project_own/pallas_call | solution.py:111
  90.5 38.9 %collective-permute-done.x_ref = bf16[2,512,1024]{2,1,0:T(8,128)(2,1)S(1)} collective-permute-done((bf16[2,512,1024]{2,1,0:T(8,128)(2,1)}, bf16[2,512,1024]{2,1,0:T(8,128)(2,1)S(1)}, u32[]{:S(2)}, u32[]{:S(2)}) %collective-permute-start) | collective-permute-done | bytes 2097184 | tf_op jit(solution)/shard_map/ppermute | solution.py:1114
  129.4 1.3 copy-done.6
  130.8 13.2 %project_halo.1.q_ref.k_ref.v_ref = bf16[2,1536,3072]{2,1,0:T(8,128)(2,1)} custom-call(bf16[2,512,1024]{2,1,0:T(8,128)(2,1)} %copy-done.6, bf16[1024,3200]{1,0:T(8,128)(2,1)} %all-gather.4.cloned.1.call-done.w_ref, f32[2,1536,128]{2,1,0:T(8,128)} %get-tuple-element.81.cos_ref, ...), custom_call_target="tpu_custom_call", output_to_operand_aliasing={{}: (4, {})} | custom-call | flops 6442450944 | bytes 14680064 | tf_op jit(solution)/shard_map/project_halo/pallas_call | solution.py:125
  143.9 50.4 %attend.1 = (bf16[2,1024,1024]{2,1,0:T(8,128)(2,1)}, bf16[1024,2048]{1,0:T(8,128)(2,1)}, f32[2,8,2,1024]{3,2,1,0:T(2,128)}) custom-call(s32[1]{0:T(128)} %bitcast.1.own_ref, s32[2,8]{1,0:T(2,128)} %get-tuple-element.84.lo_ref, s32[2,8]{1,0:T(2,128)} %get-tuple-element.85.hi_ref, bf16[2,1536,3072]{2,1,0:T(8,128)(2,1)} %project_halo.1.q_ref.k_ref.v_ref, ...), custom_call_target="tpu_custom_call" | custom-call | flops 25769803776 | bytes 33554432 | tf_op jit(solution)/shard_map/attend/pallas_call | solution.py:257
  194.3 0.0 all-gather.8.cloned.1.call-done.wd_ref
  194.3 6.7 %all-gather.6.cloned.1.call-done.w_ref = bf16[1024,6400]{1,0:T(8,128)(2,1)} async-done(((bf16[128,6400]{1,0:T(8,128)(2,1)}), bf16[1024,6400]{1,0:T(8,128)(2,1)}) %all-gather.6.cloned.1.call-update) | async-done | bytes 13107216 | tf_op jit(solution)/shard_map/all_gather | solution.py:1181
  201.0 109.7 %feed.1 = (bf16[2,1024,1024]{2,1,0:T(8,128)(2,1)}, bf16[1024,2048]{1,0:T(8,128)(2,1)}, bf16[2624,2048]{1,0:T(8,128)(2,1)}, bf16[2,1024,6656]{2,1,0:T(8,128)(2,1)...) custom-call(bf16[2,1024,1024]{2,1,0:T(8,128)(2,1)} %bitcast.35, ...), custom_call_target="tpu_custom_call" | custom-call | flops 74625056768 | bytes 67108864 | tf_op jit(solution)/shard_map/feed/pallas_call | solution.py:631
  310.7 20.6 %weigh_down.1 = bf16[1344,1024]{1,0:T(8,128)(2,1)} custom-call(bf16[2624,2048]{1,0:T(8,128)(2,1)} %get-tuple-element.38.refs_0_, bf16[2048,1024]{1,0:T(8,128)(2,1)} %bitcast.45), custom_call_target="tpu_custom_call" | custom-call | flops 11005853696 | bytes 25165824 | tf_op jit(solution)/shard_map/weigh_down/pallas_call | solution.py:726
  331.3 0.0 reduce-scatter.5.cloned.1.call-update
  331.3 0.0 reduce-scatter.3.cloned.1.call-start
  331.4 26.4 %weigh_early.1 = bf16[512,4096]{1,0:T(8,128)(2,1)} custom-call(bf16[1024,2048]{1,0:T(8,128)(2,1)} %get-tuple-element.34.refs_0_.h2t_ref, bf16[2048,6656]{1,0:T(8,128)(2,1)} %bitcast.46), custom_call_target="tpu_custom_call" | custom-call | flops 17179869184 | bytes 25165824 | tf_op jit(solution)/shard_map/weigh_early/pallas_call | solution.py:726
  357.7 0.0 copy-start.10
  357.8 0.0 reduce-scatter.3.cloned.1.call-update
  357.8 0.9 copy-done.10
  358.7 0.5 collective-permute-start.1
  359.2 3.9 collective-permute-done.1.lseh_ref
  363.1 0.6 copy-done.14
  363.7 105.5 %attend_back.1 = bf16[3,2,1024,1024]{3,2,1,0:T(8,128)(2,1)} custom-call(s32[1]{0:T(128)} %bitcast.1.own_ref, s32[2,8]{1,0:T(2,128)} %get-tuple-element.84.lo_ref, s32[2,8]{1,0:T(2,128)} %get-tuple-element.85.hi_ref, bf16[2,1536,3072]{2,1,0:T(8,128)(2,1)} %project_halo.1.q_ref.k_ref.v_ref, bf16[2,1536,3072]{2,1,0:T(8,128)(2,1)} %project_halo.1.q_ref.k_ref.v_ref, ...), custom_call_target="tpu_custom_call" | custom-call | flops 64424509440 | bytes 67108864 | tf_op jit(solution)/shard_map/attend_back/pallas_call | solution.py:431
  469.2 0.0 reduce-scatter.5.cloned.1.call-done.down_ref
  469.3 0.0 reduce-scatter.3.cloned.1.call-done.early_ref
  469.3 120.9 %close.1 = (f32[2048,1024]{1,0:T(8,128)}, bf16[128,2560]{1,0:T(8,128)(2,1)}, bf16[128,3072]{1,0:T(8,128)(2,1)}, bf16[128,4096]{1,0:T(8,128)(2,1)}, bf16[336,1024]{1,0:T(8,128)(2,1)}) custom-call(bf16[1024,2048]{1,0:T(8,128)(2,1)} %get-tuple-element.34.refs_0_.h2t_ref, bf16[1024,2048]{1,0:T(8,128)(2,1)} %get-tuple-element.35.ot_ref, ...), custom_call_target="tpu_custom_call" | custom-call | flops 53687091200 | bytes 50331648 | tf_op jit(solution)/shard_map/close/pallas_call | solution.py:1053
  590.2 1.9 maximum_convert_fusion.1
  592.1 0.3 maximum_convert_fusion
  592.5 0.0 copy-start.1
  592.5 0.2 fusion.17
  592.7 1.1 copy-done.1
  593.8 2.0 multiply_reduce_fusion
  595.9 0.5 convert_divide_fusion
  596.4 1.4 multiply_reduce_fusion.1
  597.7 0.5 convert_divide_fusion.1
  598.3 1.2 slice_convert_fusion
  599.5 0.2 copy-done.3
  599.7 2.1 copy.31
  601.8 0.8 slice-done.1
  602.6 3.4 copy.32
  (43 shorter events, 0.2 us)
Async XLA Ops:
  7.2 3.7 copy-start
  7.2 52.7 %all-gather.4.cloned.1.call-start = ((), (), s32[]{:S(2)}) async-start(), calls=%async_computation.2 | async-start | bytes 7372800 | tf_op jit(solution)/shard_map/all_gather | solution.py:1181
  10.1 1.1 copy-start.9
  10.1 184.2 %all-gather.8.cloned.1.call-start = ((), (), s32[]{:S(2)}) async-start(), calls=%async_computation.4 | async-start | bytes 6045696 | tf_op jit(solution)/shard_map/all_gather | solution.py:1181
  10.9 190.1 %all-gather.6.cloned.1.call-start = ((), (), s32[]{:S(2)}) async-start(), calls=%async_computation.3 | async-start | bytes 14745600 | tf_op jit(solution)/shard_map/all_gather | solution.py:1181
  11.2 2.1 copy-start.11
  13.2 456.0 %reduce-scatter.5.cloned.1.call-start = ((), (), s32[]{:S(2)}) async-start(), calls=%async_computation.6 | async-start | bytes 3440640 | tf_op jit(solution)/shard_map/reduce_scatter | solution.py:1206
  59.8 8.5 %slice-start.2 = ((bf16[1024,3200]{1,0:T(8,128)(2,1)}), bf16[1024,128]{1,0:T(8,128)(2,1)S(1)}, s32[]{:S(2)}) async-start(bf16[1024,3200]{1,0:T(8,128)(2,1)} %all-gather.4.cloned.1.call-done.w_ref), calls=%async_computation.9 | async-start | bytes 524288 | tf_op jit(solution)/shard_map/slice | solution.py:1188
  59.8 69.6 %collective-permute-start = (bf16[2,512,1024]{2,1,0:T(8,128)(2,1)}, bf16[2,512,1024]{2,1,0:T(8,128)(2,1)S(1)}, u32[]{:S(2)}, u32[]{:S(2)}) collective-permute-start(bf16[2,512,1024]{2,1,0:T(8,128)(2,1)} %dynamic-slice_bitcast_fusion), channel_id=1, source_target_pairs={{0,16},{16,0},{1,17},{17,1},{2,18},{18,2},{3,19},{19,3},{4,20},{20... | collective-permute-start | bytes 6291464 | tf_op jit(solution)/shard_map/ppermute | solution.py:1114
  129.4 1.3 copy-start.6
  331.3 137.9 %reduce-scatter.3.cloned.1.call-start = ((), (), s32[]{:S(2)}) async-start(), calls=%async_computation.5 | async-start | bytes 5242880 | tf_op jit(solution)/shard_map/reduce_scatter | solution.py:1206
  357.7 0.9 copy-start.10
  358.7 4.4 collective-permute-start.1
  363.1 0.6 copy-start.14
  590.2 1.9 copy-start.2
  590.2 1.9 copy-start.5
  592.5 1.3 copy-start.1
  593.8 2.1 copy-start.12
  593.8 2.6 copy-start.4
  593.8 2.6 copy-start.7
  593.8 8.0 %slice-start = ((s8[8388608]{0:T(1024)(128)(4,1)}), s8[4194304]{0:T(1024)(128)(4,1)S(1)}, s32[]{:S(2)}) async-start(s8[8388608]{0:T(1024)(128)(4,1)} %bitcast.29), calls=%async_computation.7 | async-start | bytes 8388608
  595.8 1.9 copy-start.13
  595.8 2.4 copy-start.8
  596.4 3.3 copy-start.3
  598.3 4.3 slice-start.1
Sparse Core Ops, SparseCore 0:
  10.5 49.3 all-gather.3
  61.7 62.9 all-gather.7
  126.6 74.3 all-gather.5
  331.5 40.0 reduce-scatter.4
  374.4 52.6 reduce-scatter.2

commit v3 on v2

--- a/solution.py
+++ b/solution.py
@@ -291,16 +291,16 @@
     )(own, lows, highs, qkv, qkv, qkv, marks_k, marks_q)
 
 
-def attend_back_kernel(tiles, wide, own_ref, lo_ref, hi_ref, q_ref, k_ref, v_ref, do_ref, doh_ref, lse_ref, lseh_ref,
-                       delta_ref, deltah_ref, ek_ref, eq_ref, cos_ref, sin_ref, out_ref,
-                       kx, vx, qx, dx, dn, kt, dqt, edges):
-    batch = pl.program_id(0)
+def attend_back_kernel(tiles, wide, first_batch, own_ref, lo_ref, hi_ref, q_ref, k_ref, v_ref, do_ref, doh_ref, lse_ref, lseh_ref,
+                       delta_ref, deltah_ref, ek_ref, eq_ref, cos_ref, sin_ref, *refs):
+    out_ref, kx, vx, qx, dx, dn, kt, dqt, edges = refs[-9:]
+    batch = pl.program_id(0) + first_batch
     extent = k_ref.shape[1]
     stretch = do_ref.shape[1]
     mine = stretch // TILE
     heads = 2 * wide
 
-    @pl.when((batch == 0) & (pl.program_id(1) == 0))
+    @pl.when((pl.program_id(0) == 0) & (pl.program_id(1) == 0))
     def _():
         before, after = edge_masks()
         edges[0] = before
@@ -418,21 +418,21 @@
 
 
 def attend_back(own, lows, highs, qkv, grads, grads_halo, lse, lse_halo, delta, delta_halo, marks_k, marks_q,
-                cosines, sines):
+                cosines, sines, first_batch, count, held):
     batch, extent, _ = qkv.shape
     stretch, width = grads.shape[1:]
     halo = extent - stretch
     tiles = extent // TILE
     wide = WIDE_BACK
     groups = PAIRS // wide
-    spec = lambda rows, offset: pl.BlockSpec((1, rows, wide * LANES), lambda b, p, *_: (b, 0, p + offset))
-    per = lambda rows: pl.BlockSpec((1, rows, LANES), lambda b, p, *_: (b, 0, 0))
-    numbers = lambda rows: pl.BlockSpec((1, wide, 2, rows), lambda b, p, *_: (b, p, 0, 0))
+    spec = lambda rows, offset: pl.BlockSpec((1, rows, wide * LANES), lambda b, p, *_: (b + first_batch, 0, p + offset))
+    per = lambda rows: pl.BlockSpec((1, rows, LANES), lambda b, p, *_: (b + first_batch, 0, 0))
+    numbers = lambda rows: pl.BlockSpec((1, wide, 2, rows), lambda b, p, *_: (b + first_batch, p, 0, 0))
     return pl.pallas_call(
-        functools.partial(attend_back_kernel, tiles, wide),
+        functools.partial(attend_back_kernel, tiles, wide, first_batch),
         grid_spec=pltpu.PrefetchScalarGridSpec(
             num_scalar_prefetch=3,
-            grid=(batch, groups),
+            grid=(count, groups),
             in_specs=[
                 spec(extent, 0),
                 spec(extent, groups),
@@ -444,11 +444,12 @@
                 numbers(stretch),
                 numbers(halo),
                 per(extent),
-                pl.BlockSpec((1, HEAD_DIM, extent), lambda b, p, *_: (b, 0, 0)),
+                pl.BlockSpec((1, HEAD_DIM, extent), lambda b, p, *_: (b + first_batch, 0, 0)),
                 per(stretch),
                 per(stretch),
-            ],
-            out_specs=pl.BlockSpec((3, 1, stretch, wide * LANES), lambda b, p, *_: (0, b, 0, p)),
+            ]
+            + ([] if held is None else [pl.BlockSpec(memory_space=pl.ANY)]),
+            out_specs=pl.BlockSpec((3, 1, stretch, wide * LANES), lambda b, p, *_: (0, b + first_batch, 0, p)),
             scratch_shapes=[
                 pltpu.VMEM((2 * wide, extent, LANES), BF16),
                 pltpu.VMEM((2 * wide, extent, LANES), BF16),
@@ -460,14 +461,15 @@
                 pltpu.VMEM((3, TILE, TILE), F32),
             ],
         ),
+        input_output_aliases={} if held is None else {16: 0},
         out_shape=jax.ShapeDtypeStruct((3, batch, stretch, width), BF16),
         compiler_params=params(),
         cost_estimate=pl.CostEstimate(
-            flops=5 * 2 * HEADS * batch * stretch * extent * 128, bytes_accessed=64 * 1024 * 1024, transcendentals=0
+            flops=5 * 2 * HEADS * count * stretch * extent * 128, bytes_accessed=64 * 1024 * 1024, transcendentals=0
         ),
         name="attend_back",
     )(own, lows, highs, qkv, qkv, qkv, grads, grads_halo, lse, lse_halo, delta, delta_halo, marks_k, marks_q,
-      cosines, sines)
+      cosines, sines, *([] if held is None else [held]))
 
 
 def feed_kernel(seqs, halo_tiles, x_ref, o_ref, g_ref, gain_ref, w_ref, wd_ref,
@@ -747,13 +749,12 @@
 
 LAGS = (1, 3, 5, 6, 7, 8)
 RING, RING_XY, RING_LINE = 5, 2, 4
-EARLY, DOWN_BLOCKS, LINE_LAG = 8, 4, 2
-
-
-def close_kernel(blocks, rest_blocks, rest_edge, seqs, reps, h2t_ref, ot_ref, h1t_ref, rest_ref, right_ref, three_ref, w_ref, x_ref, dr_ref, gain_ref, early_ref, down_ref,
-                 gi_ref, rest_sum, sum_ref, early_sum, down_sum,
+EARLY = 8
+
+
+def close_kernel(blocks, rest_blocks, rest_edge, seqs, reps, h2t_ref, ot_ref, h1t_ref, rest_ref, right_ref, three_ref, w_ref, x_ref, dr_ref, gain_ref, gi_ref, rest_sum, sum_ref,
                  prod, kept0, kept1x, kept1y, kept2, s0, r0, s1x, r1x, s1y, r1y, s2x, r2x, s2y, r2y,
-                 mine, ends, others, early_ends, early_others, down_ends, down_others, send_sem, recv_sem, line_sem):
+                 mine, ends, others, send_sem, recv_sem):
     step = pl.program_id(0)
     width = h1t_ref.shape[0]
     share = mine.shape[1]
@@ -804,20 +805,6 @@
         slot, turn = slot_in + which, lax.rem(n, RING_LINE)
         return line(which, mine.at[turn], ends.at[turn], others.at[turn], send_sem.at[turn, slot], recv_sem.at[turn, slot])
 
-    early_columns, down_columns = early_ends.shape[2], down_ends.shape[2]
-    extra = []
-    for k in range(down_ends.shape[0]):
-        extra.append((down_ref, down_ends, down_others, down_sum, k, slice(k * down_columns, (k + 1) * down_columns)))
-    for k in range(early_ends.shape[0]):
-        extra.append((early_ref, early_ends, early_others, early_sum, k, slice(k * early_columns, (k + 1) * early_columns)))
-
-    def extra_line(index, which):
-        source, first, second, _, k, columns = extra[index]
-        return line(
-            which, source.at[:, columns], first.at[k], second.at[k],
-            line_sem.at[0, index, which], line_sem.at[1, index, which],
-        )
-
     def start(copies):
         for each in copies:
             each.start()
@@ -842,11 +829,6 @@
         @pl.when(jnp.logical_not(inner))
         def _():
             pl.semaphore_wait(barrier, len(partners))
-
-    for index in range(len(extra)):
-        @pl.when((step == index) & jnp.logical_not(inner))
-        def _():
-            extra_line(index, 0).start()
 
     whole_blocks, split = rest_edge // CUT, rest_edge % CUT
 
@@ -888,34 +870,6 @@
             back = term if back is None else back + term
         unit, inverse = normed(x_ref[...].astype(F32))
         gi_ref[...] = dr_ref[...] + norm_back(back * gain_ref[...], unit, inverse)
-
-    for index, (source, first, second, total, k, columns) in enumerate(extra):
-        meet, share_out, close_out = (index + LINE_LAG * hop for hop in (1, 2, 3))
-
-        @pl.when((step == meet) & inner)
-        def _():
-            extra_line(index, 0).wait_recv()
-            first[k] = (source[:, columns].astype(F32) + first[k].astype(F32)).astype(BF16)
-            extra_line(index, 1).start()
-
-        @pl.when((step == share_out) & inner)
-        def _():
-            extra_line(index, 1).wait()
-            second[k] = (first[k].astype(F32) + second[k].astype(F32)).astype(BF16)
-            extra_line(index, 2).start()
-
-        @pl.when(step == close_out)
-        def _():
-            @pl.when(inner)
-            def _():
-                extra_line(index, 2).wait_send()
-
-            @pl.when(jnp.logical_not(inner))
-            def _():
-                extra_line(index, 0).wait_send()
-                extra_line(index, 2).wait_recv()
-
-            total[:, columns] = second[k]
 
     n6 = step - LAGS[5]
 
@@ -1032,17 +986,16 @@
     return right_ref.shape[1] // three_ref.shape[1]
 
 
-def close(h2t, mixed_t, h1t, rest, rest_edge, slopes, weight, x, dr, gain, early, down, seqs, dps, reps):
+def close(h2t, mixed_t, h1t, rest, rest_edge, slopes, weight, x, dr, gain, seqs, dps, reps):
     assert (dps, reps) == (4, 4)
     width, tokens = h1t.shape
     share = width // (seqs * dps)
     rest_blocks = rest.shape[1] // CUT - EARLY
     rest_edge = rest_edge - EARLY * CUT
-    blocks_of = lambda array, count: (count, array.shape[0], array.shape[1] // count)
     blocks = rest_blocks + 3 * width // CUT
     halves = width // CUT
     token_blocks = tokens // TILE
-    steps = max(blocks + token_blocks, blocks + LAGS[5], DOWN_BLOCKS + EARLY + 3 * LINE_LAG)
+    steps = max(blocks + token_blocks, blocks + LAGS[5])
     late = lambda s: jnp.clip(s - blocks, 0, token_blocks - 1)
     turn_of = lambda s: jnp.clip(s - rest_blocks, 0, blocks - rest_blocks - 1)
     fixed = lambda m, n: pl.BlockSpec((m, n), lambda s: (0, 0), pipeline_mode=pl.Buffered(1))
@@ -1064,18 +1017,12 @@
             row,
             row,
             fixed(1, width),
-            fixed(*early.shape),
-            fixed(*down.shape),
         ],
-        out_specs=[
-            row, fixed(share, rest_blocks * CUT), fixed(share, 3 * width), fixed(*early.shape), fixed(*down.shape),
-        ],
+        out_specs=[row, fixed(share, rest_blocks * CUT), fixed(share, 3 * width)],
         out_shape=[
             jax.ShapeDtypeStruct((tokens, width), F32),
             jax.ShapeDtypeStruct((share, rest_blocks * CUT), BF16),
             jax.ShapeDtypeStruct((share, 3 * width), BF16),
-            jax.ShapeDtypeStruct(early.shape, BF16),
-            jax.ShapeDtypeStruct(down.shape, BF16),
         ],
         scratch_shapes=[
             pltpu.VMEM((width, CUT), F32),
@@ -1089,18 +1036,15 @@
             *buffers(RING_XY, seqs - 1, share),
             *buffers(RING_XY, share),
             *[pltpu.VMEM((RING_LINE, share, CUT), BF16)] * 3,
-            *[pltpu.VMEM(blocks_of(early, EARLY), BF16)] * 2,
-            *[pltpu.VMEM(blocks_of(down, DOWN_BLOCKS), BF16)] * 2,
             pltpu.SemaphoreType.DMA((max(2 * RING_XY, RING_LINE), slots)),
             pltpu.SemaphoreType.DMA((max(2 * RING_XY, RING_LINE), slots)),
-            pltpu.SemaphoreType.DMA((2, EARLY + DOWN_BLOCKS, 3)),
         ],
         compiler_params=params(collective_id=1, has_side_effects=True),
         cost_estimate=pl.CostEstimate(
             flops=2 * tokens * width * (6 * width + rest.shape[1]), bytes_accessed=48 * 1024 * 1024, transcendentals=0
         ),
         name="close",
-    )(h2t, mixed_t, h1t, rest, slopes, slopes, weight, x, dr, gain, early, down)
+    )(h2t, mixed_t, h1t, rest, slopes, slopes, weight, x, dr, gain)
 
 
 def neighbours(block, axis, along, after=None):
@@ -1182,15 +1126,14 @@
     gain_rows = jnp.pad(jnp.stack([attn_gain, mlp_gain]), ((0, share - 2), (0, LANES - share)))
     qkv_full = gather(jnp.concatenate([w_qkv, gain_rows], axis=1))
     blank = jnp.zeros((share, FF_PAD - FF), BF16)
-    x_halo = neighbours(x, "seq", 1, qkv_full)
+    halo = HALF * (1 if seq_count == 2 else 2)
+    extent = stretch + halo
+    own, lows, highs, cosines, sines, marks_k, marks_q = survey(labels, stretch, extent, seq_index, seq_count)
+    x_halo = neighbours(x, "seq", 1, (qkv_full, cosines, sines, marks_k))
     rest_full = gather(jnp.concatenate([w_in[:, :FF], blank, w_in[:, FF:], blank, w_out], axis=1))
     down_full = gather(w_down)
     gains = qkv_full[:, 3 * width : 3 * width + share].reshape(shards, share, share).astype(F32)
     gain_one, gain_two = gains[:, 0].reshape(1, width), gains[:, 1].reshape(1, width)
-
-    halo = x_halo.shape[1]
-    extent = stretch + halo
-    own, lows, highs, cosines, sines, marks_k, marks_q = survey(labels, stretch, extent, seq_index, seq_count)
 
     h1t, qkv = project(x, qkv_full, cosines, sines, 0, None, extent, shards)
     qkv = project(x_halo, qkv_full, cosines, sines, stretch // TILE, qkv, extent, shards)
@@ -1214,12 +1157,19 @@
     part_early = weigh([h2t], slopes, CUT, EARLY, ((0, EARLY, ((0, CUT),)),), share, "weigh_early", 4)
     shard_early = scatter(part_early)
     do_halo, part_early = lax.optimization_barrier((do_halo, part_early))
-    slopes_qkv = attend_back(
-        own, lows, highs, qkv, do, do_halo, lse, lse_halo, delta, delta_halo, marks_k, marks_q, cosines, sines
-    )
-    grad_x, late_sum, grad_qkv, early_sum, down_sum = close(
+    def back(first_batch, count, held):
+        return attend_back(
+            own, lows, highs, qkv, do, do_halo, lse, lse_halo, delta, delta_halo, marks_k, marks_q, cosines, sines,
+            first_batch, count, held,
+        )
+
+    slopes_qkv = back(0, batch // 2, None)
+    slopes_qkv, shard_early, shard_down = lax.optimization_barrier((slopes_qkv, shard_early, shard_down))
+    early_sum, down_sum = lax.psum((shard_early, shard_down), "rep")
+    slopes_qkv = back(batch // 2, batch - batch // 2, slopes_qkv)
+    grad_x, late_sum, grad_qkv = close(
         h2t, mixed_t, h1t, slopes, 2 * FF_PAD, slopes_qkv.reshape(3, tokens, width), qkv_full, x.reshape(tokens, width), dr.reshape(tokens, width),
-        gain_one, shard_early, shard_down, seq_count, dps, lax.axis_size("rep"),
+        gain_one, seq_count, dps, lax.axis_size("rep"),
     )
     grad_qkv = grad_qkv.astype(F32)
     rest_sum = jnp.concatenate([early_sum, late_sum], axis=1).astype(F32)

time: 616 us -> 612 us (level)
  Pallas kernels: 468 us -> 452 us
  waiting for transfers between devices: 89.9 us -> 96.9 us
    pallas_call x1, Pallas kernels: 121 us -> 101 us  [close(): pl.pallas_call(functools.partial(close_kernel, blocks, rest_blocks, rest_...]
    reduce_scatter x2, waiting for transfers between devices: 0.04 us -> 6.71 us  [body(): lax.psum_scatter(part, group, scatter_dimension=0, tiled=True, axis_index...]
    pallas_call x1 -> x2, Pallas kernels: 106 us -> 111 us  [attend_back(): pl.pallas_call(functools.partial(attend_back_kernel, tiles, wide, first_b...]
  transfers between devices with their start and end apart: 7 -> 8, of which waited for: 4 -> 5; matrix products, arithmetic and copies ran while one was open for 3% -> 3% of each run, Pallas kernels for 35% -> 53%
where the time goes in v3:
time: 612 us; the launch traced here: 606 us
  Pallas kernels  452 us (74%)
  waiting for transfers between devices  96.9 us (16%)
  other arithmetic  21.5 us (4%)
  local copies, waits for them, and re-layouts  19.2 us (3%)
  between operations  14.6 us (2%)
    pallas_call x2, Pallas kernels, attend_back(): pl.pallas_call(functools.partial(attend_back_kernel, tiles, wide, first_b...  111 us
    pallas_call x1, Pallas kernels, feed(): pl.pallas_call(functools.partial(feed_kernel, seqs, halo // TILE), grid=(...  110 us
    pallas_call x1, Pallas kernels, close(): pl.pallas_call(functools.partial(close_kernel, blocks, rest_blocks, rest_...  101 us
    pallas_call x1, Pallas kernels, attend(): pl.pallas_call(functools.partial(attend_kernel, tiles, wide), grid_spec=p...  49.2 us
    ppermute x2, waiting for transfers between devices, neighbours(): return lax.ppermute(facing, axis, [(0, 1), (1, 0)])  47.3 us
    pallas_call x2, Pallas kernels, weigh(): pl.pallas_call(functools.partial(weigh_kernel, blocks, share, held, turns...  46.9 us
    all_gather x3, waiting for transfers between devices, body(): gather = lambda shard: lax.all_gather(shard, group, axis=0, tiled=True)  42.1 us
    pallas_call x1, Pallas kernels, project(): pl.pallas_call(functools.partial(project_kernel, True, shards), grid=grid...  21.2 us
  transfers between devices with their start and end apart: 8, of which 5 were waited for; matrix products, arithmetic and copies ran while one was open for 3% of the time, Pallas kernels for 53%

profile of v3, /device:TPU:0, one launch (start us, length us, event | category | flops | bytes accessed | tf_op | source)
XLA Modules:
  0.0 606.4 jit_solution(15299301273984039789)
XLA Ops:
  7.2 0.0 all-gather.4.cloned.1.call-start
  7.2 0.8 fusion.7
  8.0 2.1 pad_maximum_fusion.1
  10.1 0.0 all-gather.4.cloned.1.call-update
  10.1 0.0 all-gather.8.cloned.1.call-start
  10.2 0.7 all-gather.8.cloned.1.call-update
  10.9 0.0 all-gather.6.cloned.1.call-start
  10.9 0.3 fusion.18
  11.2 0.0 copy-start.10
  11.2 2.0 concatenate.17
  13.2 0.0 all-gather.6.cloned.1.call-update
  13.2 0.0 reduce-scatter.5.cloned.1.call-start
  13.3 0.1 slice.33
  13.4 0.1 slice.34
  13.7 0.3 fusion.3
  14.0 0.1 fusion.8
  14.1 0.1 fusion.9
  14.2 0.1 fusion.4
  14.3 3.1 dynamic-slice_bitcast_fusion
  17.4 1.3 select_convert_fusion.ek_ref
  18.7 7.0 %fusion = (f32[2,1536,128]{2,1,0:T(8,128)}, f32[2,1536,128]{2,1,0:T(8,128)}) fusion(f32[128]{0:T(128)S(1)} %get-tuple-element.86, f32[128]{0:T(128)S(1)} %get-tuple-element.87, f32[2,1536]{1,0:T(2,128)S(1)} %subtract_convert_fusion), kind=kLoop, calls=%fused_computation.6 | loop fusion | flops 786432 | bytes 3159040 | tf_op jit(solution)/shard_map/mul | solution.py:1092
  25.7 34.1 %all-gather.4.cloned.1.call-done.w_ref = bf16[1024,3200]{1,0:T(8,128)(2,1)} async-done(((bf16[128,3200]{1,0:T(8,128)(2,1)}), bf16[1024,3200]{1,0:T(8,128)(2,1)}) %all-gather.4.cloned.1.call-update) | async-done | bytes 6553616 | tf_op jit(solution)/shard_map/all_gather | solution.py:1125
  59.8 1.5 collective-permute-start
  61.3 0.6 and_select_fusion.4
  61.9 0.9 select_convert_fusion.1.eq_ref
  62.9 1.0 slice.44
  63.9 0.6 slice_bitcast_fusion
  64.5 21.2 %project_own.1 = (bf16[1024,2048]{1,0:T(8,128)(2,1)}, bf16[2,1536,3072]{2,1,0:T(8,128)(2,1)}) custom-call(bf16[2,1024,1024]{2,1,0:T(8,128)(2,1)} %bitcast.34, bf16[1024,3200]{1,0:T(8,128)(2,1)} %all-gather.4.cloned.1.call-done.w_ref, f32[2,1536,128]{2,1,0:T(8,128)} %get-tuple-element.85.cos_ref, f32[2,1536,128]{2,1,0:T(8,128)} %get-tuple-element.84.sin_ref), custom_call_target="tpu_custom_call" | custom-call | flops 12884901888 | bytes 23068672 | tf_op jit(solution)/shard_map/project_own/pallas_call | solution.py:111
  85.7 43.7 %collective-permute-done.x_ref = bf16[2,512,1024]{2,1,0:T(8,128)(2,1)S(1)} collective-permute-done((bf16[2,512,1024]{2,1,0:T(8,128)(2,1)}, bf16[2,512,1024]{2,1,0:T(8,128)(2,1)S(1)}, u32[]{:S(2)}, u32[]{:S(2)}) %collective-permute-start) | collective-permute-done | bytes 2097184 | tf_op jit(solution)/shard_map/ppermute | solution.py:1058
  129.4 1.3 copy-done.6
  130.8 13.1 %project_halo.1.q_ref.k_ref.v_ref = bf16[2,1536,3072]{2,1,0:T(8,128)(2,1)} custom-call(bf16[2,512,1024]{2,1,0:T(8,128)(2,1)} %copy-done.6, bf16[1024,3200]{1,0:T(8,128)(2,1)} %all-gather.4.cloned.1.call-done.w_ref, f32[2,1536,128]{2,1,0:T(8,128)} %get-tuple-element.85.cos_ref, ...), custom_call_target="tpu_custom_call", output_to_operand_aliasing={{}: (4, {})} | custom-call | flops 6442450944 | bytes 14680064 | tf_op jit(solution)/shard_map/project_halo/pallas_call | solution.py:125
  143.9 49.2 %attend.1 = (bf16[2,1024,1024]{2,1,0:T(8,128)(2,1)}, bf16[1024,2048]{1,0:T(8,128)(2,1)}, f32[2,8,2,1024]{3,2,1,0:T(2,128)}) custom-call(s32[1]{0:T(128)} %bitcast.1.own_ref, s32[2,8]{1,0:T(2,128)} %get-tuple-element.88.lo_ref, s32[2,8]{1,0:T(2,128)} %get-tuple-element.89.hi_ref, bf16[2,1536,3072]{2,1,0:T(8,128)(2,1)} %project_halo.1.q_ref.k_ref.v_ref, ...), custom_call_target="tpu_custom_call" | custom-call | flops 25769803776 | bytes 33554432 | tf_op jit(solution)/shard_map/attend/pallas_call | solution.py:257
  193.0 0.0 all-gather.8.cloned.1.call-done.wd_ref
  193.1 8.0 %all-gather.6.cloned.1.call-done.w_ref = bf16[1024,6400]{1,0:T(8,128)(2,1)} async-done(((bf16[128,6400]{1,0:T(8,128)(2,1)}), bf16[1024,6400]{1,0:T(8,128)(2,1)}) %all-gather.6.cloned.1.call-update) | async-done | bytes 13107216 | tf_op jit(solution)/shard_map/all_gather | solution.py:1125
  201.0 109.6 %feed.1 = (bf16[2,1024,1024]{2,1,0:T(8,128)(2,1)}, bf16[1024,2048]{1,0:T(8,128)(2,1)}, bf16[2624,2048]{1,0:T(8,128)(2,1)}, bf16[2,1024,6656]{2,1,0:T(8,128)(2,1)...) custom-call(bf16[2,1024,1024]{2,1,0:T(8,128)(2,1)} %bitcast.35, ...), custom_call_target="tpu_custom_call" | custom-call | flops 74625056768 | bytes 67108864 | tf_op jit(solution)/shard_map/feed/pallas_call | solution.py:633
  310.7 20.6 %weigh_down.1 = bf16[1344,1024]{1,0:T(8,128)(2,1)} custom-call(bf16[2624,2048]{1,0:T(8,128)(2,1)} %get-tuple-element.39.refs_0_, bf16[2048,1024]{1,0:T(8,128)(2,1)} %bitcast.45), custom_call_target="tpu_custom_call" | custom-call | flops 11005853696 | bytes 25165824 | tf_op jit(solution)/shard_map/weigh_down/pallas_call | solution.py:728
  331.2 0.0 reduce-scatter.5.cloned.1.call-update
  331.3 0.0 reduce-scatter.3.cloned.1.call-start
  331.3 26.3 %weigh_early.1 = bf16[512,4096]{1,0:T(8,128)(2,1)} custom-call(bf16[1024,2048]{1,0:T(8,128)(2,1)} %get-tuple-element.35.refs_0_.h2t_ref, bf16[2048,6656]{1,0:T(8,128)(2,1)} %bitcast.46), custom_call_target="tpu_custom_call" | custom-call | flops 17179869184 | bytes 25165824 | tf_op jit(solution)/shard_map/weigh_early/pallas_call | solution.py:728
  357.7 0.0 reduce-scatter.3.cloned.1.call-update
  357.7 0.0 all-reduce.5.cloned.1.call-start
  357.8 0.8 copy-done.9
  358.6 0.6 collective-permute-start.1
  359.2 3.6 collective-permute-done.1.lseh_ref
  362.9 0.6 copy-done.13
  363.5 56.9 %attend_back.2.refs_0_ = bf16[3,2,1024,1024]{3,2,1,0:T(8,128)(2,1)} custom-call(s32[1]{0:T(128)} %bitcast.1.own_ref, s32[2,8]{1,0:T(2,128)} %get-tuple-element.88.lo_ref, s32[2,8]{1,0:T(2,128)} %get-tuple-element.89.hi_ref, bf16[2,1536,3072]{2,1,0:T(8,128)(2,1)} %project_halo.1.q_ref.k_ref.v_ref, bf16[2,1536,3072]{2,1,0:T(8,128)(2,1)} %project_halo.1.q_ref.k_ref.v_ref, ...), custom_call_target="tpu_custom_call" | custom-call | flops 32212254720 | bytes 67108864 | tf_op jit(solution)/shard_map/attend_back/pallas_call | solution.py:431
  420.4 0.0 reduce-scatter.5.cloned.1.call-done
  420.4 6.7 %reduce-scatter.3.cloned.1.call-done = bf16[128,4096]{1,0:T(8,128)(2,1)} async-done(((bf16[512,4096]{1,0:T(8,128)(2,1)}), bf16[128,4096]{1,0:T(8,128)(2,1)}) %reduce-scatter.3.cloned.1.call-update) | async-done | bytes 1048592 | tf_op jit(solution)/shard_map/reduce_scatter | solution.py:1149
  427.1 0.0 all-reduce.5.cloned.1.call-update
  427.2 53.8 %attend_back.3 = bf16[3,2,1024,1024]{3,2,1,0:T(8,128)(2,1)} custom-call(s32[1]{0:T(128)} %bitcast.1.own_ref, s32[2,8]{1,0:T(2,128)} %get-tuple-element.88.lo_ref, s32[2,8]{1,0:T(2,128)} %get-tuple-element.89.hi_ref, bf16[2,1536,3072]{2,1,0:T(8,128)(2,1)} %project_halo.1.q_ref.k_ref.v_ref, ...), custom_call_target="tpu_custom_call", output_to_operand_aliasing={{}: (16, {})} | custom-call | flops 32212254720 | bytes 67108864 | tf_op jit(solution)/shard_map/attend_back/pallas_call | solution.py:431
  481.0 100.9 %close.1 = (f32[2048,1024]{1,0:T(8,128)}, bf16[128,2560]{1,0:T(8,128)(2,1)}, bf16[128,3072]{1,0:T(8,128)(2,1)}) custom-call(bf16[1024,2048]{1,0:T(8,128)(2,1)} %get-tuple-element.35.refs_0_.h2t_ref, bf16[1024,2048]{1,0:T(8,128)(2,1)} %get-tuple-element.36.ot_ref, bf16[1024,2048]{1,0:T(8,128)(2,1)} %get-tuple-element.37.h1t_ref, bf16[2048,6656]{1,0:T(8,128)(2,1)} %bitcast.47, ...), custom_call_target="tpu_custom_call" | custom-call | flops 53687091200 | bytes 50331648 | tf_op jit(solution)/shard_map/close/pallas_call | solution.py:1006
  582.0 2.5 multiply_reduce_fusion.1
  584.5 0.5 convert_divide_fusion.1
  585.0 0.8 maximum_convert_fusion.1
  585.9 0.6 copy-done.2
  586.4 0.3 maximum_convert_fusion
  586.8 0.2 fusion.17
  587.0 1.1 copy-done.1
  588.1 2.1 multiply_reduce_fusion
  590.2 0.5 convert_divide_fusion
  590.7 1.2 slice_convert_fusion
  591.9 2.1 copy.35
  594.1 1.9 slice-done.1
  596.0 3.4 copy.36
  (44 shorter events, 0.2 us)
Async XLA Ops:
  7.2 3.7 copy-start
  7.2 52.7 %all-gather.4.cloned.1.call-start = ((), (), s32[]{:S(2)}) async-start(), calls=%async_computation.2 | async-start | bytes 7372800 | tf_op jit(solution)/shard_map/all_gather | solution.py:1125
  10.1 1.1 copy-start.8
  10.1 182.9 %all-gather.8.cloned.1.call-start = ((), (), s32[]{:S(2)}) async-start(), calls=%async_computation.4 | async-start | bytes 6045696 | tf_op jit(solution)/shard_map/all_gather | solution.py:1125
  10.9 190.1 %all-gather.6.cloned.1.call-start = ((), (), s32[]{:S(2)}) async-start(), calls=%async_computation.3 | async-start | bytes 14745600 | tf_op jit(solution)/shard_map/all_gather | solution.py:1125
  11.2 2.1 copy-start.10
  13.2 407.2 %reduce-scatter.5.cloned.1.call-start = ((), (), s32[]{:S(2)}) async-start(), calls=%async_computation.6 | async-start | bytes 3440640 | tf_op jit(solution)/shard_map/reduce_scatter | solution.py:1149
  59.8 69.6 %collective-permute-start = (bf16[2,512,1024]{2,1,0:T(8,128)(2,1)}, bf16[2,512,1024]{2,1,0:T(8,128)(2,1)S(1)}, u32[]{:S(2)}, u32[]{:S(2)}) collective-permute-start(bf16[2,512,1024]{2,1,0:T(8,128)(2,1)} %dynamic-slice_bitcast_fusion), channel_id=1, source_target_pairs={{0,16},{16,0},{1,17},{17,1},{2,18},{18,2},{3,19},{19,3},{4,20},{20... | collective-permute-start | bytes 6291464 | tf_op jit(solution)/shard_map/ppermute | solution.py:1058
  129.4 1.3 copy-start.6
  331.3 95.9 %reduce-scatter.3.cloned.1.call-start = ((), (), s32[]{:S(2)}) async-start(), calls=%async_computation.5 | async-start | bytes 5242880 | tf_op jit(solution)/shard_map/reduce_scatter | solution.py:1149
  357.7 0.9 copy-start.9
  357.7 227.3 %all-reduce.5.cloned.1.call-start = ((), (), s32[]{:S(2)}) async-start(), calls=%async_computation.7 | async-start | bytes 3473408 | tf_op jit(solution)/shard_map/psum | solution.py:1168
  358.6 4.3 collective-permute-start.1
  362.9 0.6 copy-start.13
  481.0 100.9 %copy-start.4 = (bf16[128,3072]{1,0:T(8,128)(2,1)S(1)}, bf16[128,3072]{1,0:T(8,128)(2,1)}, u32[]{:S(2)}) copy-start(bf16[128,3072]{1,0:T(8,128)(2,1)} %param.14) | copy-start | bytes 2359300
  581.9 2.6 copy-start.11
  581.9 3.1 copy-start.5
  585.0 1.4 copy-start.2
  586.8 1.3 copy-start.1
  586.8 3.4 copy-start.12
  586.8 3.9 copy-start.7
  588.1 3.8 copy-start.3
  588.1 6.0 slice-start
  590.7 5.2 slice-start.1
Sparse Core Ops, SparseCore 0:
  10.5 49.3 all-gather.3
  61.7 62.9 all-gather.7
  126.6 74.3 all-gather.5
  331.4 40.1 reduce-scatter.4
  374.4 52.6 reduce-scatter.2
  429.6 74.7 all-reduce.4

commit v4 on v3

--- a/solution.py
+++ b/solution.py
@@ -747,9 +747,9 @@
     )(*lefts, right)
 
 
-LAGS = (1, 3, 5, 6, 7, 8)
-RING, RING_XY, RING_LINE = 5, 2, 4
-EARLY = 8
+LAGS = (1, 3, 5, 7, 9, 11)
+RING, RING_XY, RING_LINE = 5, 2, 8
+EARLY = 7
 
 
 def close_kernel(blocks, rest_blocks, rest_edge, seqs, reps, h2t_ref, ot_ref, h1t_ref, rest_ref, right_ref, three_ref, w_ref, x_ref, dr_ref, gain_ref, gi_ref, rest_sum, sum_ref,
@@ -1132,13 +1132,14 @@
     x_halo = neighbours(x, "seq", 1, (qkv_full, cosines, sines, marks_k))
     rest_full = gather(jnp.concatenate([w_in[:, :FF], blank, w_in[:, FF:], blank, w_out], axis=1))
     down_full = gather(w_down)
-    gains = qkv_full[:, 3 * width : 3 * width + share].reshape(shards, share, share).astype(F32)
-    gain_one, gain_two = gains[:, 0].reshape(1, width), gains[:, 1].reshape(1, width)
 
     h1t, qkv = project(x, qkv_full, cosines, sines, 0, None, extent, shards)
     qkv = project(x_halo, qkv_full, cosines, sines, stretch // TILE, qkv, extent, shards)
     mixed, mixed_t, lse = attend(own, lows, highs, qkv, marks_k, marks_q, stretch)
     lse_halo = neighbours(lse, "seq", 3)
+    late_full, mixed, lse_halo = lax.optimization_barrier((qkv_full, mixed, lse_halo))
+    gains = late_full[:, 3 * width : 3 * width + share].reshape(shards, share, share).astype(F32)
+    gain_one, gain_two = gains[:, 0].reshape(1, width), gains[:, 1].reshape(1, width)
     result, h2t, hidt, slopes, dr, do, delta, do_halo, delta_halo = feed(
         x, mixed, seeds, gain_two, rest_full, down_full, seq_count, halo
     )

time: 612 us -> 630 us (1.029)
  Pallas kernels: 452 us -> 472 us
    pallas_call x1, Pallas kernels: 101 us -> 117 us  [close(): pl.pallas_call(functools.partial(close_kernel, blocks, rest_blocks, rest_...]
    all_gather x3, waiting for transfers between devices: 42.1 us -> 34.4 us  [body(): gather = lambda shard: lax.all_gather(shard, group, axis=0, tiled=True)]
  transfers between devices with their start and end apart: 8 -> 8, of which waited for: 5 -> 5; matrix products, arithmetic and copies ran while one was open for 3% -> 3% of each run, Pallas kernels for 53% -> 46%
where the time goes in v4:
time: 630 us; the launch traced here: 621 us
  Pallas kernels  472 us (75%)
  waiting for transfers between devices  93 us (15%)
  other arithmetic  21.5 us (3%)
  local copies, waits for them, and re-layouts  18.3 us (3%)
  between operations  14.6 us (2%)
    pallas_call x1, Pallas kernels, close(): pl.pallas_call(functools.partial(close_kernel, blocks, rest_blocks, rest_...  117 us
    pallas_call x2, Pallas kernels, attend_back(): pl.pallas_call(functools.partial(attend_back_kernel, tiles, wide, first_b...  116 us
    pallas_call x1, Pallas kernels, feed(): pl.pallas_call(functools.partial(feed_kernel, seqs, halo // TILE), grid=(...  110 us
    pallas_call x1, Pallas kernels, attend(): pl.pallas_call(functools.partial(attend_kernel, tiles, wide), grid_spec=p...  51.4 us
    ppermute x2, waiting for transfers between devices, neighbours(): return lax.ppermute(facing, axis, [(0, 1), (1, 0)])  49.5 us
    pallas_call x2, Pallas kernels, weigh(): pl.pallas_call(functools.partial(weigh_kernel, blocks, share, held, turns...  44.3 us
    all_gather x3, waiting for transfers between devices, body(): gather = lambda shard: lax.all_gather(shard, group, axis=0, tiled=True)  34.4 us
    pallas_call x1, Pallas kernels, project(): pl.pallas_call(functools.partial(project_kernel, True, shards), grid=grid...  21.2 us
  transfers between devices with their start and end apart: 8, of which 5 were waited for; matrix products, arithmetic and copies ran while one was open for 3% of the time, Pallas kernels for 46%

profile of v4, /device:TPU:0, one launch (start us, length us, event | category | flops | bytes accessed | tf_op | source)
XLA Modules:
  0.0 621.3 jit_solution(11551563805646191178)
XLA Ops:
  7.2 0.0 copy-start
  7.2 0.0 all-gather.4.cloned.1.call-start
  7.2 0.8 fusion.7
  8.0 2.1 pad_maximum_fusion.1
  10.1 0.0 all-gather.4.cloned.1.call-update
  10.1 0.0 all-gather.8.cloned.1.call-start
  10.2 0.7 all-gather.8.cloned.1.call-update
  10.9 0.0 all-gather.6.cloned.1.call-start
  10.9 0.3 fusion.18
  11.2 0.0 copy-start.9
  11.2 1.9 concatenate.17
  13.2 0.0 all-gather.6.cloned.1.call-update
  13.2 0.0 reduce-scatter.5.cloned.1.call-start
  13.3 0.1 slice.34
  13.4 0.1 slice.33
  13.6 0.3 fusion.3
  14.0 0.1 fusion.8
  14.1 0.1 fusion.4
  14.2 3.1 dynamic-slice_bitcast_fusion
  17.3 1.4 select_convert_fusion.ek_ref
  18.6 7.0 %fusion = (f32[2,1536,128]{2,1,0:T(8,128)}, f32[2,1536,128]{2,1,0:T(8,128)}) fusion(f32[128]{0:T(128)S(1)} %get-tuple-element.92, f32[128]{0:T(128)S(1)} %get-tuple-element.93, f32[2,1536]{1,0:T(2,128)S(1)} %subtract_convert_fusion), kind=kLoop, calls=%fused_computation.6 | loop fusion | flops 786432 | bytes 3159040 | tf_op jit(solution)/shard_map/mul | solution.py:1092
  25.6 34.2 %all-gather.4.cloned.1.call-done.w_ref = bf16[1024,3200]{1,0:T(8,128)(2,1)} async-done(((bf16[128,3200]{1,0:T(8,128)(2,1)}), bf16[1024,3200]{1,0:T(8,128)(2,1)}) %all-gather.4.cloned.1.call-update) | async-done | bytes 6553616 | tf_op jit(solution)/shard_map/all_gather | solution.py:1125
  59.8 1.5 collective-permute-start
  61.3 0.1 fusion.9
  61.4 0.6 and_select_fusion.4
  62.0 0.9 select_convert_fusion.1.eq_ref
  62.9 21.2 %project_own.1 = (bf16[1024,2048]{1,0:T(8,128)(2,1)}, bf16[2,1536,3072]{2,1,0:T(8,128)(2,1)}) custom-call(bf16[2,1024,1024]{2,1,0:T(8,128)(2,1)} %bitcast.34, bf16[1024,3200]{1,0:T(8,128)(2,1)} %all-gather.4.cloned.1.call-done.w_ref, f32[2,1536,128]{2,1,0:T(8,128)} %get-tuple-element.91.cos_ref, f32[2,1536,128]{2,1,0:T(8,128)} %get-tuple-element.90.sin_ref), custom_call_target="tpu_custom_call" | custom-call | flops 12884901888 | bytes 23068672 | tf_op jit(solution)/shard_map/project_own/pallas_call | solution.py:111
  84.2 45.2 %collective-permute-done.x_ref = bf16[2,512,1024]{2,1,0:T(8,128)(2,1)S(1)} collective-permute-done((bf16[2,512,1024]{2,1,0:T(8,128)(2,1)}, bf16[2,512,1024]{2,1,0:T(8,128)(2,1)S(1)}, u32[]{:S(2)}, u32[]{:S(2)}) %collective-permute-start) | collective-permute-done | bytes 2097184 | tf_op jit(solution)/shard_map/ppermute | solution.py:1058
  129.4 1.3 copy-done.6
  130.8 13.1 %project_halo.1.q_ref.k_ref.v_ref = bf16[2,1536,3072]{2,1,0:T(8,128)(2,1)} custom-call(bf16[2,512,1024]{2,1,0:T(8,128)(2,1)} %copy-done.6, bf16[1024,3200]{1,0:T(8,128)(2,1)} %all-gather.4.cloned.1.call-done.w_ref, f32[2,1536,128]{2,1,0:T(8,128)} %get-tuple-element.91.cos_ref, ...), custom_call_target="tpu_custom_call", output_to_operand_aliasing={{}: (4, {})} | custom-call | flops 6442450944 | bytes 14680064 | tf_op jit(solution)/shard_map/project_halo/pallas_call | solution.py:125
  143.9 51.4 %attend.1 = (bf16[2,1024,1024]{2,1,0:T(8,128)(2,1)}, bf16[1024,2048]{1,0:T(8,128)(2,1)}, f32[2,8,2,1024]{3,2,1,0:T(2,128)}) custom-call(s32[1]{0:T(128)} %bitcast.3.own_ref, s32[2,8]{1,0:T(2,128)} %get-tuple-element.94.lo_ref, s32[2,8]{1,0:T(2,128)} %get-tuple-element.95.hi_ref, bf16[2,1536,3072]{2,1,0:T(8,128)(2,1)} %project_halo.1.q_ref.k_ref.v_ref, ...), custom_call_target="tpu_custom_call" | custom-call | flops 25769803776 | bytes 33554432 | tf_op jit(solution)/shard_map/attend/pallas_call | solution.py:257
  195.3 0.8 constant_dynamic-slice_fusion
  196.1 4.3 collective-permute-done.1.lseh_ref
  200.5 0.6 slice_bitcast_fusion
  201.1 0.1 all-gather.6.cloned.1.call-done.w_ref
  201.2 109.5 %feed.1 = (bf16[2,1024,1024]{2,1,0:T(8,128)(2,1)}, bf16[1024,2048]{1,0:T(8,128)(2,1)}, bf16[2624,2048]{1,0:T(8,128)(2,1)}, bf16[2,1024,6656]{2,1,0:T(8,128)(2,1)...) custom-call(bf16[2,1024,1024]{2,1,0:T(8,128)(2,1)} %bitcast.35, ...), custom_call_target="tpu_custom_call" | custom-call | flops 74625056768 | bytes 67108864 | tf_op jit(solution)/shard_map/feed/pallas_call | solution.py:633
  310.7 20.6 %weigh_down.1 = bf16[1344,1024]{1,0:T(8,128)(2,1)} custom-call(bf16[2624,2048]{1,0:T(8,128)(2,1)} %get-tuple-element.45.refs_0_, bf16[2048,1024]{1,0:T(8,128)(2,1)} %bitcast.45), custom_call_target="tpu_custom_call" | custom-call | flops 11005853696 | bytes 25165824 | tf_op jit(solution)/shard_map/weigh_down/pallas_call | solution.py:728
  331.3 0.0 reduce-scatter.5.cloned.1.call-update
  331.4 0.0 reduce-scatter.3.cloned.1.call-start
  331.4 23.8 %weigh_early.1 = bf16[512,3584]{1,0:T(8,128)(2,1)} custom-call(bf16[1024,2048]{1,0:T(8,128)(2,1)} %get-tuple-element.41.refs_0_.h2t_ref, bf16[2048,6656]{1,0:T(8,128)(2,1)} %bitcast.46), custom_call_target="tpu_custom_call" | custom-call | flops 15032385536 | bytes 25165824 | tf_op jit(solution)/shard_map/weigh_early/pallas_call | solution.py:728
  355.2 0.0 reduce-scatter.3.cloned.1.call-update
  355.2 0.0 all-reduce.5.cloned.1.call-start
  355.2 61.9 %attend_back.2.refs_0_ = bf16[3,2,1024,1024]{3,2,1,0:T(8,128)(2,1)} custom-call(s32[1]{0:T(128)} %bitcast.3.own_ref, s32[2,8]{1,0:T(2,128)} %get-tuple-element.94.lo_ref, s32[2,8]{1,0:T(2,128)} %get-tuple-element.95.hi_ref, bf16[2,1536,3072]{2,1,0:T(8,128)(2,1)} %project_halo.1.q_ref.k_ref.v_ref, bf16[2,1536,3072]{2,1,0:T(8,128)(2,1)} %project_halo.1.q_ref.k_ref.v_ref, ...), custom_call_target="tpu_custom_call" | custom-call | flops 32212254720 | bytes 67108864 | tf_op jit(solution)/shard_map/attend_back/pallas_call | solution.py:431
  417.2 0.0 reduce-scatter.5.cloned.1.call-done
  417.2 8.3 %reduce-scatter.3.cloned.1.call-done = bf16[128,3584]{1,0:T(8,128)(2,1)} async-done(((bf16[512,3584]{1,0:T(8,128)(2,1)}), bf16[128,3584]{1,0:T(8,128)(2,1)}) %reduce-scatter.3.cloned.1.call-update) | async-done | bytes 917520 | tf_op jit(solution)/shard_map/reduce_scatter | solution.py:1150
  425.5 53.9 %attend_back.3 = bf16[3,2,1024,1024]{3,2,1,0:T(8,128)(2,1)} custom-call(s32[1]{0:T(128)} %bitcast.3.own_ref, s32[2,8]{1,0:T(2,128)} %get-tuple-element.94.lo_ref, s32[2,8]{1,0:T(2,128)} %get-tuple-element.95.hi_ref, bf16[2,1536,3072]{2,1,0:T(8,128)(2,1)} %project_halo.1.q_ref.k_ref.v_ref, ...), custom_call_target="tpu_custom_call", output_to_operand_aliasing={{}: (16, {})} | custom-call | flops 32212254720 | bytes 67108864 | tf_op jit(solution)/shard_map/attend_back/pallas_call | solution.py:431
  479.4 0.0 all-reduce.5.cloned.1.call-update
  479.4 0.0 copy-start.5
  479.4 116.8 %close.1 = (f32[2048,1024]{1,0:T(8,128)}, bf16[128,3072]{1,0:T(8,128)(2,1)}, bf16[128,3072]{1,0:T(8,128)(2,1)}) custom-call(bf16[1024,2048]{1,0:T(8,128)(2,1)} %get-tuple-element.41.refs_0_.h2t_ref, bf16[1024,2048]{1,0:T(8,128)(2,1)} %get-tuple-element.42.ot_ref, bf16[1024,2048]{1,0:T(8,128)(2,1)} %get-tuple-element.43.h1t_ref, bf16[2048,6656]{1,0:T(8,128)(2,1)} %bitcast.47, ...), custom_call_target="tpu_custom_call" | custom-call | flops 53687091200 | bytes 50331648 | tf_op jit(solution)/shard_map/close/pallas_call | solution.py:1006
  596.3 0.0 copy-start.10
  596.3 2.6 multiply_reduce_fusion.1
  598.9 0.5 convert_divide_fusion.1
  599.4 0.8 maximum_convert_fusion.1
  600.2 0.5 copy-done.3
  600.8 0.3 maximum_convert_fusion
  601.1 0.8 copy-done.7
  601.9 1.2 slice_convert_fusion
  603.1 0.2 fusion.17
  603.3 1.1 copy-done.1
  604.4 2.0 multiply_reduce_fusion
  606.4 0.5 convert_divide_fusion
  607.0 2.1 copy.35
  609.1 1.8 slice-done.1
  610.9 3.4 copy.36
  (43 shorter events, 0.2 us)
Async XLA Ops:
  7.2 3.7 copy-start
  7.2 52.7 %all-gather.4.cloned.1.call-start = ((), (), s32[]{:S(2)}) async-start(), calls=%async_computation.2 | async-start | bytes 7372800 | tf_op jit(solution)/shard_map/all_gather | solution.py:1125
  10.1 1.1 copy-start.8
  10.1 190.9 %all-gather.8.cloned.1.call-start = ((), (), s32[]{:S(2)}) async-start(), calls=%async_computation.4 | async-start | bytes 6045696 | tf_op jit(solution)/shard_map/all_gather | solution.py:1125
  10.9 190.3 %all-gather.6.cloned.1.call-start = ((), (), s32[]{:S(2)}) async-start(), calls=%async_computation.3 | async-start | bytes 14745600 | tf_op jit(solution)/shard_map/all_gather | solution.py:1125
  11.2 2.0 copy-start.9
  13.2 404.0 %reduce-scatter.5.cloned.1.call-start = ((), (), s32[]{:S(2)}) async-start(), calls=%async_computation.6 | async-start | bytes 3440640 | tf_op jit(solution)/shard_map/reduce_scatter | solution.py:1150
  59.8 69.6 %collective-permute-start = (bf16[2,512,1024]{2,1,0:T(8,128)(2,1)}, bf16[2,512,1024]{2,1,0:T(8,128)(2,1)S(1)}, u32[]{:S(2)}, u32[]{:S(2)}) collective-permute-start(bf16[2,512,1024]{2,1,0:T(8,128)(2,1)} %dynamic-slice_bitcast_fusion), channel_id=1, source_target_pairs={{0,16},{16,0},{1,17},{17,1},{2,18},{18,2},{3,19},{19,3},{4,20},{20... | collective-permute-start | bytes 6291464 | tf_op jit(solution)/shard_map/ppermute | solution.py:1058
  129.4 1.3 copy-start.6
  143.9 56.5 %slice-start.2 = ((bf16[1024,3200]{1,0:T(8,128)(2,1)}), bf16[1024,128]{1,0:T(8,128)(2,1)S(1)}, s32[]{:S(2)}) async-start(bf16[1024,3200]{1,0:T(8,128)(2,1)} %all-gather.4.cloned.1.call-done.w_ref), calls=%async_computation.10 | async-start | bytes 524288 | tf_op jit(solution)/shard_map/slice | solution.py:1141
  196.1 4.3 collective-permute-start.1
  200.4 110.3 %copy-start.12 = (f32[2,8,2,512]{3,2,1,0:T(2,128)}, f32[2,8,2,512]{3,2,1,0:T(2,128)S(1)}, u32[]{:S(2)}) copy-start(f32[2,8,2,512]{3,2,1,0:T(2,128)S(1)} %collective-permute-done.1.lseh_ref) | copy-start | bytes 196612
  331.4 94.1 %reduce-scatter.3.cloned.1.call-start = ((), (), s32[]{:S(2)}) async-start(), calls=%async_computation.5 | async-start | bytes 4587520 | tf_op jit(solution)/shard_map/reduce_scatter | solution.py:1150
  355.2 244.2 %all-reduce.5.cloned.1.call-start = ((), (), s32[]{:S(2)}) async-start(), calls=%async_computation.7 | async-start | bytes 3211264 | tf_op jit(solution)/shard_map/psum | solution.py:1169
  479.4 116.9 %copy-start.5 = (bf16[128,3072]{1,0:T(8,128)(2,1)S(1)}, bf16[128,3072]{1,0:T(8,128)(2,1)}, u32[]{:S(2)}) copy-start(bf16[128,3072]{1,0:T(8,128)(2,1)} %param.14) | copy-start | bytes 2359300
  596.3 2.6 copy-start.10
  596.3 3.1 copy-start.4
  599.4 1.4 copy-start.3
  600.8 1.1 copy-start.7
  603.1 1.3 copy-start.1
  603.1 3.4 copy-start.11
  603.2 3.7 copy-start.2
  604.4 4.7 slice-start
  607.0 4.0 slice-start.1
Sparse Core Ops, SparseCore 0:
  10.5 49.3 all-gather.3
  61.7 62.9 all-gather.7
  126.6 74.5 all-gather.5
  331.5 42.7 reduce-scatter.4
  377.1 48.3 reduce-scatter.2
  479.5 94.9 all-reduce.4

commit v5 on v4

--- a/solution.py
+++ b/solution.py
@@ -747,14 +747,15 @@
     )(*lefts, right)
 
 
-LAGS = (1, 3, 5, 7, 9, 11)
-RING, RING_XY, RING_LINE = 5, 2, 8
-EARLY = 7
-
-
-def close_kernel(blocks, rest_blocks, rest_edge, seqs, reps, h2t_ref, ot_ref, h1t_ref, rest_ref, right_ref, three_ref, w_ref, x_ref, dr_ref, gain_ref, gi_ref, rest_sum, sum_ref,
+LAGS = (1, 3, 5, 6, 7, 8)
+RING, RING_XY, RING_LINE = 5, 2, 4
+EARLY, DOWN_BLOCKS, LINE_LAG = 8, 4, 2
+
+
+def close_kernel(blocks, rest_blocks, rest_edge, seqs, reps, h2t_ref, ot_ref, h1t_ref, rest_ref, right_ref, three_ref, w_ref, x_ref, dr_ref, gain_ref, down_ref,
+                 gi_ref, rest_sum, sum_ref, down_sum,
                  prod, kept0, kept1x, kept1y, kept2, s0, r0, s1x, r1x, s1y, r1y, s2x, r2x, s2y, r2y,
-                 mine, ends, others, send_sem, recv_sem):
+                 mine, ends, others, down_ends, down_others, send_sem, recv_sem, line_sem):
     step = pl.program_id(0)
     width = h1t_ref.shape[0]
     share = mine.shape[1]
@@ -805,6 +806,18 @@
         slot, turn = slot_in + which, lax.rem(n, RING_LINE)
         return line(which, mine.at[turn], ends.at[turn], others.at[turn], send_sem.at[turn, slot], recv_sem.at[turn, slot])
 
+    down_columns = down_ends.shape[2]
+    extra = []
+    for k in range(down_ends.shape[0]):
+        extra.append((down_ref, down_ends, down_others, down_sum, k, slice(k * down_columns, (k + 1) * down_columns)))
+
+    def extra_line(index, which):
+        source, first, second, _, k, columns = extra[index]
+        return line(
+            which, source.at[:, columns], first.at[k], second.at[k],
+            line_sem.at[0, index, which], line_sem.at[1, index, which],
+        )
+
     def start(copies):
         for each in copies:
             each.start()
@@ -829,6 +842,11 @@
         @pl.when(jnp.logical_not(inner))
         def _():
             pl.semaphore_wait(barrier, len(partners))
+
+    for index in range(len(extra)):
+        @pl.when((step == index) & jnp.logical_not(inner))
+        def _():
+            extra_line(index, 0).start()
 
     whole_blocks, split = rest_edge // CUT, rest_edge % CUT
 
@@ -870,6 +888,34 @@
             back = term if back is None else back + term
         unit, inverse = normed(x_ref[...].astype(F32))
         gi_ref[...] = dr_ref[...] + norm_back(back * gain_ref[...], unit, inverse)
+
+    for index, (source, first, second, total, k, columns) in enumerate(extra):
+        meet, share_out, close_out = (index + LINE_LAG * hop for hop in (1, 2, 3))
+
+        @pl.when((step == meet) & inner)
+        def _():
+            extra_line(index, 0).wait_recv()
+            first[k] = (source[:, columns].astype(F32) + first[k].astype(F32)).astype(BF16)
+            extra_line(index, 1).start()
+
+        @pl.when((step == share_out) & inner)
+        def _():
+            extra_line(index, 1).wait()
+            second[k] = (first[k].astype(F32) + second[k].astype(F32)).astype(BF16)
+            extra_line(index, 2).start()
+
+        @pl.when(step == close_out)
+        def _():
+            @pl.when(inner)
+            def _():
+                extra_line(index, 2).wait_send()
+
+            @pl.when(jnp.logical_not(inner))
+            def _():
+                extra_line(index, 0).wait_send()
+                extra_line(index, 2).wait_recv()
+
+            total[:, columns] = second[k]
 
     n6 = step - LAGS[5]
 
@@ -986,16 +1032,17 @@
     return right_ref.shape[1] // three_ref.shape[1]
 
 
-def close(h2t, mixed_t, h1t, rest, rest_edge, slopes, weight, x, dr, gain, seqs, dps, reps):
+def close(h2t, mixed_t, h1t, rest, rest_edge, slopes, weight, x, dr, gain, down, seqs, dps, reps):
     assert (dps, reps) == (4, 4)
     width, tokens = h1t.shape
     share = width // (seqs * dps)
     rest_blocks = rest.shape[1] // CUT - EARLY
     rest_edge = rest_edge - EARLY * CUT
+    blocks_of = lambda array, count: (count, array.shape[0], array.shape[1] // count)
     blocks = rest_blocks + 3 * width // CUT
     halves = width // CUT
     token_blocks = tokens // TILE
-    steps = max(blocks + token_blocks, blocks + LAGS[5])
+    steps = max(blocks + token_blocks, blocks + LAGS[5], DOWN_BLOCKS + 3 * LINE_LAG)
     late = lambda s: jnp.clip(s - blocks, 0, token_blocks - 1)
     turn_of = lambda s: jnp.clip(s - rest_blocks, 0, blocks - rest_blocks - 1)
     fixed = lambda m, n: pl.BlockSpec((m, n), lambda s: (0, 0), pipeline_mode=pl.Buffered(1))
@@ -1017,12 +1064,16 @@
             row,
             row,
             fixed(1, width),
+            fixed(*down.shape),
         ],
-        out_specs=[row, fixed(share, rest_blocks * CUT), fixed(share, 3 * width)],
+        out_specs=[
+            row, fixed(share, rest_blocks * CUT), fixed(share, 3 * width), fixed(*down.shape),
+        ],
         out_shape=[
             jax.ShapeDtypeStruct((tokens, width), F32),
             jax.ShapeDtypeStruct((share, rest_blocks * CUT), BF16),
             jax.ShapeDtypeStruct((share, 3 * width), BF16),
+            jax.ShapeDtypeStruct(down.shape, BF16),
         ],
         scratch_shapes=[
             pltpu.VMEM((width, CUT), F32),
@@ -1036,15 +1087,17 @@
             *buffers(RING_XY, seqs - 1, share),
             *buffers(RING_XY, share),
             *[pltpu.VMEM((RING_LINE, share, CUT), BF16)] * 3,
+            *[pltpu.VMEM(blocks_of(down, DOWN_BLOCKS), BF16)] * 2,
             pltpu.SemaphoreType.DMA((max(2 * RING_XY, RING_LINE), slots)),
             pltpu.SemaphoreType.DMA((max(2 * RING_XY, RING_LINE), slots)),
+            pltpu.SemaphoreType.DMA((2, DOWN_BLOCKS, 3)),
         ],
         compiler_params=params(collective_id=1, has_side_effects=True),
         cost_estimate=pl.CostEstimate(
-            flops=2 * tokens * width * (6 * width + rest.shape[1]), bytes_accessed=48 * 1024 * 1024, transcendentals=0
+            flops=tokens * width * width // 4, bytes_accessed=4 * 1024 * 1024, transcendentals=0
         ),
         name="close",
-    )(h2t, mixed_t, h1t, rest, slopes, slopes, weight, x, dr, gain)
+    )(h2t, mixed_t, h1t, rest, slopes, slopes, weight, x, dr, gain, down)
 
 
 def neighbours(block, axis, along, after=None):
@@ -1149,15 +1202,16 @@
     pairs = [list(range(core, seq_count * dps, 2)) for core in range(2)]
     scatter = lambda part: lax.psum_scatter(part, group, scatter_dimension=0, tiled=True, axis_index_groups=pairs)
     slopes = slopes.reshape(tokens, -1)
+    part_early = weigh([h2t], slopes, CUT, EARLY, ((0, EARLY, ((0, CUT),)),), share, "weigh_early", 4)
+    shard_early = scatter(part_early)
+    hidt, part_early = lax.optimization_barrier((hidt, part_early))
     part_down = weigh(
         [hidt], seeds.reshape(tokens, width), TILE, width // TILE, ((0, width // TILE, ((0, TILE),)),),
         w_down.shape[0], "weigh_down", 3,
     )
     shard_down = scatter(part_down)
-    slopes, part_down = lax.optimization_barrier((slopes, part_down))
-    part_early = weigh([h2t], slopes, CUT, EARLY, ((0, EARLY, ((0, CUT),)),), share, "weigh_early", 4)
-    shard_early = scatter(part_early)
-    do_halo, part_early = lax.optimization_barrier((do_halo, part_early))
+    do_halo, part_down = lax.optimization_barrier((do_halo, part_down))
+
     def back(first_batch, count, held):
         return attend_back(
             own, lows, highs, qkv, do, do_halo, lse, lse_halo, delta, delta_halo, marks_k, marks_q, cosines, sines,
@@ -1165,12 +1219,12 @@
         )
 
     slopes_qkv = back(0, batch // 2, None)
-    slopes_qkv, shard_early, shard_down = lax.optimization_barrier((slopes_qkv, shard_early, shard_down))
-    early_sum, down_sum = lax.psum((shard_early, shard_down), "rep")
+    slopes_qkv, shard_early = lax.optimization_barrier((slopes_qkv, shard_early))
+    early_sum = lax.psum(shard_early, "rep")
     slopes_qkv = back(batch // 2, batch - batch // 2, slopes_qkv)
-    grad_x, late_sum, grad_qkv = close(
+    grad_x, late_sum, grad_qkv, down_sum = close(
         h2t, mixed_t, h1t, slopes, 2 * FF_PAD, slopes_qkv.reshape(3, tokens, width), qkv_full, x.reshape(tokens, width), dr.reshape(tokens, width),
-        gain_one, seq_count, dps, lax.axis_size("rep"),
+        gain_one, shard_down, seq_count, dps, lax.axis_size("rep"),
     )
     grad_qkv = grad_qkv.astype(F32)
     rest_sum = jnp.concatenate([early_sum, late_sum], axis=1).astype(F32)

time: 630 us -> 607 us (0.963)
  Pallas kernels: 472 us -> 460 us
  waiting for transfers between devices: 93 us -> 82.9 us
    pallas_call x1, Pallas kernels: 117 us -> 101 us  [close(): pl.pallas_call(functools.partial(close_kernel, blocks, rest_blocks, rest_...]
    reduce_scatter x2, waiting for transfers between devices: 8.32 us -> 0.03 us  [body(): lax.psum_scatter(part, group, scatter_dimension=0, tiled=True, axis_index...]
  transfers between devices with their start and end apart: 8 -> 8, of which waited for: 5 -> 3; matrix products, arithmetic and copies ran while one was open for 3% -> 4% of each run, Pallas kernels for 46% -> 54%
where the time goes in v5:
time: 607 us; the launch traced here: 600 us
  Pallas kernels  460 us (76%)
  waiting for transfers between devices  82.9 us (14%)
  other arithmetic  22.7 us (4%)
  local copies, waits for them, and re-layouts  16.5 us (3%)
  between operations  14.6 us (2%)
    pallas_call x2, Pallas kernels, attend_back(): pl.pallas_call(functools.partial(attend_back_kernel, tiles, wide, first_b...  115 us
    pallas_call x1, Pallas kernels, feed(): pl.pallas_call(functools.partial(feed_kernel, seqs, halo // TILE), grid=(...  110 us
    pallas_call x1, Pallas kernels, close(): pl.pallas_call(functools.partial(close_kernel, blocks, rest_blocks, rest_...  101 us
    pallas_call x1, Pallas kernels, attend(): pl.pallas_call(functools.partial(attend_kernel, tiles, wide), grid_spec=p...  51.5 us
    pallas_call x2, Pallas kernels, weigh(): pl.pallas_call(functools.partial(weigh_kernel, blocks, share, held, turns...  48.8 us
    ppermute x2, waiting for transfers between devices, neighbours(): return lax.ppermute(facing, axis, [(0, 1), (1, 0)])  47.8 us
    all_gather x3, waiting for transfers between devices, body(): gather = lambda shard: lax.all_gather(shard, group, axis=0, tiled=True)  34.2 us
    pallas_call x1, Pallas kernels, project(): pl.pallas_call(functools.partial(project_kernel, True, shards), grid=grid...  21.2 us
  transfers between devices with their start and end apart: 8, of which 3 were waited for; matrix products, arithmetic and copies ran while one was open for 4% of the time, Pallas kernels for 54%

profile of v5, /device:TPU:0, one launch (start us, length us, event | category | flops | bytes accessed | tf_op | source)
XLA Modules:
  0.0 600.1 jit_solution(5119834331582437681)
XLA Ops:
  7.2 0.0 copy-start
  7.2 0.0 all-gather.4.cloned.1.call-start
  7.2 0.8 fusion.7
  8.0 2.1 pad_maximum_fusion.1
  10.1 0.0 all-gather.4.cloned.1.call-update
  10.1 0.0 all-gather.8.cloned.1.call-start
  10.2 0.7 all-gather.8.cloned.1.call-update
  10.9 0.0 all-gather.6.cloned.1.call-start
  10.9 0.3 fusion.18
  11.2 0.0 copy-done.8
  11.2 0.0 copy-start.9
  11.2 1.9 concatenate.17
  13.2 0.0 all-gather.6.cloned.1.call-update
  13.2 0.0 reduce-scatter.3.cloned.1.call-start
  13.3 0.1 slice.34
  13.4 0.1 slice.33
  13.6 0.3 fusion.3
  14.0 0.1 fusion.8
  14.1 0.1 fusion.4
  14.2 3.1 dynamic-slice_bitcast_fusion
  17.3 1.3 select_convert_fusion.ek_ref
  18.6 7.0 %fusion = (f32[2,1536,128]{2,1,0:T(8,128)}, f32[2,1536,128]{2,1,0:T(8,128)}) fusion(f32[128]{0:T(128)S(1)} %get-tuple-element.90, f32[128]{0:T(128)S(1)} %get-tuple-element.91, f32[2,1536]{1,0:T(2,128)S(1)} %subtract_convert_fusion), kind=kLoop, calls=%fused_computation.6 | loop fusion | flops 786432 | bytes 3159040 | tf_op jit(solution)/shard_map/mul | solution.py:1145
  25.6 34.2 %all-gather.4.cloned.1.call-done.w_ref = bf16[1024,3200]{1,0:T(8,128)(2,1)} async-done(((bf16[128,3200]{1,0:T(8,128)(2,1)}), bf16[1024,3200]{1,0:T(8,128)(2,1)}) %all-gather.4.cloned.1.call-update) | async-done | bytes 6553616 | tf_op jit(solution)/shard_map/all_gather | solution.py:1178
  59.8 1.5 collective-permute-start
  61.3 0.1 fusion.9
  61.4 0.5 and_select_fusion.4
  61.9 0.9 select_convert_fusion.1.eq_ref
  62.9 21.2 %project_own.1 = (bf16[1024,2048]{1,0:T(8,128)(2,1)}, bf16[2,1536,3072]{2,1,0:T(8,128)(2,1)}) custom-call(bf16[2,1024,1024]{2,1,0:T(8,128)(2,1)} %bitcast.34, bf16[1024,3200]{1,0:T(8,128)(2,1)} %all-gather.4.cloned.1.call-done.w_ref, f32[2,1536,128]{2,1,0:T(8,128)} %get-tuple-element.89.cos_ref, f32[2,1536,128]{2,1,0:T(8,128)} %get-tuple-element.88.sin_ref), custom_call_target="tpu_custom_call" | custom-call | flops 12884901888 | bytes 23068672 | tf_op jit(solution)/shard_map/project_own/pallas_call | solution.py:111
  84.1 45.3 %collective-permute-done.x_ref = bf16[2,512,1024]{2,1,0:T(8,128)(2,1)S(1)} collective-permute-done((bf16[2,512,1024]{2,1,0:T(8,128)(2,1)}, bf16[2,512,1024]{2,1,0:T(8,128)(2,1)S(1)}, u32[]{:S(2)}, u32[]{:S(2)}) %collective-permute-start) | collective-permute-done | bytes 2097184 | tf_op jit(solution)/shard_map/ppermute | solution.py:1111
  129.4 1.3 copy-done.6
  130.8 13.1 %project_halo.1.q_ref.k_ref.v_ref = bf16[2,1536,3072]{2,1,0:T(8,128)(2,1)} custom-call(bf16[2,512,1024]{2,1,0:T(8,128)(2,1)} %copy-done.6, bf16[1024,3200]{1,0:T(8,128)(2,1)} %all-gather.4.cloned.1.call-done.w_ref, f32[2,1536,128]{2,1,0:T(8,128)} %get-tuple-element.89.cos_ref, ...), custom_call_target="tpu_custom_call", output_to_operand_aliasing={{}: (4, {})} | custom-call | flops 6442450944 | bytes 14680064 | tf_op jit(solution)/shard_map/project_halo/pallas_call | solution.py:125
  143.9 51.5 %attend.1 = (bf16[2,1024,1024]{2,1,0:T(8,128)(2,1)}, bf16[1024,2048]{1,0:T(8,128)(2,1)}, f32[2,8,2,1024]{3,2,1,0:T(2,128)}) custom-call(s32[1]{0:T(128)} %bitcast.3.own_ref, s32[2,8]{1,0:T(2,128)} %get-tuple-element.92.lo_ref, s32[2,8]{1,0:T(2,128)} %get-tuple-element.93.hi_ref, bf16[2,1536,3072]{2,1,0:T(8,128)(2,1)} %project_halo.1.q_ref.k_ref.v_ref, ...), custom_call_target="tpu_custom_call" | custom-call | flops 25769803776 | bytes 33554432 | tf_op jit(solution)/shard_map/attend/pallas_call | solution.py:257
  195.4 0.8 constant_dynamic-slice_fusion
  196.3 1.8 collective-permute-start.1
  198.0 2.5 collective-permute-done.1.lseh_ref
  200.6 0.6 slice_bitcast_fusion
  201.2 110.0 %feed.1 = (bf16[2,1024,1024]{2,1,0:T(8,128)(2,1)}, bf16[1024,2048]{1,0:T(8,128)(2,1)}, bf16[2624,2048]{1,0:T(8,128)(2,1)}, bf16[2,1024,6656]{2,1,0:T(8,128)(2,1)...) custom-call(bf16[2,1024,1024]{2,1,0:T(8,128)(2,1)} %bitcast.35, ...), custom_call_target="tpu_custom_call" | custom-call | flops 74625056768 | bytes 67108864 | tf_op jit(solution)/shard_map/feed/pallas_call | solution.py:633
  311.2 28.2 %weigh_early.1 = bf16[512,4096]{1,0:T(8,128)(2,1)} custom-call(bf16[1024,2048]{1,0:T(8,128)(2,1)} %get-tuple-element.41.refs_0_.h2t_ref, bf16[2048,6656]{1,0:T(8,128)(2,1)} %bitcast.32), custom_call_target="tpu_custom_call" | custom-call | flops 17179869184 | bytes 25165824 | tf_op jit(solution)/shard_map/weigh_early/pallas_call | solution.py:728
  339.4 0.0 reduce-scatter.3.cloned.1.call-update
  339.4 0.0 reduce-scatter.5.cloned.1.call-start
  339.5 20.6 %weigh_down.1 = bf16[1344,1024]{1,0:T(8,128)(2,1)} custom-call(bf16[2624,2048]{1,0:T(8,128)(2,1)} %get-tuple-element.48.refs_0_, bf16[2048,1024]{1,0:T(8,128)(2,1)} %bitcast.50), custom_call_target="tpu_custom_call" | custom-call | flops 11005853696 | bytes 25165824 | tf_op jit(solution)/shard_map/weigh_down/pallas_call | solution.py:728
  360.1 0.0 reduce-scatter.5.cloned.1.call-update
  360.1 0.0 all-reduce.4.cloned.1.call-start
  360.1 57.1 %attend_back.2.refs_0_ = bf16[3,2,1024,1024]{3,2,1,0:T(8,128)(2,1)} custom-call(s32[1]{0:T(128)} %bitcast.3.own_ref, s32[2,8]{1,0:T(2,128)} %get-tuple-element.92.lo_ref, s32[2,8]{1,0:T(2,128)} %get-tuple-element.93.hi_ref, bf16[2,1536,3072]{2,1,0:T(8,128)(2,1)} %project_halo.1.q_ref.k_ref.v_ref, bf16[2,1536,3072]{2,1,0:T(8,128)(2,1)} %project_halo.1.q_ref.k_ref.v_ref, ...), custom_call_target="tpu_custom_call" | custom-call | flops 32212254720 | bytes 67108864 | tf_op jit(solution)/shard_map/attend_back/pallas_call | solution.py:431
  417.3 0.0 reduce-scatter.3.cloned.1.call-done
  417.3 0.0 all-reduce.4.cloned.1.call-update
  417.3 57.4 %attend_back.3 = bf16[3,2,1024,1024]{3,2,1,0:T(8,128)(2,1)} custom-call(s32[1]{0:T(128)} %bitcast.3.own_ref, s32[2,8]{1,0:T(2,128)} %get-tuple-element.92.lo_ref, s32[2,8]{1,0:T(2,128)} %get-tuple-element.93.hi_ref, bf16[2,1536,3072]{2,1,0:T(8,128)(2,1)} %project_halo.1.q_ref.k_ref.v_ref, ...), custom_call_target="tpu_custom_call", output_to_operand_aliasing={{}: (16, {})} | custom-call | flops 32212254720 | bytes 67108864 | tf_op jit(solution)/shard_map/attend_back/pallas_call | solution.py:431
  474.7 0.0 reduce-scatter.5.cloned.1.call-done.down_ref
  474.7 0.0 copy-start.4
  474.8 100.7 %close.1 = (f32[2048,1024]{1,0:T(8,128)}, bf16[128,2560]{1,0:T(8,128)(2,1)}, bf16[128,3072]{1,0:T(8,128)(2,1)}, bf16[336,1024]{1,0:T(8,128)(2,1)}) custom-call(bf16[1024,2048]{1,0:T(8,128)(2,1)} %get-tuple-element.41.refs_0_.h2t_ref, bf16[1024,2048]{1,0:T(8,128)(2,1)} %get-tuple-element.42.ot_ref, bf16[1024,2048]{1,0:T(8,128)(2,1)} %get-tuple-element.43.h1t_ref, ...), custom_call_target="tpu_custom_call" | custom-call | flops 536870912 | bytes 4194304 | tf_op jit(solution)/shard_map/close/pallas_call | solution.py:1053
  575.5 0.0 copy-start.10
  575.5 2.6 multiply_reduce_fusion.1
  578.1 0.5 convert_divide_fusion.1
  578.7 1.2 slice_convert_fusion
  579.9 1.6 maximum_convert_fusion
  581.4 0.0 copy-start.1
  581.5 0.2 fusion.17
  581.7 1.1 copy-done.1
  582.8 2.0 multiply_reduce_fusion
  584.8 0.5 convert_divide_fusion
  585.4 0.8 maximum_convert_fusion.1
  586.2 2.1 copy.34
  588.3 1.3 slice-done.2
  589.7 3.4 copy.35
  (43 shorter events, 0.2 us)
Async XLA Ops:
  7.2 3.7 copy-start
  7.2 52.7 %all-gather.4.cloned.1.call-start = ((), (), s32[]{:S(2)}) async-start(), calls=%async_computation.2 | async-start | bytes 7372800 | tf_op jit(solution)/shard_map/all_gather | solution.py:1178
  10.1 1.1 copy-start.8
  10.1 191.1 %all-gather.8.cloned.1.call-start = ((), (), s32[]{:S(2)}) async-start(), calls=%async_computation.4 | async-start | bytes 6045696 | tf_op jit(solution)/shard_map/all_gather | solution.py:1178
  10.9 190.3 %all-gather.6.cloned.1.call-start = ((), (), s32[]{:S(2)}) async-start(), calls=%async_computation.3 | async-start | bytes 14745600 | tf_op jit(solution)/shard_map/all_gather | solution.py:1178
  11.2 2.0 copy-start.9
  13.2 404.1 %reduce-scatter.3.cloned.1.call-start = ((), (), s32[]{:S(2)}) async-start(), calls=%async_computation.5 | async-start | bytes 5242880 | tf_op jit(solution)/shard_map/reduce_scatter | solution.py:1203
  59.8 69.6 %collective-permute-start = (bf16[2,512,1024]{2,1,0:T(8,128)(2,1)}, bf16[2,512,1024]{2,1,0:T(8,128)(2,1)S(1)}, u32[]{:S(2)}, u32[]{:S(2)}) collective-permute-start(bf16[2,512,1024]{2,1,0:T(8,128)(2,1)} %dynamic-slice_bitcast_fusion), channel_id=1, source_target_pairs={{0,16},{16,0},{1,17},{17,1},{2,18},{18,2},{3,19},{19,3},{4,20},{20... | collective-permute-start | bytes 6291464 | tf_op jit(solution)/shard_map/ppermute | solution.py:1111
  129.4 1.3 copy-start.6
  143.9 56.7 %slice-start = ((bf16[1024,3200]{1,0:T(8,128)(2,1)}), bf16[1024,128]{1,0:T(8,128)(2,1)S(1)}, s32[]{:S(2)}) async-start(bf16[1024,3200]{1,0:T(8,128)(2,1)} %all-gather.4.cloned.1.call-done.w_ref), calls=%async_computation.8 | async-start | bytes 524288 | tf_op jit(solution)/shard_map/slice | solution.py:1194
  196.3 4.3 collective-permute-start.1
  200.5 110.6 %copy-start.12 = (f32[2,8,2,512]{3,2,1,0:T(2,128)}, f32[2,8,2,512]{3,2,1,0:T(2,128)S(1)}, u32[]{:S(2)}) copy-start(f32[2,8,2,512]{3,2,1,0:T(2,128)S(1)} %collective-permute-done.1.lseh_ref) | copy-start | bytes 196612
  339.4 135.3 %reduce-scatter.5.cloned.1.call-start = ((), (), s32[]{:S(2)}) async-start(), calls=%async_computation.6 | async-start | bytes 3440640 | tf_op jit(solution)/shard_map/reduce_scatter | solution.py:1203
  360.1 219.8 %all-reduce.4.cloned.1.call-start = ((), (), s32[]{:S(2)}) async-start(), calls=%async_computation.7 | async-start | bytes 2097152 | tf_op jit(solution)/shard_map/psum | solution.py:1223
  474.7 100.8 %copy-start.4 = (bf16[128,3072]{1,0:T(8,128)(2,1)S(1)}, bf16[128,3072]{1,0:T(8,128)(2,1)}, u32[]{:S(2)}) copy-start(bf16[128,3072]{1,0:T(8,128)(2,1)} %param.14) | copy-start | bytes 2359300
  575.5 2.6 copy-start.10
  575.5 3.1 copy-start.7
  575.5 4.3 copy-start.5
  581.4 1.3 copy-start.1
  581.5 4.7 copy-start.3
  582.8 2.1 copy-start.11
  582.8 2.6 copy-start.2
  582.8 5.6 slice-start.1
  585.4 4.3 slice-start.2
Sparse Core Ops, SparseCore 0:
  10.5 49.3 all-gather.3
  61.7 62.9 all-gather.7
  126.6 74.3 all-gather.5
  339.5 50.9 reduce-scatter.2
  393.7 40.6 reduce-scatter.4
  436.7 51.8 all-reduce.3

commit v6 on v5

--- a/solution.py
+++ b/solution.py
@@ -749,7 +749,7 @@
 
 LAGS = (1, 3, 5, 6, 7, 8)
 RING, RING_XY, RING_LINE = 5, 2, 4
-EARLY, DOWN_BLOCKS, LINE_LAG = 8, 4, 2
+EARLY, DOWN_BLOCKS, LINE_LAG = 10, 4, 2
 
 
 def close_kernel(blocks, rest_blocks, rest_edge, seqs, reps, h2t_ref, ot_ref, h1t_ref, rest_ref, right_ref, three_ref, w_ref, x_ref, dr_ref, gain_ref, down_ref,

time: 607 us -> 610 us (level)
  transfers between devices with their start and end apart: 8 -> 8, of which waited for: 3 -> 3; matrix products, arithmetic and copies ran while one was open for 4% -> 4% of each run, Pallas kernels for 54% -> 53%
where the time goes in v6:
time: 610 us; the launch traced here: 606 us
  Pallas kernels  461 us (76%)
  waiting for transfers between devices  82.6 us (14%)
  other arithmetic  22.8 us (4%)
  local copies, waits for them, and re-layouts  16.6 us (3%)
  between operations  14.6 us (2%)
  starting transfers between devices  7.9 us (1%)
    pallas_call x2, Pallas kernels, attend_back(): pl.pallas_call(functools.partial(attend_back_kernel, tiles, wide, first_b...  111 us
    pallas_call x1, Pallas kernels, feed(): pl.pallas_call(functools.partial(feed_kernel, seqs, halo // TILE), grid=(...  110 us
    pallas_call x1, Pallas kernels, close(): pl.pallas_call(functools.partial(close_kernel, blocks, rest_blocks, rest_...  104 us
    pallas_call x2, Pallas kernels, weigh(): pl.pallas_call(functools.partial(weigh_kernel, blocks, share, held, turns...  52.2 us
    pallas_call x1, Pallas kernels, attend(): pl.pallas_call(functools.partial(attend_kernel, tiles, wide), grid_spec=p...  49.2 us
    ppermute x2, waiting for transfers between devices, neighbours(): return lax.ppermute(facing, axis, [(0, 1), (1, 0)])  47.5 us
    all_gather x3, waiting for transfers between devices, body(): gather = lambda shard: lax.all_gather(shard, group, axis=0, tiled=True)  34.3 us
    pallas_call x1, Pallas kernels, project(): pl.pallas_call(functools.partial(project_kernel, True, shards), grid=grid...  21.2 us
  transfers between devices with their start and end apart: 8, of which 3 were waited for; matrix products, arithmetic and copies ran while one was open for 4% of the time, Pallas kernels for 53%

profile of v6, /device:TPU:0, one launch (start us, length us, event | category | flops | bytes accessed | tf_op | source)
XLA Modules:
  0.0 605.9 jit_solution(14946590176589492717)
XLA Ops:
  7.2 0.0 copy-start
  7.2 0.0 all-gather.4.cloned.1.call-start
  7.2 0.8 fusion.7
  8.0 2.1 pad_maximum_fusion.1
  10.1 0.0 all-gather.4.cloned.1.call-update
  10.1 0.0 all-gather.8.cloned.1.call-start
  10.2 0.7 all-gather.8.cloned.1.call-update
  10.9 0.0 all-gather.6.cloned.1.call-start
  10.9 0.3 fusion.18
  11.2 0.0 copy-start.9
  11.2 1.9 concatenate.17
  13.2 0.0 all-gather.6.cloned.1.call-update
  13.2 0.0 reduce-scatter.3.cloned.1.call-start
  13.3 0.1 slice.34
  13.4 0.1 slice.33
  13.6 0.3 fusion.3
  14.0 0.1 fusion.8
  14.1 0.1 fusion.4
  14.2 3.1 dynamic-slice_bitcast_fusion
  17.3 1.3 select_convert_fusion.ek_ref
  18.6 7.0 %fusion = (f32[2,1536,128]{2,1,0:T(8,128)}, f32[2,1536,128]{2,1,0:T(8,128)}) fusion(f32[128]{0:T(128)S(1)} %get-tuple-element.90, f32[128]{0:T(128)S(1)} %get-tuple-element.91, f32[2,1536]{1,0:T(2,128)S(1)} %subtract_convert_fusion), kind=kLoop, calls=%fused_computation.6 | loop fusion | flops 786432 | bytes 3159040 | tf_op jit(solution)/shard_map/mul | solution.py:1145
  25.6 34.3 %all-gather.4.cloned.1.call-done.w_ref = bf16[1024,3200]{1,0:T(8,128)(2,1)} async-done(((bf16[128,3200]{1,0:T(8,128)(2,1)}), bf16[1024,3200]{1,0:T(8,128)(2,1)}) %all-gather.4.cloned.1.call-update) | async-done | bytes 6553616 | tf_op jit(solution)/shard_map/all_gather | solution.py:1178
  59.9 1.5 collective-permute-start
  61.3 0.1 fusion.9
  61.4 0.6 and_select_fusion.4
  62.0 0.9 select_convert_fusion.1.eq_ref
  62.9 21.2 %project_own.1 = (bf16[1024,2048]{1,0:T(8,128)(2,1)}, bf16[2,1536,3072]{2,1,0:T(8,128)(2,1)}) custom-call(bf16[2,1024,1024]{2,1,0:T(8,128)(2,1)} %bitcast.34, bf16[1024,3200]{1,0:T(8,128)(2,1)} %all-gather.4.cloned.1.call-done.w_ref, f32[2,1536,128]{2,1,0:T(8,128)} %get-tuple-element.89.cos_ref, f32[2,1536,128]{2,1,0:T(8,128)} %get-tuple-element.88.sin_ref), custom_call_target="tpu_custom_call" | custom-call | flops 12884901888 | bytes 23068672 | tf_op jit(solution)/shard_map/project_own/pallas_call | solution.py:111
  84.2 45.3 %collective-permute-done.x_ref = bf16[2,512,1024]{2,1,0:T(8,128)(2,1)S(1)} collective-permute-done((bf16[2,512,1024]{2,1,0:T(8,128)(2,1)}, bf16[2,512,1024]{2,1,0:T(8,128)(2,1)S(1)}, u32[]{:S(2)}, u32[]{:S(2)}) %collective-permute-start) | collective-permute-done | bytes 2097184 | tf_op jit(solution)/shard_map/ppermute | solution.py:1111
  129.5 1.3 copy-done.5
  130.8 13.1 %project_halo.1.q_ref.k_ref.v_ref = bf16[2,1536,3072]{2,1,0:T(8,128)(2,1)} custom-call(bf16[2,512,1024]{2,1,0:T(8,128)(2,1)} %copy-done.5, bf16[1024,3200]{1,0:T(8,128)(2,1)} %all-gather.4.cloned.1.call-done.w_ref, f32[2,1536,128]{2,1,0:T(8,128)} %get-tuple-element.89.cos_ref, ...), custom_call_target="tpu_custom_call", output_to_operand_aliasing={{}: (4, {})} | custom-call | flops 6442450944 | bytes 14680064 | tf_op jit(solution)/shard_map/project_halo/pallas_call | solution.py:125
  143.9 49.2 %attend.1 = (bf16[2,1024,1024]{2,1,0:T(8,128)(2,1)}, bf16[1024,2048]{1,0:T(8,128)(2,1)}, f32[2,8,2,1024]{3,2,1,0:T(2,128)}) custom-call(s32[1]{0:T(128)} %bitcast.3.own_ref, s32[2,8]{1,0:T(2,128)} %get-tuple-element.92.lo_ref, s32[2,8]{1,0:T(2,128)} %get-tuple-element.93.hi_ref, bf16[2,1536,3072]{2,1,0:T(8,128)(2,1)} %project_halo.1.q_ref.k_ref.v_ref, ...), custom_call_target="tpu_custom_call" | custom-call | flops 25769803776 | bytes 33554432 | tf_op jit(solution)/shard_map/attend/pallas_call | solution.py:257
  193.2 0.8 constant_dynamic-slice_fusion
  194.0 6.2 %collective-permute-start.1 = (f32[2,8,2,512]{3,2,1,0:T(2,128)S(1)}, f32[2,8,2,512]{3,2,1,0:T(2,128)S(1)}, u32[]{:S(2)}, u32[]{:S(2)}) collective-permute-start(f32[2,8,2,512]{3,2,1,0:T(2,128)S(1)} %constant_dynamic-slice_fusion), channel_id=1, source_target_pairs={{0,16},{16,0},{1,17},{17,1},{2,18},{18,2},{3,19},{19,3},{4,20},{20... | collective-permute-start | bytes 196616 | tf_op jit(solution)/shard_map/ppermute | solution.py:1111
  200.2 2.2 collective-permute-done.1.lseh_ref
  202.4 0.0 slice-done
  202.5 0.6 slice_bitcast_fusion
  203.1 110.2 %feed.1 = (bf16[2,1024,1024]{2,1,0:T(8,128)(2,1)}, bf16[1024,2048]{1,0:T(8,128)(2,1)}, bf16[2624,2048]{1,0:T(8,128)(2,1)}, bf16[2,1024,6656]{2,1,0:T(8,128)(2,1)...) custom-call(bf16[2,1024,1024]{2,1,0:T(8,128)(2,1)} %bitcast.35, ...), custom_call_target="tpu_custom_call" | custom-call | flops 74625056768 | bytes 67108864 | tf_op jit(solution)/shard_map/feed/pallas_call | solution.py:633
  313.4 31.6 %weigh_early.1 = bf16[512,5120]{1,0:T(8,128)(2,1)} custom-call(bf16[1024,2048]{1,0:T(8,128)(2,1)} %get-tuple-element.41.refs_0_.h2t_ref, bf16[2048,6656]{1,0:T(8,128)(2,1)} %bitcast.32), custom_call_target="tpu_custom_call" | custom-call | flops 21474836480 | bytes 25165824 | tf_op jit(solution)/shard_map/weigh_early/pallas_call | solution.py:728
  345.0 0.0 reduce-scatter.3.cloned.1.call-update
  345.0 0.0 reduce-scatter.5.cloned.1.call-start
  345.0 20.6 %weigh_down.1 = bf16[1344,1024]{1,0:T(8,128)(2,1)} custom-call(bf16[2624,2048]{1,0:T(8,128)(2,1)} %get-tuple-element.48.refs_0_, bf16[2048,1024]{1,0:T(8,128)(2,1)} %bitcast.50), custom_call_target="tpu_custom_call" | custom-call | flops 11005853696 | bytes 25165824 | tf_op jit(solution)/shard_map/weigh_down/pallas_call | solution.py:728
  365.6 0.0 reduce-scatter.5.cloned.1.call-update
  365.7 0.0 all-reduce.4.cloned.1.call-start
  365.7 58.3 %attend_back.2.refs_0_ = bf16[3,2,1024,1024]{3,2,1,0:T(8,128)(2,1)} custom-call(s32[1]{0:T(128)} %bitcast.3.own_ref, s32[2,8]{1,0:T(2,128)} %get-tuple-element.92.lo_ref, s32[2,8]{1,0:T(2,128)} %get-tuple-element.93.hi_ref, bf16[2,1536,3072]{2,1,0:T(8,128)(2,1)} %project_halo.1.q_ref.k_ref.v_ref, bf16[2,1536,3072]{2,1,0:T(8,128)(2,1)} %project_halo.1.q_ref.k_ref.v_ref, ...), custom_call_target="tpu_custom_call" | custom-call | flops 32212254720 | bytes 67108864 | tf_op jit(solution)/shard_map/attend_back/pallas_call | solution.py:431
  424.0 0.0 reduce-scatter.3.cloned.1.call-done
  424.0 0.0 all-reduce.4.cloned.1.call-update
  424.1 52.7 %attend_back.3 = bf16[3,2,1024,1024]{3,2,1,0:T(8,128)(2,1)} custom-call(s32[1]{0:T(128)} %bitcast.3.own_ref, s32[2,8]{1,0:T(2,128)} %get-tuple-element.92.lo_ref, s32[2,8]{1,0:T(2,128)} %get-tuple-element.93.hi_ref, bf16[2,1536,3072]{2,1,0:T(8,128)(2,1)} %project_halo.1.q_ref.k_ref.v_ref, ...), custom_call_target="tpu_custom_call", output_to_operand_aliasing={{}: (16, {})} | custom-call | flops 32212254720 | bytes 67108864 | tf_op jit(solution)/shard_map/attend_back/pallas_call | solution.py:431
  476.8 0.0 reduce-scatter.5.cloned.1.call-done.down_ref
  476.8 0.0 copy-start.4
  476.9 104.3 %close.1 = (f32[2048,1024]{1,0:T(8,128)}, bf16[128,1536]{1,0:T(8,128)(2,1)}, bf16[128,3072]{1,0:T(8,128)(2,1)}, bf16[336,1024]{1,0:T(8,128)(2,1)}) custom-call(bf16[1024,2048]{1,0:T(8,128)(2,1)} %get-tuple-element.41.refs_0_.h2t_ref, bf16[1024,2048]{1,0:T(8,128)(2,1)} %get-tuple-element.42.ot_ref, bf16[1024,2048]{1,0:T(8,128)(2,1)} %get-tuple-element.43.h1t_ref, ...), custom_call_target="tpu_custom_call" | custom-call | flops 536870912 | bytes 4194304 | tf_op jit(solution)/shard_map/close/pallas_call | solution.py:1053
  581.2 0.0 copy-start.10
  581.2 2.6 multiply_reduce_fusion.1
  583.8 0.5 convert_divide_fusion.1
  584.3 1.2 slice_convert_fusion
  585.5 1.6 maximum_convert_fusion
  587.2 0.0 copy-start.1
  587.2 0.2 fusion.17
  587.4 1.1 copy-done.1
  588.5 2.1 multiply_reduce_fusion
  590.6 0.5 convert_divide_fusion
  591.1 0.8 maximum_convert_fusion.1
  592.0 2.1 copy.34
  594.1 1.3 slice-done.2
  595.4 3.4 copy.35
  (43 shorter events, 0.2 us)
Async XLA Ops:
  7.2 3.7 copy-start
  7.2 52.7 %all-gather.4.cloned.1.call-start = ((), (), s32[]{:S(2)}) async-start(), calls=%async_computation.2 | async-start | bytes 7372800 | tf_op jit(solution)/shard_map/all_gather | solution.py:1178
  10.1 1.1 copy-start.8
  10.1 193.0 %all-gather.8.cloned.1.call-start = ((), (), s32[]{:S(2)}) async-start(), calls=%async_computation.4 | async-start | bytes 6045696 | tf_op jit(solution)/shard_map/all_gather | solution.py:1178
  10.9 192.2 %all-gather.6.cloned.1.call-start = ((), (), s32[]{:S(2)}) async-start(), calls=%async_computation.3 | async-start | bytes 14745600 | tf_op jit(solution)/shard_map/all_gather | solution.py:1178
  11.2 2.0 copy-start.9
  13.2 410.9 %reduce-scatter.3.cloned.1.call-start = ((), (), s32[]{:S(2)}) async-start(), calls=%async_computation.5 | async-start | bytes 6553600 | tf_op jit(solution)/shard_map/reduce_scatter | solution.py:1203
  59.9 69.6 %collective-permute-start = (bf16[2,512,1024]{2,1,0:T(8,128)(2,1)}, bf16[2,512,1024]{2,1,0:T(8,128)(2,1)S(1)}, u32[]{:S(2)}, u32[]{:S(2)}) collective-permute-start(bf16[2,512,1024]{2,1,0:T(8,128)(2,1)} %dynamic-slice_bitcast_fusion), channel_id=1, source_target_pairs={{0,16},{16,0},{1,17},{17,1},{2,18},{18,2},{3,19},{19,3},{4,20},{20... | collective-permute-start | bytes 6291464 | tf_op jit(solution)/shard_map/ppermute | solution.py:1111
  129.4 1.3 copy-start.5
  143.9 58.5 %slice-start = ((bf16[1024,3200]{1,0:T(8,128)(2,1)}), bf16[1024,128]{1,0:T(8,128)(2,1)S(1)}, s32[]{:S(2)}) async-start(bf16[1024,3200]{1,0:T(8,128)(2,1)} %all-gather.4.cloned.1.call-done.w_ref), calls=%async_computation.8 | async-start | bytes 524288 | tf_op jit(solution)/shard_map/slice | solution.py:1194
  194.0 8.4 %collective-permute-start.1 = (f32[2,8,2,512]{3,2,1,0:T(2,128)S(1)}, f32[2,8,2,512]{3,2,1,0:T(2,128)S(1)}, u32[]{:S(2)}, u32[]{:S(2)}) collective-permute-start(f32[2,8,2,512]{3,2,1,0:T(2,128)S(1)} %constant_dynamic-slice_fusion), channel_id=1, source_target_pairs={{0,16},{16,0},{1,17},{17,1},{2,18},{18,2},{3,19},{19,3},{4,20},{20... | collective-permute-start | bytes 196616 | tf_op jit(solution)/shard_map/ppermute | solution.py:1111
  202.4 110.9 %copy-start.12 = (f32[2,8,2,512]{3,2,1,0:T(2,128)}, f32[2,8,2,512]{3,2,1,0:T(2,128)S(1)}, u32[]{:S(2)}) copy-start(f32[2,8,2,512]{3,2,1,0:T(2,128)S(1)} %collective-permute-done.1.lseh_ref) | copy-start | bytes 196612
  345.0 131.8 %reduce-scatter.5.cloned.1.call-start = ((), (), s32[]{:S(2)}) async-start(), calls=%async_computation.6 | async-start | bytes 3440640 | tf_op jit(solution)/shard_map/reduce_scatter | solution.py:1203
  365.7 219.9 %all-reduce.4.cloned.1.call-start = ((), (), s32[]{:S(2)}) async-start(), calls=%async_computation.7 | async-start | bytes 2621440 | tf_op jit(solution)/shard_map/psum | solution.py:1223
  476.8 104.3 %copy-start.4 = (bf16[128,3072]{1,0:T(8,128)(2,1)S(1)}, bf16[128,3072]{1,0:T(8,128)(2,1)}, u32[]{:S(2)}) copy-start(bf16[128,3072]{1,0:T(8,128)(2,1)} %param.14) | copy-start | bytes 2359300
  581.2 2.6 copy-start.10
  581.2 3.1 copy-start.7
  581.2 4.3 copy-start.6
  587.2 1.3 copy-start.1
  587.2 4.8 copy-start.3
  588.5 2.1 copy-start.11
  588.5 2.6 copy-start.2
  588.5 5.6 slice-start.1
  591.1 4.3 slice-start.2
Sparse Core Ops, SparseCore 0:
  10.5 49.3 all-gather.3
  61.7 62.9 all-gather.7
  126.6 74.5 all-gather.5
  345.1 61.9 reduce-scatter.2
  410.0 40.6 reduce-scatter.4
  452.9 74.4 all-reduce.3
